TPU v7x, 512 devices: a whole 4x8x8 slice. The times are simulated.
512 devices in a mesh: space: 32 (over y_lo, z, core), grain: 16 (over x, y_hi).
Axes of the slice: x: 4, y: 8 (y_hi: 4, y_lo: 2; y = y_hi * 2 + y_lo), z: 8, core: 2. Of those that a mesh axis runs over, the one named last changes fastest.
Arguments:
- grain_ids: int32 [3, 512, 2048], P(None, 'space'), may hold values from 0 to 95
- group_of: int32 [96], P('grain'), may hold values from 0 to 3
- group_mobility: float32 [4], replicated, may hold values from 0.3 to 1.5
- seed_noise: float32 [96, 3, 512, 2048], P('grain', None, 'space'), may hold values from -0.25 to 0.25
- concentration: float32 [3, 512, 2048], P(None, 'space'), may hold values from 0.1 to 0.7
Outputs:
- order_params: float32 [96, 3, 512, 2048], P('grain', None, 'space')
- solute: float32 [3, 512, 2048], P(None, 'space')
All inputs are finite; a program needn't handle non-finite values.
Results may differ from a plain program's by a relative error of at most 0.0001.
Values sent between devices are 32-bit elements; how exact they have to be, the bound alone decides.
No kernel may reach another device: no remote copies, remote signals or barrier semaphores. Data moves between devices by JAX's collectives and lax.ppermute only.
A program may use at most 64 MiB of HBM per device.

v0:
```python
import jax
import jax.numpy as jnp
from jax import lax
from jax.sharding import PartitionSpec as P

STEPS = 2


coef_quad = 1.0
coef_quart = 1.0
cross_gamma = 1.5
gradient_kappa = 0.5
solute_beta = 0.6
bulk_stiff = 1.0
solute_mean = 0.4
solute_kappa = 0.25
solute_mobility = 0.3
time_step = 0.1


def padded_2(cells, sides, width):
    for axis, dim in sides:
        count = lax.axis_size(axis)
        head = lax.slice_in_dim(cells, 0, width, axis=dim)
        tail = lax.slice_in_dim(cells, cells.shape[dim] - width, cells.shape[dim], axis=dim)
        cells = jnp.concatenate(
            [
                lax.ppermute(tail, axis, [(i, (i + 1) % count) for i in range(count)]),
                cells,
                lax.ppermute(head, axis, [((i + 1) % count, i) for i in range(count)]),
            ],
            axis=dim,
        )
    return cells


def laplace_padded(padded):
    center = padded[..., 1:-1, :]
    along_x = padded[..., 2:, :] + padded[..., :-2, :]
    along_y = jnp.roll(center, 1, -1) + jnp.roll(center, -1, -1)
    edged = jnp.concatenate([center[..., :1, :, :], center, center[..., -1:, :, :]], axis=-3)
    along_z = edged[..., 2:, :, :] + edged[..., :-2, :, :]
    return along_x + along_y + along_z - 6.0 * center


def shards(grain_ids, group_of, group_mobility, seed_noise, concentration):
    local_grains = seed_noise.shape[0]
    first = lax.axis_index("grain") * local_grains
    owned = first + jnp.arange(local_grains, dtype=jnp.int32)
    eta = (grain_ids[None] == owned[:, None, None, None]).astype(jnp.float32) * 0.9 + seed_noise
    table = (
        group_of[:, None] == jnp.arange(group_mobility.shape[0], dtype=jnp.int32)[None, :]
    ).astype(jnp.float32)
    mobility = jnp.sum(table * group_mobility[None, :], 1)
    solute = concentration
    for step in range(STEPS):
        padded = padded_2(eta, (("space", 2),), 1)
        lap_eta = laplace_padded(padded)
        square = eta * eta
        sum_two, sum_four = lax.psum((jnp.sum(square, 0), jnp.sum(square * square, 0)), "grain")
        solute_padded = padded_2(solute, (("space", 1),), 1)
        potential = (
            2.0 * bulk_stiff * (solute - solute_mean)
            - solute_beta * (sum_two * sum_two - sum_four)
            - solute_kappa * laplace_padded(solute_padded)
        )
        potential_padded = padded_2(potential, (("space", 1),), 1)
        lap_potential = laplace_padded(potential_padded)
        force = (
            -coef_quad * eta
            + coef_quart * eta * square
            + eta
            * (sum_two[None] - square)
            * (2.0 * cross_gamma - 4.0 * solute_beta * solute)[None]
            - gradient_kappa * lap_eta
        )
        new_solute = solute + time_step * solute_mobility * lap_potential
        eta = eta - time_step * mobility[:, None, None, None] * force
        solute = new_solute
    return (eta, solute)


def solution(mesh):
    placed = (
        P(None, "space", None),
        P("grain"),
        P(),
        P("grain", None, "space", None),
        P(None, "space", None),
    )
    return jax.shard_map(
        shards,
        mesh=mesh,
        in_specs=placed,
        out_specs=(P("grain", None, "space", None), P(None, "space", None)),
        check_vma=False,
    )
```

profile of v0, /device:TPU:1, one launch (start us, length us, event | category | flops | bytes accessed | tf_op | source)
XLA Modules:
  0.0 430.5 jit_solution(371741461738500969)
XLA Ops:
  7.2 0.0 all-reduce.4.cloned.1.call-start
  7.2 6.2 %multiply_reduce_fusion.1 = (f32[3,16,2048]{2,1,0:T(8,128)}, f32[3,16,2048]{2,1,0:T(8,128)}, f32[6,3,16,2048]{3,0,2,1:T(8,128)S(1)}) fusion(f32[6,3,16,2048]{3,2,1,0:T(8,128)} %param.8, s32[6]{0:T(128)S(1)} %iota_add_fusion, s32[3,16,2048]{2,1,0:T(8,128)} %param.5), kind=kLoop, calls=%fused_computation.32 | loop fusion | flops 3932160 | bytes 5898264 | tf_op jit(solution)/shard_map/reduce_sum | solution.py:60
  13.4 0.8 fusion.52
  14.2 8.8 %collective-permute-start = (f32[6,3,1,2048]{3,0,2,1:T(8,128)}, f32[6,3,1,2048]{3,0,2,1:T(8,128)}, u32[]{:S(2)}, u32[]{:S(2)}) collective-permute-start(f32[6,3,1,2048]{3,0,2,1:T(8,128)} %get-tuple-element.24), channel_id=1, source_target_pairs={{16,0},{32,16},{48,32},{64,48},{80,64},{96,80},{112,96},{128,112},... | collective-permute-start | bytes 442376 | tf_op jit(solution)/shard_map/ppermute | solution.py:30
  23.0 1.9 collective-permute-start.1
  25.0 0.0 all-reduce.4.cloned.1.call-update
  25.0 0.0 all-reduce.6.cloned.1.call-start
  25.0 0.7 fusion.70
  25.7 6.0 %collective-permute-start.2 = (f32[3,1,2048]{2,1,0:T(1,128)}, f32[3,1,2048]{2,1,0:T(1,128)}, u32[]{:S(2)}, u32[]{:S(2)}) collective-permute-start(f32[3,1,2048]{2,1,0:T(1,128)} %get-tuple-element.61), channel_id=1, source_target_pairs={{16,0},{32,16},{48,32},{64,48},{80,64},{96,80},{112,96},{128,112},... | collective-permute-start | bytes 73736 | tf_op jit(solution)/shard_map/ppermute | solution.py:30
  31.7 1.9 collective-permute-start.3
  33.7 3.8 fusion.54
  37.5 1.5 fusion.55
  39.0 0.8 fusion.53
  39.8 0.9 multiply_subtract_fusion.1
  40.6 1.0 fusion.68
  41.6 0.7 fusion.71
  42.3 0.7 fusion.69
  43.0 0.1 select_reduce_fusion
  43.1 145.7 %all-reduce.4.cloned.1.call-done = f32[3,16,2048]{2,1,0:T(8,128)} async-done(((f32[3,16,2048]{2,1,0:T(8,128)}), f32[3,16,2048]{2,1,0:T(8,128)}) %all-reduce.4.cloned.1.call-update) | async-done | bytes 393232 | tf_op jit(solution)/shard_map/psum | solution.py:60
  188.8 12.1 %multiply_reduce_fusion = (f32[3,16,2048]{2,1,0:T(8,128)}, f32[3,16,2048]{2,1,0:T(8,128)}, f32[6,3,16,2048]{3,0,2,1:T(8,128)S(1)}) fusion(f32[6,3,16,2048]{3,0,2,1:T(8,128)} %copy-done, f32[6,1,16,2048]{3,0,2,1:T(8,128)} %get-tuple-element.31, f32[6,1,16,2048]{3,0,2,1:T(8,128)} %get-tuple-element.30, f32[6,3,16,1]{3,0,2,1:T(8,128)} %get-tuple-element.27, ...), kind=kLoop, calls=%fused_computation.31 | loop fusion | flops 16318464 | bytes 12877848 | tf_op jit(solution)/shard_map/reduce_sum | solution.py:60
  200.9 1.4 fusion.51
  202.4 0.0 all-reduce.6.cloned.1.call-update
  202.4 0.8 fusion.50
  203.2 3.8 fusion.48
  207.0 0.8 fusion.49
  207.8 13.1 %collective-permute-start.6 = (f32[6,3,1,2048]{3,0,2,1:T(8,128)}, f32[6,3,1,2048]{3,0,2,1:T(8,128)}, u32[]{:S(2)}, u32[]{:S(2)}) collective-permute-start(f32[6,3,1,2048]{3,0,2,1:T(8,128)} %get-tuple-element.20), channel_id=1, source_target_pairs={{16,0},{32,16},{48,32},{64,48},{80,64},{96,80},{112,96},{128,112},... | collective-permute-start | bytes 442376 | tf_op jit(solution)/shard_map/ppermute | solution.py:30
  220.8 3.2 collective-permute-start.7
  224.0 154.4 %all-reduce.6.cloned.1.call-done = (f32[3,16,2048]{2,1,0:T(8,128)}, f32[3,16,2048]{2,1,0:T(8,128)}, f32[3,16,2048]{2,1,0:T(8,128)}) async-done(((f32[3,16,2048]{2,1,0:T(8,128)}, f32[3,16,2048]{2,1,0:T(8,128)}, f32[3,16,2048]{2,1,0:T(8,128)}), (f32[3,16,2048]{2,1,0:T(8,128)}, f32[3,16,2048]{2,1,0:T(8,128)}, f32[3,16,2048]{2,1,0:T(8,128)})) %all-reduce.6.cloned.1.call-update) | async-done | bytes 1179664 | tf_op jit(solution)/shard_map/psum | solution.py:60
  378.4 2.0 fusion.43
  380.4 0.2 fusion.66
  380.7 12.2 %collective-permute-start.4 = (f32[3,1,2048]{2,1,0:T(1,128)S(1)}, f32[3,1,2048]{2,1,0:T(1,128)S(1)}, u32[]{:S(2)}, u32[]{:S(2)}) collective-permute-start(f32[3,1,2048]{2,1,0:T(1,128)S(1)} %get-tuple-element.49), channel_id=1, source_target_pairs={{16,0},{32,16},{48,32},{64,48},{80,64},{96,80},{112,96},{128,112},... | collective-permute-start | bytes 73736 | tf_op jit(solution)/shard_map/ppermute | solution.py:30
  392.9 3.6 collective-permute-start.5
  396.5 0.1 fusion.65
  396.6 0.8 collective-permute-done.5
  397.4 0.3 multiply_subtract_fusion
  397.7 0.2 fusion.60
  398.0 4.8 %collective-permute-start.8 = (f32[3,1,2048]{2,1,0:T(1,128)S(1)}, f32[3,1,2048]{2,1,0:T(1,128)S(1)}, u32[]{:S(2)}, u32[]{:S(2)}) collective-permute-start(f32[3,1,2048]{2,1,0:T(1,128)S(1)} %get-tuple-element.45), channel_id=1, source_target_pairs={{16,0},{32,16},{48,32},{64,48},{80,64},{96,80},{112,96},{128,112},... | collective-permute-start | bytes 73736 | tf_op jit(solution)/shard_map/ppermute | solution.py:30
  402.8 2.1 collective-permute-start.9
  405.0 5.8 %fusion.6 = f32[6,3,16,2048]{3,0,2,1:T(8,128)S(1)} fusion(f32[6,3,16,2048]{3,0,2,1:T(8,128)S(1)} %get-tuple-element.15, f32[6,1,16,2048]{3,0,2,1:T(8,128)S(1)} %copy-done.5, f32[6,1,16,2048]{3,0,2,1:T(8,128)S(1)} %copy-done.4, f32[6,3,1,2048]{3,0,2,1:T(8,128)} %collective-permute-done.7, f32[6,3,1,2048]{3,0,2,1:T(8,128)} %collective-permute-done.6, ...), kind=kLoop, calls=%fused_computation.7 | loop fusion | flops 14155776 | bytes 12091416 | tf_op jit(solution)/shard_map/sub | solution.py:78
  410.8 0.1 fusion.61
  410.9 2.8 copy.10
  413.7 0.3 fusion.29
  414.0 0.2 fusion.56
  414.3 2.4 collective-permute-start.10
  416.7 3.2 collective-permute-start.11
  419.9 0.1 fusion.57
  419.9 2.7 collective-permute-done.11
  422.6 1.0 fusion.22
  (42 shorter events, 0.3 us)
Async XLA Ops:
  7.2 181.6 %all-reduce.4.cloned.1.call-start = ((), (), s32[]{:S(2)}) async-start(), calls=%async_computation | async-start | bytes 786432 | tf_op jit(solution)/shard_map/psum | solution.py:60
  7.2 17.8 %copy-start.1 = (f32[3,16,2048]{2,1,0:T(8,128)S(1)}, f32[3,16,2048]{2,1,0:T(8,128)}, u32[]{:S(2)}) copy-start(f32[3,16,2048]{2,1,0:T(8,128)} %param.9) | copy-start | bytes 1179652
  13.4 25.5 %copy-start = (f32[6,3,16,2048]{3,0,2,1:T(8,128)}, f32[6,3,16,2048]{3,0,2,1:T(8,128)S(1)}, u32[]{:S(2)}) copy-start(f32[6,3,16,2048]{3,0,2,1:T(8,128)S(1)} %get-tuple-element.32) | copy-start | bytes 7077892
  14.2 28.9 %collective-permute-start = (f32[6,3,1,2048]{3,0,2,1:T(8,128)}, f32[6,3,1,2048]{3,0,2,1:T(8,128)}, u32[]{:S(2)}, u32[]{:S(2)}) collective-permute-start(f32[6,3,1,2048]{3,0,2,1:T(8,128)} %get-tuple-element.24), channel_id=1, source_target_pairs={{16,0},{32,16},{48,32},{64,48},{80,64},{96,80},{112,96},{128,112},... | collective-permute-start | bytes 442376 | tf_op jit(solution)/shard_map/ppermute | solution.py:30
  23.0 20.1 %collective-permute-start.1 = (f32[6,3,1,2048]{3,0,2,1:T(8,128)}, f32[6,3,1,2048]{3,0,2,1:T(8,128)}, u32[]{:S(2)}, u32[]{:S(2)}) collective-permute-start(f32[6,3,1,2048]{3,0,2,1:T(8,128)} %get-tuple-element.25), channel_id=1, source_target_pairs={{0,16},{16,32},{32,48},{48,64},{64,80},{80,96},{96,112},{112,128},... | collective-permute-start | bytes 442376 | tf_op jit(solution)/shard_map/ppermute | solution.py:28
  25.0 353.4 %all-reduce.6.cloned.1.call-start = ((), (), s32[]{:S(2)}) async-start(), calls=%async_computation.1 | async-start | bytes 2359296 | tf_op jit(solution)/shard_map/psum | solution.py:60
  25.7 198.3 %collective-permute-start.2 = (f32[3,1,2048]{2,1,0:T(1,128)}, f32[3,1,2048]{2,1,0:T(1,128)}, u32[]{:S(2)}, u32[]{:S(2)}) collective-permute-start(f32[3,1,2048]{2,1,0:T(1,128)} %get-tuple-element.61), channel_id=1, source_target_pairs={{16,0},{32,16},{48,32},{64,48},{80,64},{96,80},{112,96},{128,112},... | collective-permute-start | bytes 73736 | tf_op jit(solution)/shard_map/ppermute | solution.py:30
  31.7 192.3 %collective-permute-start.3 = (f32[3,1,2048]{2,1,0:T(1,128)}, f32[3,1,2048]{2,1,0:T(1,128)}, u32[]{:S(2)}, u32[]{:S(2)}) collective-permute-start(f32[3,1,2048]{2,1,0:T(1,128)} %get-tuple-element.62), channel_id=1, source_target_pairs={{0,16},{16,32},{32,48},{48,64},{64,80},{80,96},{96,112},{112,128},... | collective-permute-start | bytes 73736 | tf_op jit(solution)/shard_map/ppermute | solution.py:28
  37.5 5.5 %copy-start.10 = (f32[4]{0:T(128)S(1)}, f32[4]{0:T(128)}, u32[]{:S(2)}) copy-start(f32[4]{0:T(128)} %param.7) | copy-start | bytes 52
  37.5 5.5 %copy-start.11 = (s32[6]{0:T(128)S(1)}, s32[6]{0:T(128)}, u32[]{:S(2)}) copy-start(s32[6]{0:T(128)} %param.6) | copy-start | bytes 76
  207.8 197.2 %collective-permute-start.6 = (f32[6,3,1,2048]{3,0,2,1:T(8,128)}, f32[6,3,1,2048]{3,0,2,1:T(8,128)}, u32[]{:S(2)}, u32[]{:S(2)}) collective-permute-start(f32[6,3,1,2048]{3,0,2,1:T(8,128)} %get-tuple-element.20), channel_id=1, source_target_pairs={{16,0},{32,16},{48,32},{64,48},{80,64},{96,80},{112,96},{128,112},... | collective-permute-start | bytes 442376 | tf_op jit(solution)/shard_map/ppermute | solution.py:30
  220.8 184.1 %collective-permute-start.7 = (f32[6,3,1,2048]{3,0,2,1:T(8,128)}, f32[6,3,1,2048]{3,0,2,1:T(8,128)}, u32[]{:S(2)}, u32[]{:S(2)}) collective-permute-start(f32[6,3,1,2048]{3,0,2,1:T(8,128)} %get-tuple-element.21), channel_id=1, source_target_pairs={{0,16},{16,32},{32,48},{48,64},{64,80},{80,96},{96,112},{112,128},... | collective-permute-start | bytes 442376 | tf_op jit(solution)/shard_map/ppermute | solution.py:28
  378.4 26.6 %copy-start.4 = (f32[6,1,16,2048]{3,0,2,1:T(8,128)S(1)}, f32[6,1,16,2048]{3,0,2,1:T(8,128)}, u32[]{:S(2)}) copy-start(f32[6,1,16,2048]{3,0,2,1:T(8,128)} %get-tuple-element.22) | copy-start | bytes 2359300
  378.4 26.6 %copy-start.5 = (f32[6,1,16,2048]{3,0,2,1:T(8,128)S(1)}, f32[6,1,16,2048]{3,0,2,1:T(8,128)}, u32[]{:S(2)}) copy-start(f32[6,1,16,2048]{3,0,2,1:T(8,128)} %get-tuple-element.23) | copy-start | bytes 2359300
  380.4 24.6 %copy-start.3 = (f32[6,3,16,2047]{3,0,2,1:T(8,128)S(1)}, f32[6,3,16,2047]{3,0,2,1:T(8,128)}, u32[]{:S(2)}) copy-start(f32[6,3,16,2047]{3,0,2,1:T(8,128)} %get-tuple-element.17) | copy-start | bytes 7074436
  380.6 24.4 %copy-start.2 = (f32[6,3,16,2047]{3,0,2,1:T(8,128)S(1)}, f32[6,3,16,2047]{3,0,2,1:T(8,128)}, u32[]{:S(2)}) copy-start(f32[6,3,16,2047]{3,0,2,1:T(8,128)} %get-tuple-element.16) | copy-start | bytes 7074436
  380.6 24.4 %copy-start.6 = (f32[3,16,2048]{2,1,0:T(8,128)S(1)}, f32[3,16,2048]{2,1,0:T(8,128)}, u32[]{:S(2)}) copy-start(f32[3,16,2048]{2,1,0:T(8,128)} %get-tuple-element.11) | copy-start | bytes 1179652
  380.6 24.4 %copy-start.7 = (f32[6,3,16,1]{3,0,2,1:T(8,128)S(1)}, f32[6,3,16,1]{3,0,2,1:T(8,128)}, u32[]{:S(2)}) copy-start(f32[6,3,16,1]{3,0,2,1:T(8,128)} %get-tuple-element.18) | copy-start | bytes 3460
  380.6 24.4 %copy-start.8 = (f32[6,3,16,1]{3,0,2,1:T(8,128)S(1)}, f32[6,3,16,1]{3,0,2,1:T(8,128)}, u32[]{:S(2)}) copy-start(f32[6,3,16,1]{3,0,2,1:T(8,128)} %get-tuple-element.19) | copy-start | bytes 3460
  380.7 15.9 %collective-permute-start.4 = (f32[3,1,2048]{2,1,0:T(1,128)S(1)}, f32[3,1,2048]{2,1,0:T(1,128)S(1)}, u32[]{:S(2)}, u32[]{:S(2)}) collective-permute-start(f32[3,1,2048]{2,1,0:T(1,128)S(1)} %get-tuple-element.49), channel_id=1, source_target_pairs={{16,0},{32,16},{48,32},{64,48},{80,64},{96,80},{112,96},{128,112},... | collective-permute-start | bytes 73736 | tf_op jit(solution)/shard_map/ppermute | solution.py:30
  392.9 4.5 %collective-permute-start.5 = (f32[3,1,2048]{2,1,0:T(1,128)S(1)}, f32[3,1,2048]{2,1,0:T(1,128)S(1)}, u32[]{:S(2)}, u32[]{:S(2)}) collective-permute-start(f32[3,1,2048]{2,1,0:T(1,128)S(1)} %get-tuple-element.50), channel_id=1, source_target_pairs={{0,16},{16,32},{32,48},{48,64},{64,80},{80,96},{96,112},{112,128},... | collective-permute-start | bytes 73736 | tf_op jit(solution)/shard_map/ppermute | solution.py:28
  398.0 15.7 %collective-permute-start.8 = (f32[3,1,2048]{2,1,0:T(1,128)S(1)}, f32[3,1,2048]{2,1,0:T(1,128)S(1)}, u32[]{:S(2)}, u32[]{:S(2)}) collective-permute-start(f32[3,1,2048]{2,1,0:T(1,128)S(1)} %get-tuple-element.45), channel_id=1, source_target_pairs={{16,0},{32,16},{48,32},{64,48},{80,64},{96,80},{112,96},{128,112},... | collective-permute-start | bytes 73736 | tf_op jit(solution)/shard_map/ppermute | solution.py:30
  402.8 10.9 %collective-permute-start.9 = (f32[3,1,2048]{2,1,0:T(1,128)S(1)}, f32[3,1,2048]{2,1,0:T(1,128)S(1)}, u32[]{:S(2)}, u32[]{:S(2)}) collective-permute-start(f32[3,1,2048]{2,1,0:T(1,128)S(1)} %get-tuple-element.46), channel_id=1, source_target_pairs={{0,16},{16,32},{32,48},{48,64},{64,80},{80,96},{96,112},{112,128},... | collective-permute-start | bytes 73736 | tf_op jit(solution)/shard_map/ppermute | solution.py:28
  410.8 2.9 copy-start.9
  414.3 5.7 %collective-permute-start.10 = (f32[3,1,2048]{2,1,0:T(1,128)S(1)}, f32[3,1,2048]{2,1,0:T(1,128)S(1)}, u32[]{:S(2)}, u32[]{:S(2)}) collective-permute-start(f32[3,1,2048]{2,1,0:T(1,128)S(1)} %get-tuple-element.37), channel_id=1, source_target_pairs={{16,0},{32,16},{48,32},{64,48},{80,64},{96,80},{112,96},{128,112},... | collective-permute-start | bytes 73736 | tf_op jit(solution)/shard_map/ppermute | solution.py:30
  416.7 5.9 %collective-permute-start.11 = (f32[3,1,2048]{2,1,0:T(1,128)S(1)}, f32[3,1,2048]{2,1,0:T(1,128)S(1)}, u32[]{:S(2)}, u32[]{:S(2)}) collective-permute-start(f32[3,1,2048]{2,1,0:T(1,128)S(1)} %get-tuple-element.38), channel_id=1, source_target_pairs={{0,16},{16,32},{32,48},{48,64},{64,80},{80,96},{96,112},{112,128},... | collective-permute-start | bytes 73736 | tf_op jit(solution)/shard_map/ppermute | solution.py:28
Sparse Core Ops, SparseCore 0:
  25.1 163.6 all-reduce.3
  202.5 175.8 all-reduce.5
where the time goes:
time: 434 us; the launch traced here: 431 us
  waiting for transfers between devices  304 us (70%)
  starting transfers between devices  63.2 us (15%)
  other arithmetic  28.7 us (7%)
  local copies, waits for them, and re-layouts  20.5 us (5%)
  between operations  14.4 us (3%)
    psum x2, waiting for transfers between devices, shards(): lax.psum((jnp.sum(square, 0), jnp.sum(square * square, 0)), 'grain')  300 us
    ppermute x6, starting transfers between devices, padded_2(): lax.ppermute(head, axis, [((i + 1) % count, i) for i in range(count)])  47.3 us
    reduce_sum x2, other arithmetic, shards(): jnp.sum(square * square, 0)  18.3 us
    ppermute x6, starting transfers between devices, padded_2(): lax.ppermute(tail, axis, [(i, (i + 1) % count) for i in range(count)])  15.8 us
    slice x12, local copies, waits for them, and re-layouts, laplace_padded(): along_y = jnp.roll(center, 1, -1) + jnp.roll(center, -1, -1)  11.6 us
  transfers between devices with their start and end apart: 14, of which 4 were waited for; matrix products, arithmetic and copies ran while one was open for 9% of the time, Pallas kernels for 0%

commit v1 on v0

v1 whole, which is shorter than its diff:
```python
import jax
import jax.numpy as jnp
from jax import lax
from jax.experimental import pallas as pl
from jax.experimental.pallas import tpu as pltpu
from jax.sharding import Mesh, PartitionSpec as P

GRAINS, PLANES, ROWS, COLS, LANES = 6, 3, 16, 2048, 128
BLOCKS = COLS // LANES
SPACE = ("yl", "z", "core")
GRAIN = ("x", "yh")

coef_quad = 1.0
coef_quart = 1.0
cross_gamma = 1.5
gradient_kappa = 0.5
solute_beta = 0.6
bulk_stiff = 1.0
solute_mean = 0.4
solute_kappa = 0.25
solute_mobility = 0.3
time_step = 0.1

F32 = jnp.float32
VMEM_LIMIT = 48 * 1024 * 1024


def shape(*dims):
    return jax.ShapeDtypeStruct(dims, F32)


def params():
    return pltpu.CompilerParams(vmem_limit_bytes=VMEM_LIMIT)


def whole(*dims):
    return pl.BlockSpec(dims, lambda *_: (0,) * len(dims))


def smem():
    return pl.BlockSpec(memory_space=pltpu.SMEM)


def along_columns(value):
    return pltpu.roll(value, 1, 1) + pltpu.roll(value, COLS - 1, 1)


def beside(planes):
    return (planes[0] + planes[1], planes[0] + planes[2], planes[1] + planes[2])


def column_block(block):
    return slice(block * LANES, (block + 1) * LANES)


def first_sums(first_ref, noise_ref, ids_ref, solute_ref, sums_ref, next_ref, prev_ref):
    for plane in range(PLANES):
        ids = ids_ref[plane]
        two = four = None
        for grain in range(GRAINS):
            seed = jnp.where(ids == first_ref[0] + grain, 0.9, 0.0).astype(F32)
            eta = seed + noise_ref[grain, plane]
            row = grain * PLANES + plane
            prev_ref[row : row + 1, :] = eta[:1]
            next_ref[row : row + 1, :] = eta[ROWS - 1 :]
            square = eta * eta
            two = square if two is None else two + square
            four = square * square if four is None else four + square * square
        for block in range(sums_ref.shape[0]):
            sums_ref[block, plane] = two[:, column_block(block)]
            sums_ref[block, PLANES + plane] = four[:, column_block(block)]
        row = GRAINS * PLANES + 3 * plane
        prev_ref[row : row + 3, :] = solute_ref[plane, :3]
        next_ref[row : row + 3, :] = solute_ref[plane, ROWS - 3 :]


def call_first_sums(first, noise, ids, solute):
    width = 512
    edge = GRAINS * PLANES + 3 * PLANES
    return pl.pallas_call(
        first_sums,
        grid=(COLS // width,),
        in_specs=[
            smem(),
            pl.BlockSpec((GRAINS, PLANES, ROWS, width), lambda i: (0, 0, 0, i)),
            pl.BlockSpec((PLANES, ROWS, width), lambda i: (0, 0, i)),
            pl.BlockSpec((PLANES, ROWS, width), lambda i: (0, 0, i)),
        ],
        out_specs=[
            pl.BlockSpec((width // LANES, 2 * PLANES, ROWS, LANES), lambda i: (i, 0, 0, 0)),
            pl.BlockSpec((edge, width), lambda i: (0, i)),
            pl.BlockSpec((edge, width), lambda i: (0, i)),
        ],
        out_shape=[
            shape(BLOCKS, 2 * PLANES, ROWS, LANES),
            shape(edge, COLS),
            shape(edge, COLS),
        ],
        compiler_params=params(),
        name="first_sums",
    )(first, noise, ids, solute)


def factors(sums_ref, solute_ref, base_ref, slope_ref):
    for plane in range(PLANES):
        for block in range(BLOCKS):
            columns = column_block(block)
            cross = 2.0 * cross_gamma - 4.0 * solute_beta * solute_ref[plane, :, columns]
            base_ref[plane, :, columns] = (
                coef_quad - 6.0 * gradient_kappa - sums_ref[block, plane] * cross
            )
            slope_ref[plane, :, columns] = cross - coef_quart


def stepped(planes, above, below, rate, base_ref, slope_ref):
    rows = lax.broadcasted_iota(jnp.int32, (ROWS, COLS), 0)
    out = []
    for plane, across in zip(range(PLANES), beside(planes)):
        eta = planes[plane]
        up = jnp.where(rows == 0, above[plane], pltpu.roll(eta, 1, 0))
        down = jnp.where(rows == ROWS - 1, below[plane], pltpu.roll(eta, ROWS - 1, 0))
        around = up + down + along_columns(eta) + across
        bracket = base_ref[plane] + slope_ref[plane] * (eta * eta)
        out.append(eta + rate * (eta * bracket + gradient_kappa * around))
    return out


def halo_rows(ref, grain):
    return [ref[pl.ds(grain * PLANES + plane, 1), :] for plane in range(PLANES)]


def first_step(
    first_ref, group_ref, mobility_ref, noise_ref, ids_ref, solute_ref, sums_ref, above_ref, below_ref,
    eta_ref, next_sums_ref, next_ref, prev_ref, base_ref, slope_ref,
):
    grain = pl.program_id(0)

    @pl.when(grain == 0)
    def _():
        factors(sums_ref, solute_ref, base_ref, slope_ref)
        for plane in range(PLANES):
            row = GRAINS * PLANES + 2 * plane
            for block in range(BLOCKS):
                columns = column_block(block)
                two, four = sums_ref[block, plane], sums_ref[block, PLANES + plane]
                bulk = solute_beta * (two * two - four)
                prev_ref[row : row + 2, columns] = bulk[:2]
                next_ref[row : row + 2, columns] = bulk[ROWS - 2 :]

    rate = time_step * mobility_ref[group_ref[grain]]
    planes = [
        jnp.where(ids_ref[plane] == first_ref[0] + grain, 0.9, 0.0).astype(F32) + noise_ref[0, plane]
        for plane in range(PLANES)
    ]
    out = stepped(planes, halo_rows(above_ref, grain), halo_rows(below_ref, grain), rate, base_ref, slope_ref)
    for plane in range(PLANES):
        eta = out[plane]
        eta_ref[0, plane] = eta
        row = pl.ds(grain * PLANES + plane, 1)
        prev_ref[row, :] = eta[:1]
        next_ref[row, :] = eta[ROWS - 1 :]
    for plane in range(PLANES):
        square = out[plane] * out[plane]
        fourth = square * square

        @pl.when(grain == 0)
        def _():
            for block in range(BLOCKS):
                next_sums_ref[block, plane] = square[:, column_block(block)]
                next_sums_ref[block, PLANES + plane] = fourth[:, column_block(block)]

        @pl.when(grain != 0)
        def _():
            for block in range(BLOCKS):
                next_sums_ref[block, plane] += square[:, column_block(block)]
                next_sums_ref[block, PLANES + plane] += fourth[:, column_block(block)]


def call_first_step(first, groups, mobility, noise, ids, solute, sums, above, below):
    edge = GRAINS * PLANES + 2 * PLANES
    grain_block = pl.BlockSpec((1, PLANES, ROWS, COLS), lambda i: (i, 0, 0, 0))
    return pl.pallas_call(
        first_step,
        grid=(GRAINS,),
        in_specs=[
            smem(), smem(), smem(), grain_block,
            whole(*ids.shape), whole(*solute.shape), whole(*sums.shape),
            whole(*above.shape), whole(*below.shape),
        ],
        out_specs=[grain_block, whole(*sums.shape), whole(edge, COLS), whole(edge, COLS)],
        out_shape=[shape(*noise.shape), shape(*sums.shape), shape(edge, COLS), shape(edge, COLS)],
        scratch_shapes=[pltpu.VMEM(solute.shape, F32)] * 2,
        compiler_params=params(),
        name="first_step",
    )(first, groups, mobility, noise, ids, solute, sums, above, below)


PAD = 8
DEEP = ROWS + 2 * PAD


def laplace(planes):
    height = planes[0].shape[0]
    return [
        pltpu.roll(value, 1, 0) + pltpu.roll(value, height - 1, 0) + along_columns(value) + across - 6.0 * value
        for value, across in zip(planes, beside(planes))
    ]


def solute_step(
    solute_ref, sums_ref, above_ref, below_ref, mid_above_ref, mid_below_ref,
    out_ref, part_ref, deep_ref, bulk_ref,
):
    for plane in range(PLANES):
        for ref in (deep_ref, bulk_ref):
            ref[plane, :PAD] = jnp.zeros((PAD, COLS), F32)
            ref[plane, PAD + ROWS :] = jnp.zeros((PAD, COLS), F32)
        row = GRAINS * PLANES + 3 * plane
        deep_ref[plane, PAD - 3 : PAD] = above_ref[row : row + 3, :]
        deep_ref[plane, PAD : PAD + ROWS] = solute_ref[plane]
        deep_ref[plane, PAD + ROWS : PAD + ROWS + 3] = below_ref[row : row + 3, :]
        row = GRAINS * PLANES + 2 * plane
        bulk_ref[plane, PAD - 2 : PAD] = mid_above_ref[row : row + 2, :]
        bulk_ref[plane, PAD + ROWS : PAD + ROWS + 2] = mid_below_ref[row : row + 2, :]
        for block in range(BLOCKS):
            two, four = sums_ref[block, plane], sums_ref[block, PLANES + plane]
            bulk_ref[plane, PAD : PAD + ROWS, column_block(block)] = solute_beta * (two * two - four)
    solute = [deep_ref[plane] for plane in range(PLANES)]
    potential = [
        2.0 * bulk_stiff * (solute[plane] - solute_mean) - bulk_ref[plane] - solute_kappa * lap
        for plane, lap in enumerate(laplace(solute))
    ]
    moved = [
        solute[plane] + time_step * solute_mobility * lap for plane, lap in enumerate(laplace(potential))
    ]
    for plane, lap in enumerate(laplace(moved)):
        part = 2.0 * bulk_stiff * (moved[plane] - solute_mean) - solute_kappa * lap
        out_ref[plane] = moved[plane][PAD : PAD + ROWS]
        part_ref[plane] = part[PAD : PAD + ROWS]


def call_solute_step(solute, sums, above, below, mid_above, mid_below):
    return pl.pallas_call(
        solute_step,
        out_shape=[shape(*solute.shape)] * 2,
        scratch_shapes=[pltpu.VMEM((PLANES, DEEP, COLS), F32)] * 2,
        compiler_params=params(),
        name="solute_step",
    )(solute, sums, above, below, mid_above, mid_below)


def second_potential(part_ref, sums_ref, out_ref, next_ref, prev_ref):
    for plane in range(PLANES):
        for block in range(BLOCKS):
            columns = column_block(block)
            two, four = sums_ref[block, plane], sums_ref[block, PLANES + plane]
            potential = part_ref[plane, :, columns] - solute_beta * (two * two - four)
            out_ref[plane, :, columns] = potential
            prev_ref[plane : plane + 1, columns] = potential[:1]
            next_ref[plane : plane + 1, columns] = potential[ROWS - 1 :]


def call_second_potential(part, sums):
    return pl.pallas_call(
        second_potential,
        out_shape=[shape(*part.shape), shape(PLANES, COLS), shape(PLANES, COLS)],
        compiler_params=params(),
        name="second_potential",
    )(part, sums)


def second_step(
    group_ref, mobility_ref, old_ref, solute_ref, sums_ref, above_ref, below_ref, eta_ref, base_ref, slope_ref
):
    grain = pl.program_id(0)

    @pl.when(grain == 0)
    def _():
        factors(sums_ref, solute_ref, base_ref, slope_ref)

    rate = time_step * mobility_ref[group_ref[grain]]
    planes = [old_ref[0, plane] for plane in range(PLANES)]
    out = stepped(planes, halo_rows(above_ref, grain), halo_rows(below_ref, grain), rate, base_ref, slope_ref)
    for plane in range(PLANES):
        eta_ref[0, plane] = out[plane]


def call_second_step(groups, mobility, eta, solute, sums, above, below):
    grain_block = pl.BlockSpec((1, PLANES, ROWS, COLS), lambda i: (i, 0, 0, 0))
    return pl.pallas_call(
        second_step,
        grid=(GRAINS,),
        in_specs=[
            smem(), smem(), grain_block, whole(*solute.shape), whole(*sums.shape),
            whole(*above.shape), whole(*below.shape),
        ],
        out_specs=grain_block,
        out_shape=shape(*eta.shape),
        scratch_shapes=[pltpu.VMEM(solute.shape, F32)] * 2,
        compiler_params=params(),
        cost_estimate=pl.CostEstimate(flops=20_000_000, bytes_accessed=10_000_000, transcendentals=0),
        name="second_step",
    )(groups, mobility, eta, solute, sums, above, below)


def solute_end(solute_ref, potential_ref, above_ref, below_ref, out_ref):
    rows = lax.broadcasted_iota(jnp.int32, (ROWS, COLS), 0)
    planes = [potential_ref[plane] for plane in range(PLANES)]
    for plane, across in enumerate(beside(planes)):
        value = planes[plane]
        up = jnp.where(rows == 0, above_ref[plane : plane + 1, :], pltpu.roll(value, 1, 0))
        down = jnp.where(rows == ROWS - 1, below_ref[plane : plane + 1, :], pltpu.roll(value, ROWS - 1, 0))
        lap = up + down + along_columns(value) + across - 6.0 * value
        out_ref[plane] = solute_ref[plane] + time_step * solute_mobility * lap


def call_solute_end(solute, potential, above, below):
    return pl.pallas_call(
        solute_end,
        out_shape=shape(*solute.shape),
        compiler_params=params(),
        name="solute_end",
    )(solute, potential, above, below)


def exchange(to_next, to_prev, count):
    above = lax.ppermute(to_next, SPACE, [(i, (i + 1) % count) for i in range(count)])
    below = lax.ppermute(to_prev, SPACE, [((i + 1) % count, i) for i in range(count)])
    return above, below


def total(sums):
    along, across = lax.axis_size("x"), lax.axis_size("yh")
    parts = sums.reshape((along, across) + sums.shape[1:])
    parts = jnp.sum(lax.all_to_all(parts, "x", 0, 0, tiled=True), 0)
    parts = jnp.sum(lax.all_to_all(parts, "yh", 0, 0, tiled=True), 0)
    parts = lax.all_gather(parts, "yh", axis=0)
    return lax.all_gather(parts, "x", axis=0).reshape(sums.shape)


def shards(grain_ids, group_of, group_mobility, seed_noise, concentration):
    count = lax.axis_size("yl") * lax.axis_size("z") * lax.axis_size("core")
    first = (lax.axis_index(GRAIN) * GRAINS).astype(jnp.int32).reshape(1)
    sums, to_next, to_prev = call_first_sums(first, seed_noise, grain_ids, concentration)
    above, below = exchange(to_next, to_prev, count)
    sums = total(sums)
    eta, next_sums, to_next, to_prev = call_first_step(
        first, group_of, group_mobility, seed_noise, grain_ids, concentration, sums, above, below
    )
    mid_above, mid_below = exchange(to_next, to_prev, count)
    next_sums = total(next_sums)
    solute, part = call_solute_step(concentration, sums, above, below, mid_above, mid_below)
    potential, to_next, to_prev = call_second_potential(part, next_sums)
    end_above, end_below = exchange(to_next, to_prev, count)
    eta = call_second_step(group_of, group_mobility, eta, solute, next_sums, mid_above, mid_below)
    solute = call_solute_end(solute, potential, end_above, end_below)
    return eta, solute


def solution(mesh):
    fine = Mesh(mesh.devices.reshape(2, 8, 2, 4, 4), SPACE + GRAIN)
    placed = (
        P(None, SPACE, None),
        P(GRAIN),
        P(),
        P(GRAIN, None, SPACE, None),
        P(None, SPACE, None),
    )
    return jax.shard_map(
        shards,
        mesh=fine,
        in_specs=placed,
        out_specs=(P(GRAIN, None, SPACE, None), P(None, SPACE, None)),
        check_vma=False,
    )
```

time: 434 us -> 164 us (0.38)
  waiting for transfers between devices: 304 us -> 3.36 us
  blocking collectives: 0 us -> 73.4 us
  other arithmetic: 28.7 us -> 3.65 us
  between operations: 14.4 us -> 0.84 us
  Pallas kernels: 0 us -> 13.3 us
  starting transfers between devices: 63.2 us -> 51.5 us
  local copies, waits for them, and re-layouts: 20.5 us -> 15 us
    psum x2 -> x0, waiting for transfers between devices: 300 us -> none  [shards(): lax.psum((jnp.sum(square, 0), jnp.sum(square * square, 0)), 'grain')]
    all_gather x0 -> x4, blocking collectives: none -> 48.8 us  [the longest x2 28 us: total(): parts = lax.all_gather(parts, 'yh', axis=0)]
    ppermute x12 -> x6, starting transfers between devices: 63.2 us -> 37.5 us  [the longest x3 25.6 us: exchange(): lax.ppermute(to_next, SPACE, [(i, (i + 1) % count) for i in range(count)])]
    all_to_all x0 -> x2, blocking collectives: none -> 24.6 us  [total(): parts = jnp.sum(lax.all_to_all(parts, 'x', 0, 0, tiled=True), 0)]
    slice x24 -> x0, local copies, waits for them, and re-layouts: 17.7 us -> none  [the longest x12 11.6 us: laplace_padded(): along_y = jnp.roll(center, 1, -1) + jnp.roll(center, -1, -1)]
    reduce_sum x3 -> x4, other arithmetic: 18.4 us -> 3.65 us  [the longest x2 2.61 us: total(): parts = jnp.sum(lax.all_to_all(parts, 'x', 0, 0, tiled=True), 0)]
    all_to_all x0 -> x2, starting transfers between devices: none -> 13.9 us  [total(): parts = jnp.sum(lax.all_to_all(parts, 'yh', 0, 0, tiled=True), 0)]
    pallas_call x0 -> x6, Pallas kernels: none -> 13.3 us  [the longest x1 5.25 us: call_first_step(): pl.pallas_call(first_step, grid=(GRAINS,), in_specs=[smem(), smem(), smem...]
  transfers between devices with their start and end apart: 14 -> 8, of which waited for: 4 -> 1; matrix products, arithmetic and copies ran while one was open for 9% -> 0% of each run, Pallas kernels for 0% -> 4%
where the time goes in v1:
time: 164 us; the launch traced here: 161 us
  blocking collectives  73.4 us (45%)
  starting transfers between devices  51.5 us (31%)
  local copies, waits for them, and re-layouts  15 us (9%)
  Pallas kernels  13.3 us (8%)
  other arithmetic  3.65 us (2%)
  waiting for transfers between devices  3.36 us (2%)
    all_gather x2, blocking collectives, total(): parts = lax.all_gather(parts, 'yh', axis=0)  28 us
    ppermute x3, starting transfers between devices, exchange(): lax.ppermute(to_next, SPACE, [(i, (i + 1) % count) for i in range(count)])  25.6 us
    all_to_all x2, blocking collectives, total(): parts = jnp.sum(lax.all_to_all(parts, 'x', 0, 0, tiled=True), 0)  24.6 us
    all_gather x2, blocking collectives, total(): return lax.all_gather(parts, 'x', axis=0).reshape(sums.shape)  20.8 us
    unnamed x46, local copies, waits for them, and re-layouts  15 us
    all_to_all x2, starting transfers between devices, total(): parts = jnp.sum(lax.all_to_all(parts, 'yh', 0, 0, tiled=True), 0)  13.9 us
    ppermute x3, starting transfers between devices, exchange(): lax.ppermute(to_prev, SPACE, [((i + 1) % count, i) for i in range(count)])  11.9 us
    pallas_call x1, Pallas kernels, call_first_step(): pl.pallas_call(first_step, grid=(GRAINS,), in_specs=[smem(), smem(), smem...  5.25 us
  transfers between devices with their start and end apart: 8, of which 1 were waited for; matrix products, arithmetic and copies ran while one was open for 0% of the time, Pallas kernels for 4%

profile of v1, /device:TPU:1, one launch (start us, length us, event | category | flops | bytes accessed | tf_op | source)
XLA Modules:
  0.0 161.0 jit_solution(9650736347462667545)
XLA Ops:
  0.6 0.0 copy-start
  0.6 1.7 %copy-done = f32[6,3,16,2048]{3,2,1,0:T(8,128)S(1)} copy-done((f32[6,3,16,2048]{3,2,1,0:T(8,128)S(1)}, f32[6,3,16,2048]{3,2,1,0:T(8,128)}, u32[]{:S(2)}) %copy-start) | copy-done | bytes 2359320
  2.3 1.0 copy-done.1
  3.3 1.0 copy-done.5
  4.3 1.0 first_sums.1
  5.3 0.0 copy-start.2
  5.3 0.0 copy-start.19
  5.3 0.0 copy-start.20
  5.4 13.1 %all_to_all.20 = f32[4,4,6,16,128]{4,3,2,1,0:T(8,128)S(1)} all-to-all(f32[4,4,6,16,128]{4,3,2,1,0:T(8,128)S(1)} %bitcast.6), channel_id=1, replica_groups=mesh['yl'=2,'z'=8,'core'=2,'x'=4,'yh'=4] {'x'}, dimensions={0} | all-to-all | bytes 1572864 | tf_op jit(solution)/shard_map/all_to_all | solution.py:335
  18.5 0.7 reduce_sum.36
  19.2 9.9 %all-to-all-start.1 = ((f32[4,6,16,128]{3,2,1,0:T(8,128)}), f32[4,6,16,128]{3,2,1,0:T(8,128)S(1)}, u32[]{:S(2)}, u32[]{:S(2)}) async-start(f32[4,6,16,128]{3,2,1,0:T(8,128)} %reduce_sum.36), calls=%async_computation.1 | async-start | bytes 393216 | tf_op jit(solution)/shard_map/all_to_all | solution.py:336
  29.0 6.0 %collective-permute-start = (f32[27,2048]{1,0:T(8,128)S(1)}, f32[27,2048]{1,0:T(8,128)S(1)}, u32[]{:S(2)}, u32[]{:S(2)}) collective-permute-start(f32[27,2048]{1,0:T(8,128)S(1)} %get-tuple-element.15), channel_id=1, source_target_pairs={{0,16},{16,32},{32,48},{48,64},{64,80},{80,96},{96,112},{112,128},... | collective-permute-start | bytes 663560 | tf_op jit(solution)/shard_map/ppermute | solution.py:327
  35.1 1.9 %collective-permute-start.1 = (f32[27,2048]{1,0:T(8,128)S(1)}, f32[27,2048]{1,0:T(8,128)S(1)}, u32[]{:S(2)}, u32[]{:S(2)}) collective-permute-start(f32[27,2048]{1,0:T(8,128)S(1)} %get-tuple-element.16), channel_id=1, source_target_pairs={{16,0},{32,16},{48,32},{64,48},{80,64},{96,80},{112,96},{128,112},... | collective-permute-start | bytes 663560 | tf_op jit(solution)/shard_map/ppermute | solution.py:328
  37.0 14.4 %all-gather = f32[24,16,128]{2,1,0:T(8,128)S(1)} all-gather(f32[6,16,128]{2,1,0:T(8,128)S(1)} %reduce_sum.37), channel_id=2, replica_groups=mesh['yl'=2,'z'=8,'core'=2,'x'=4,'yh'=4] {'yh'}, dimensions={0}, use_global_device_ids=true | all-gather | bytes 245760 | tf_op jit(solution)/shard_map/all_gather | solution.py:337
  51.4 10.4 %all-gather.1.sums_ref = f32[16,6,16,128]{3,2,1,0:T(8,128)S(1)} all-gather(f32[4,6,16,128]{3,2,1,0:T(8,128)S(1)} %bitcast.7), channel_id=3, replica_groups=mesh['yl'=2,'z'=8,'core'=2,'x'=4,'yh'=4] {'x'}, dimensions={0}, use_global_device_ids=true | all-gather | bytes 983040 | tf_op jit(solution)/shard_map/all_gather | solution.py:338
  61.8 0.7 copy-done.7
  62.5 0.0 collective-permute-done.1.below_ref
  62.5 0.7 copy-done.10
  63.2 1.0 copy-done.6
  64.2 0.9 copy-done.8
  65.2 0.9 copy-done.11
  66.1 5.3 %first_step.1 = (f32[6,3,16,2048]{3,2,1,0:T(8,128)S(1)}, f32[16,6,16,128]{3,2,1,0:T(8,128)S(1)}, f32[24,2048]{1,0:T(8,128)S(1)}, f32[24,2048]{1,0:T(8,128)S(1)}) custom-call(s32[1]{0:T(128)} %bitcast.first_ref, s32[6]{0:T(128)S(1)} %copy-done.19, f32[4]{0:T(128)S(1)} %copy-done.20, f32[6,3,16,2048]{3,2,1,0:T(8,128)} %noise_ref.3, ...), custom_call_target="tpu_custom_call" | custom-call | tf_op jit(solution)/shard_map/first_step/pallas_call | solution.py:182
  71.4 0.7 copy-done.21
  72.1 0.7 copy-done.22
  72.7 11.4 %all_to_all.21 = f32[4,4,6,16,128]{4,3,2,1,0:T(8,128)} all-to-all(f32[4,4,6,16,128]{4,3,2,1,0:T(8,128)S(1)} %bitcast.5), channel_id=1, replica_groups=mesh['yl'=2,'z'=8,'core'=2,'x'=4,'yh'=4] {'x'}, dimensions={0} | all-to-all | bytes 1572864 | tf_op jit(solution)/shard_map/all_to_all | solution.py:335
  84.2 1.9 %reduce_sum.38 = f32[4,6,16,128]{3,2,1,0:T(8,128)} reduce(f32[4,4,6,16,128]{4,3,2,1,0:T(8,128)} %all_to_all.21, f32[]{:T(128)} %constant.12.clone.1), dimensions={0}, to_apply=%region_2.0 | reduce | flops 147456 | bytes 983044 | tf_op jit(solution)/shard_map/reduce_sum | solution.py:335
  86.1 4.1 %all-to-all-start.3 = ((f32[4,6,16,128]{3,2,1,0:T(8,128)}), f32[4,6,16,128]{3,2,1,0:T(8,128)}, u32[]{:S(2)}, u32[]{:S(2)}) async-start(f32[4,6,16,128]{3,2,1,0:T(8,128)} %reduce_sum.38), calls=%async_computation.3 | async-start | bytes 393216 | tf_op jit(solution)/shard_map/all_to_all | solution.py:336
  90.1 11.3 %collective-permute-start.2 = (f32[24,2048]{1,0:T(8,128)}, f32[24,2048]{1,0:T(8,128)S(1)}, u32[]{:S(2)}, u32[]{:S(2)}) collective-permute-start(f32[24,2048]{1,0:T(8,128)} %copy-done.22), channel_id=1, source_target_pairs={{0,16},{16,32},{32,48},{48,64},{64,80},{80,96},{96,112},{112,128},... | collective-permute-start | bytes 589832 | tf_op jit(solution)/shard_map/ppermute | solution.py:327
  101.5 4.2 %collective-permute-start.3 = (f32[24,2048]{1,0:T(8,128)}, f32[24,2048]{1,0:T(8,128)S(1)}, u32[]{:S(2)}, u32[]{:S(2)}) collective-permute-start(f32[24,2048]{1,0:T(8,128)} %copy-done.21), channel_id=1, source_target_pairs={{16,0},{32,16},{48,32},{64,48},{80,64},{96,80},{112,96},{128,112},... | collective-permute-start | bytes 589832 | tf_op jit(solution)/shard_map/ppermute | solution.py:328
  105.7 0.0 collective-permute-done.2.mid_above_ref.above_ref
  105.7 3.3 %collective-permute-done.3.mid_below_ref.below_ref = f32[24,2048]{1,0:T(8,128)S(1)} collective-permute-done((f32[24,2048]{1,0:T(8,128)}, f32[24,2048]{1,0:T(8,128)S(1)}, u32[]{:S(2)}, u32[]{:S(2)}) %collective-permute-start.3) | collective-permute-done | bytes 196640 | tf_op jit(solution)/shard_map/ppermute | solution.py:328
  109.1 0.9 copy-done.9
  110.0 0.9 copy-done.12
  111.0 1.5 solute_step.1
  112.5 0.0 copy-start.3
  112.5 0.7 copy-done.3
  113.2 0.7 copy-done.13
  113.9 0.7 copy-done.15
  114.6 0.7 copy-done.17
  115.3 1.0 reduce_sum.39
  116.3 13.7 %all-gather.2 = f32[24,16,128]{2,1,0:T(8,128)S(1)} all-gather(f32[6,16,128]{2,1,0:T(8,128)S(1)} %reduce_sum.39), channel_id=4, replica_groups=mesh['yl'=2,'z'=8,'core'=2,'x'=4,'yh'=4] {'yh'}, dimensions={0}, use_global_device_ids=true | all-gather | bytes 245760 | tf_op jit(solution)/shard_map/all_gather | solution.py:337
  130.0 10.4 %all-gather.3.sums_ref = f32[16,6,16,128]{3,2,1,0:T(8,128)S(1)} all-gather(f32[4,6,16,128]{3,2,1,0:T(8,128)S(1)} %bitcast.8), channel_id=5, replica_groups=mesh['yl'=2,'z'=8,'core'=2,'x'=4,'yh'=4] {'x'}, dimensions={0}, use_global_device_ids=true | all-gather | bytes 983040 | tf_op jit(solution)/shard_map/all_gather | solution.py:338
  140.4 1.0 copy-done.18
  141.4 0.1 second_potential.1
  141.5 8.3 %collective-permute-start.4 = (f32[3,2048]{1,0:T(4,128)S(1)}, f32[3,2048]{1,0:T(4,128)S(1)}, u32[]{:S(2)}, u32[]{:S(2)}) collective-permute-start(f32[3,2048]{1,0:T(4,128)S(1)} %get-tuple-element.24), channel_id=1, source_target_pairs={{0,16},{16,32},{32,48},{48,64},{64,80},{80,96},{96,112},{112,128},... | collective-permute-start | bytes 73736 | tf_op jit(solution)/shard_map/ppermute | solution.py:327
  149.8 5.8 %collective-permute-start.5 = (f32[3,2048]{1,0:T(4,128)S(1)}, f32[3,2048]{1,0:T(4,128)S(1)}, u32[]{:S(2)}, u32[]{:S(2)}) collective-permute-start(f32[3,2048]{1,0:T(4,128)S(1)} %get-tuple-element.25), channel_id=1, source_target_pairs={{16,0},{32,16},{48,32},{64,48},{80,64},{96,80},{112,96},{128,112},... | collective-permute-start | bytes 73736 | tf_op jit(solution)/shard_map/ppermute | solution.py:328
  155.6 4.4 %second_step.1 = f32[6,3,16,2048]{3,2,1,0:T(8,128)} custom-call(s32[6]{0:T(128)S(1)} %copy-done.19, f32[4]{0:T(128)S(1)} %copy-done.20, f32[6,3,16,2048]{3,2,1,0:T(8,128)S(1)} %get-tuple-element.17.old_ref, f32[3,16,2048]{2,1,0:T(8,128)S(1)} %copy-done.4, f32[16,6,16,128]{3,2,1,0:T(8,128)S(1)} %all-gather.3.sums_ref, f32[24,2048]{1,0:T(8,128)S(1)} %copy-done.14, ...), custom_call_target="tpu_custom_call" | custom-call | flops 20000000 | bytes 10000000 | tf_op jit(solution)/shard_map/second_step/pallas_call | solution.py:290
  159.9 1.1 solute_end.1
  (30 shorter events, 0.1 us)
Async XLA Ops:
  0.6 1.7 %copy-start = (f32[6,3,16,2048]{3,2,1,0:T(8,128)S(1)}, f32[6,3,16,2048]{3,2,1,0:T(8,128)}, u32[]{:S(2)}) copy-start(f32[6,3,16,2048]{3,2,1,0:T(8,128)} %noise_ref.3) | copy-start | bytes 7077892
  2.3 1.0 copy-start.1
  3.3 1.0 copy-start.5
  5.3 57.9 %copy-start.2 = (f32[3,16,2048]{2,1,0:T(8,128)S(1)}, f32[3,16,2048]{2,1,0:T(8,128)}, u32[]{:S(2)}) copy-start(f32[3,16,2048]{2,1,0:T(8,128)} %solute_ref.5) | copy-start | bytes 1179652
  5.3 57.9 %copy-start.19 = (s32[6]{0:T(128)S(1)}, s32[6]{0:T(128)}, u32[]{:S(2)}) copy-start(s32[6]{0:T(128)} %group_ref.3) | copy-start | bytes 76
  5.3 57.9 %copy-start.20 = (f32[4]{0:T(128)S(1)}, f32[4]{0:T(128)}, u32[]{:S(2)}) copy-start(f32[4]{0:T(128)} %mobility_ref.3) | copy-start | bytes 52
  19.2 17.8 %all-to-all-start.1 = ((f32[4,6,16,128]{3,2,1,0:T(8,128)}), f32[4,6,16,128]{3,2,1,0:T(8,128)S(1)}, u32[]{:S(2)}, u32[]{:S(2)}) async-start(f32[4,6,16,128]{3,2,1,0:T(8,128)} %reduce_sum.36), calls=%async_computation.1 | async-start | bytes 393216 | tf_op jit(solution)/shard_map/all_to_all | solution.py:336
  29.0 32.8 %collective-permute-start = (f32[27,2048]{1,0:T(8,128)S(1)}, f32[27,2048]{1,0:T(8,128)S(1)}, u32[]{:S(2)}, u32[]{:S(2)}) collective-permute-start(f32[27,2048]{1,0:T(8,128)S(1)} %get-tuple-element.15), channel_id=1, source_target_pairs={{0,16},{16,32},{32,48},{48,64},{64,80},{80,96},{96,112},{112,128},... | collective-permute-start | bytes 663560 | tf_op jit(solution)/shard_map/ppermute | solution.py:327
  35.1 27.4 %collective-permute-start.1 = (f32[27,2048]{1,0:T(8,128)S(1)}, f32[27,2048]{1,0:T(8,128)S(1)}, u32[]{:S(2)}, u32[]{:S(2)}) collective-permute-start(f32[27,2048]{1,0:T(8,128)S(1)} %get-tuple-element.16), channel_id=1, source_target_pairs={{16,0},{32,16},{48,32},{64,48},{80,64},{96,80},{112,96},{128,112},... | collective-permute-start | bytes 663560 | tf_op jit(solution)/shard_map/ppermute | solution.py:328
  61.8 0.7 copy-start.7
  62.5 0.7 copy-start.10
  63.2 1.0 copy-start.6
  64.2 0.9 copy-start.8
  65.2 0.9 copy-start.11
  71.4 0.7 copy-start.21
  72.1 0.7 copy-start.22
  86.1 29.2 %all-to-all-start.3 = ((f32[4,6,16,128]{3,2,1,0:T(8,128)}), f32[4,6,16,128]{3,2,1,0:T(8,128)}, u32[]{:S(2)}, u32[]{:S(2)}) async-start(f32[4,6,16,128]{3,2,1,0:T(8,128)} %reduce_sum.38), calls=%async_computation.3 | async-start | bytes 393216 | tf_op jit(solution)/shard_map/all_to_all | solution.py:336
  90.1 15.6 %collective-permute-start.2 = (f32[24,2048]{1,0:T(8,128)}, f32[24,2048]{1,0:T(8,128)S(1)}, u32[]{:S(2)}, u32[]{:S(2)}) collective-permute-start(f32[24,2048]{1,0:T(8,128)} %copy-done.22), channel_id=1, source_target_pairs={{0,16},{16,32},{32,48},{48,64},{64,80},{80,96},{96,112},{112,128},... | collective-permute-start | bytes 589832 | tf_op jit(solution)/shard_map/ppermute | solution.py:327
  101.5 7.6 %collective-permute-start.3 = (f32[24,2048]{1,0:T(8,128)}, f32[24,2048]{1,0:T(8,128)S(1)}, u32[]{:S(2)}, u32[]{:S(2)}) collective-permute-start(f32[24,2048]{1,0:T(8,128)} %copy-done.21), channel_id=1, source_target_pairs={{16,0},{32,16},{48,32},{64,48},{80,64},{96,80},{112,96},{128,112},... | collective-permute-start | bytes 589832 | tf_op jit(solution)/shard_map/ppermute | solution.py:328
  109.1 1.0 copy-start.9
  110.0 0.9 copy-start.12
  112.5 0.7 copy-start.3
  113.2 0.7 copy-start.13
  113.9 0.7 copy-start.15
  114.6 0.7 copy-start.17
  115.3 40.2 %copy-start.4 = (f32[3,16,2048]{2,1,0:T(8,128)S(1)}, f32[3,16,2048]{2,1,0:T(8,128)}, u32[]{:S(2)}) copy-start(f32[3,16,2048]{2,1,0:T(8,128)} %copy-done.3) | copy-start | bytes 1179652
  115.3 40.2 %copy-start.14 = (f32[24,2048]{1,0:T(8,128)S(1)}, f32[24,2048]{1,0:T(8,128)}, u32[]{:S(2)}) copy-start(f32[24,2048]{1,0:T(8,128)} %copy-done.13) | copy-start | bytes 589828
  115.3 40.2 %copy-start.16 = (f32[24,2048]{1,0:T(8,128)S(1)}, f32[24,2048]{1,0:T(8,128)}, u32[]{:S(2)}) copy-start(f32[24,2048]{1,0:T(8,128)} %copy-done.15) | copy-start | bytes 589828
  140.4 1.0 copy-start.18
  141.5 18.4 %collective-permute-start.4 = (f32[3,2048]{1,0:T(4,128)S(1)}, f32[3,2048]{1,0:T(4,128)S(1)}, u32[]{:S(2)}, u32[]{:S(2)}) collective-permute-start(f32[3,2048]{1,0:T(4,128)S(1)} %get-tuple-element.24), channel_id=1, source_target_pairs={{0,16},{16,32},{32,48},{48,64},{64,80},{80,96},{96,112},{112,128},... | collective-permute-start | bytes 73736 | tf_op jit(solution)/shard_map/ppermute | solution.py:327
  149.8 10.2 %collective-permute-start.5 = (f32[3,2048]{1,0:T(4,128)S(1)}, f32[3,2048]{1,0:T(4,128)S(1)}, u32[]{:S(2)}, u32[]{:S(2)}) collective-permute-start(f32[3,2048]{1,0:T(4,128)S(1)} %get-tuple-element.25), channel_id=1, source_target_pairs={{16,0},{32,16},{48,32},{64,48},{80,64},{96,80},{112,96},{128,112},... | collective-permute-start | bytes 73736 | tf_op jit(solution)/shard_map/ppermute | solution.py:328

commit v2 on v1

--- a/solution.py
+++ b/solution.py
@@ -22,15 +22,15 @@
 time_step = 0.1
 
 F32 = jnp.float32
-VMEM_LIMIT = 48 * 1024 * 1024
+MIB = 1024 * 1024
 
 
 def shape(*dims):
     return jax.ShapeDtypeStruct(dims, F32)
 
 
-def params():
-    return pltpu.CompilerParams(vmem_limit_bytes=VMEM_LIMIT)
+def params(mib=16):
+    return pltpu.CompilerParams(vmem_limit_bytes=mib * MIB)
 
 
 def whole(*dims):
@@ -96,7 +96,7 @@
             shape(edge, COLS),
             shape(edge, COLS),
         ],
-        compiler_params=params(),
+        compiler_params=params(60),
         name="first_sums",
     )(first, noise, ids, solute)
 
@@ -329,13 +329,17 @@
     return above, below
 
 
+def spread(value, axis):
+    copies = jnp.broadcast_to(value[None], (lax.axis_size(axis),) + value.shape)
+    return lax.all_to_all(copies, axis, 0, 0, tiled=True)
+
+
 def total(sums):
-    along, across = lax.axis_size("x"), lax.axis_size("yh")
-    parts = sums.reshape((along, across) + sums.shape[1:])
+    along = lax.axis_size("x")
+    parts = sums.reshape((along, BLOCKS // along) + sums.shape[1:])
     parts = jnp.sum(lax.all_to_all(parts, "x", 0, 0, tiled=True), 0)
-    parts = jnp.sum(lax.all_to_all(parts, "yh", 0, 0, tiled=True), 0)
-    parts = lax.all_gather(parts, "yh", axis=0)
-    return lax.all_gather(parts, "x", axis=0).reshape(sums.shape)
+    parts = jnp.sum(spread(parts, "yh"), 0)
+    return spread(parts, "x").reshape(sums.shape)
 
 
 def shards(grain_ids, group_of, group_mobility, seed_noise, concentration):

time: 164 us -> 154 us (0.939)
  the two profiles are of different devices: /device:TPU:1 before, /device:TPU:8 now
where the time goes in v2:
time: 154 us; the launch traced here: 153 us
  blocking collectives  77.7 us (50%)
  starting transfers between devices  39 us (25%)
  Pallas kernels  14.6 us (9%)
  local copies, waits for them, and re-layouts  13.5 us (9%)
  waiting for transfers between devices  6.66 us (4%)
    all_to_all x2, blocking collectives, spread(): return lax.all_to_all(copies, axis, 0, 0, tiled=True)  47.4 us
    all_to_all x2, blocking collectives, total(): parts = jnp.sum(lax.all_to_all(parts, 'x', 0, 0, tiled=True), 0)  30.3 us
    ppermute x3, starting transfers between devices, exchange(): lax.ppermute(to_prev, SPACE, [((i + 1) % count, i) for i in range(count)])  26.3 us
    unnamed x38, local copies, waits for them, and re-layouts  10.5 us
    all_to_all x2, starting transfers between devices, spread(): return lax.all_to_all(copies, axis, 0, 0, tiled=True)  6.99 us
    ppermute x3, starting transfers between devices, exchange(): lax.ppermute(to_next, SPACE, [(i, (i + 1) % count) for i in range(count)])  5.76 us
    pallas_call x1, Pallas kernels, call_second_step(): pl.pallas_call(second_step, grid=(GRAINS,), in_specs=[smem(), smem(), gra...  4.35 us
    pallas_call x1, Pallas kernels, call_first_sums(): pl.pallas_call(first_sums, grid=(COLS // width,), in_specs=[smem(), pl.Bl...  4 us
  transfers between devices with their start and end apart: 8, of which 4 were waited for; matrix products, arithmetic and copies ran while one was open for 0% of the time, Pallas kernels for 4%

profile of v2, /device:TPU:8, one launch (start us, length us, event | category | flops | bytes accessed | tf_op | source)
XLA Modules:
  0.0 153.2 jit_solution(8611406938718937313)
XLA Ops:
  0.6 4.0 %first_sums.1 = (f32[16,6,16,128]{3,2,1,0:T(8,128)}, f32[27,2048]{1,0:T(8,128)}, f32[27,2048]{1,0:T(8,128)}) custom-call(s32[1]{0:T(128)} %bitcast.first_ref, f32[6,3,16,2048]{3,2,1,0:T(8,128)} %noise_ref.3, s32[3,16,2048]{2,1,0:T(8,128)} %ids_ref.3, f32[3,16,2048]{2,1,0:T(8,128)} %solute_ref.5), custom_call_target="tpu_custom_call" | custom-call | tf_op jit(solution)/shard_map/first_sums/pallas_call | solution.py:80
  4.6 16.6 %all_to_all.30 = f32[4,4,6,16,128]{4,3,2,1,0:T(8,128)S(1)} all-to-all(f32[4,4,6,16,128]{4,3,2,1,0:T(8,128)} %bitcast.10), channel_id=1, replica_groups=mesh['yl'=2,'z'=8,'core'=2,'x'=4,'yh'=4] {'x'}, dimensions={0} | all-to-all | bytes 1572864 | tf_op jit(solution)/shard_map/all_to_all | solution.py:340
  21.2 0.1 reduce_sum.36
  21.3 0.1 broadcast_in_dim.8
  21.3 0.0 copy-start
  21.4 0.0 copy-start.1
  21.4 0.0 copy-start.13
  21.4 0.0 copy-start.14
  21.4 24.6 %all_to_all.31 = f32[4,4,6,16,128]{4,3,2,1,0:T(8,128)S(1)} all-to-all(f32[4,4,6,16,128]{4,3,2,1,0:T(8,128)S(1)} %broadcast_in_dim.8), channel_id=1, replica_groups=mesh['yl'=2,'z'=8,'core'=2,'x'=4,'yh'=4] {'yh'}, dimensions={0} | all-to-all | bytes 1572864 | tf_op jit(solution)/shard_map/all_to_all | solution.py:334
  46.0 0.7 reduce_sum.37
  46.8 1.9 %broadcast_in_dim.9 = f32[4,4,6,16,128]{4,3,2,1,0:T(8,128)} broadcast(f32[4,6,16,128]{3,2,1,0:T(8,128)} %reduce_sum.37), dimensions={1,2,3,4} | broadcast | bytes 983040 | tf_op jit(solution)/shard_map/broadcast_in_dim | solution.py:333
  48.6 3.5 %all-to-all-start.2 = ((f32[4,4,6,16,128]{4,3,2,1,0:T(8,128)}), f32[4,4,6,16,128]{4,3,2,1,0:T(8,128)S(1)}, u32[]{:S(2)}, u32[]{:S(2)}) async-start(f32[4,4,6,16,128]{4,3,2,1,0:T(8,128)} %broadcast_in_dim.9), calls=%async_computation.2 | async-start | bytes 1572864 | tf_op jit(solution)/shard_map/all_to_all | solution.py:334
  52.1 1.9 %collective-permute-start = (f32[27,2048]{1,0:T(8,128)}, f32[27,2048]{1,0:T(8,128)S(1)}, u32[]{:S(2)}, u32[]{:S(2)}) collective-permute-start(f32[27,2048]{1,0:T(8,128)} %get-tuple-element.15), channel_id=1, source_target_pairs={{0,16},{16,32},{32,48},{48,64},{64,80},{80,96},{96,112},{112,128},... | collective-permute-start | bytes 663560 | tf_op jit(solution)/shard_map/ppermute | solution.py:327
  54.1 11.8 %collective-permute-start.1 = (f32[27,2048]{1,0:T(8,128)}, f32[27,2048]{1,0:T(8,128)S(1)}, u32[]{:S(2)}, u32[]{:S(2)}) collective-permute-start(f32[27,2048]{1,0:T(8,128)} %get-tuple-element.16), channel_id=1, source_target_pairs={{16,0},{32,16},{48,32},{64,48},{80,64},{96,80},{112,96},{128,112},... | collective-permute-start | bytes 663560 | tf_op jit(solution)/shard_map/ppermute | solution.py:328
  65.8 2.3 %collective-permute-done.above_ref = f32[27,2048]{1,0:T(8,128)S(1)} collective-permute-done((f32[27,2048]{1,0:T(8,128)}, f32[27,2048]{1,0:T(8,128)S(1)}, u32[]{:S(2)}, u32[]{:S(2)}) %collective-permute-start) | collective-permute-done | bytes 221216 | tf_op jit(solution)/shard_map/ppermute | solution.py:327
  68.2 0.7 copy-done.5
  68.9 1.2 collective-permute-done.1.below_ref
  70.0 0.7 copy-done.8
  70.8 0.0 copy-start.4
  70.8 1.0 copy-done.4
  71.8 0.9 copy-done.6
  72.7 0.9 copy-done.9
  73.7 3.6 %first_step.1 = (f32[6,3,16,2048]{3,2,1,0:T(8,128)S(1)}, f32[16,6,16,128]{3,2,1,0:T(8,128)S(1)}, f32[24,2048]{1,0:T(8,128)S(1)}, f32[24,2048]{1,0:T(8,128)S(1)}) custom-call(s32[1]{0:T(128)} %bitcast.first_ref, s32[6]{0:T(128)S(1)} %copy-done.13, f32[4]{0:T(128)S(1)} %copy-done.14, f32[6,3,16,2048]{3,2,1,0:T(8,128)S(1)} %copy-done, ...), custom_call_target="tpu_custom_call" | custom-call | tf_op jit(solution)/shard_map/first_step/pallas_call | solution.py:182
  77.3 0.0 copy-start.2
  77.3 1.4 copy-done.2
  78.7 0.7 copy-done.15
  79.4 0.7 copy-done.17
  80.0 13.7 %all_to_all.32 = f32[4,4,6,16,128]{4,3,2,1,0:T(8,128)S(1)} all-to-all(f32[4,4,6,16,128]{4,3,2,1,0:T(8,128)S(1)} %bitcast.9), channel_id=1, replica_groups=mesh['yl'=2,'z'=8,'core'=2,'x'=4,'yh'=4] {'x'}, dimensions={0} | all-to-all | bytes 1572864 | tf_op jit(solution)/shard_map/all_to_all | solution.py:340
  93.8 0.1 reduce_sum.38
  93.9 0.1 broadcast_in_dim.10
  93.9 0.0 copy-start.7
  94.0 22.8 %all_to_all.33 = f32[4,4,6,16,128]{4,3,2,1,0:T(8,128)S(1)} all-to-all(f32[4,4,6,16,128]{4,3,2,1,0:T(8,128)S(1)} %broadcast_in_dim.10), channel_id=1, replica_groups=mesh['yl'=2,'z'=8,'core'=2,'x'=4,'yh'=4] {'yh'}, dimensions={0} | all-to-all | bytes 1572864 | tf_op jit(solution)/shard_map/all_to_all | solution.py:334
  116.7 0.1 reduce_sum.39
  116.8 1.0 broadcast_in_dim.11
  117.7 3.5 %all-to-all-start.5 = ((f32[4,4,6,16,128]{4,3,2,1,0:T(8,128)}), f32[4,4,6,16,128]{4,3,2,1,0:T(8,128)S(1)}, u32[]{:S(2)}, u32[]{:S(2)}) async-start(f32[4,4,6,16,128]{4,3,2,1,0:T(8,128)} %broadcast_in_dim.11), calls=%async_computation.5 | async-start | bytes 1572864 | tf_op jit(solution)/shard_map/all_to_all | solution.py:334
  121.3 1.9 %collective-permute-start.2 = (f32[24,2048]{1,0:T(8,128)S(1)}, f32[24,2048]{1,0:T(8,128)S(1)}, u32[]{:S(2)}, u32[]{:S(2)}) collective-permute-start(f32[24,2048]{1,0:T(8,128)S(1)} %copy-done.18), channel_id=1, source_target_pairs={{0,16},{16,32},{32,48},{48,64},{64,80},{80,96},{96,112},{112,128},... | collective-permute-start | bytes 589832 | tf_op jit(solution)/shard_map/ppermute | solution.py:327
  123.2 8.3 %collective-permute-start.3 = (f32[24,2048]{1,0:T(8,128)S(1)}, f32[24,2048]{1,0:T(8,128)S(1)}, u32[]{:S(2)}, u32[]{:S(2)}) collective-permute-start(f32[24,2048]{1,0:T(8,128)S(1)} %copy-done.16), channel_id=1, source_target_pairs={{16,0},{32,16},{48,32},{64,48},{80,64},{96,80},{112,96},{128,112},... | collective-permute-start | bytes 589832 | tf_op jit(solution)/shard_map/ppermute | solution.py:328
  131.5 1.4 collective-permute-done.2.mid_above_ref.above_ref
  132.9 1.8 %collective-permute-done.3.mid_below_ref.below_ref = f32[24,2048]{1,0:T(8,128)S(1)} collective-permute-done((f32[24,2048]{1,0:T(8,128)S(1)}, f32[24,2048]{1,0:T(8,128)S(1)}, u32[]{:S(2)}, u32[]{:S(2)}) %collective-permute-start.3) | collective-permute-done | bytes 196640 | tf_op jit(solution)/shard_map/ppermute | solution.py:328
  134.7 1.5 solute_step.1
  136.2 0.7 copy-done.11
  136.9 1.0 copy-done.12
  137.9 0.1 second_potential.1
  138.0 1.9 %collective-permute-start.4 = (f32[3,2048]{1,0:T(4,128)S(1)}, f32[3,2048]{1,0:T(4,128)S(1)}, u32[]{:S(2)}, u32[]{:S(2)}) collective-permute-start(f32[3,2048]{1,0:T(4,128)S(1)} %get-tuple-element.24), channel_id=1, source_target_pairs={{0,16},{16,32},{32,48},{48,64},{64,80},{80,96},{96,112},{112,128},... | collective-permute-start | bytes 73736 | tf_op jit(solution)/shard_map/ppermute | solution.py:327
  139.9 6.2 %collective-permute-start.5 = (f32[3,2048]{1,0:T(4,128)S(1)}, f32[3,2048]{1,0:T(4,128)S(1)}, u32[]{:S(2)}, u32[]{:S(2)}) collective-permute-start(f32[3,2048]{1,0:T(4,128)S(1)} %get-tuple-element.25), channel_id=1, source_target_pairs={{16,0},{32,16},{48,32},{64,48},{80,64},{96,80},{112,96},{128,112},... | collective-permute-start | bytes 73736 | tf_op jit(solution)/shard_map/ppermute | solution.py:328
  146.1 1.7 %copy-done.3 = f32[6,3,16,2048]{3,2,1,0:T(8,128)S(1)} copy-done((f32[6,3,16,2048]{3,2,1,0:T(8,128)S(1)}, f32[6,3,16,2048]{3,2,1,0:T(8,128)}, u32[]{:S(2)}) %copy-start.3) | copy-done | bytes 2359320
  147.8 4.3 %second_step.1 = f32[6,3,16,2048]{3,2,1,0:T(8,128)} custom-call(s32[6]{0:T(128)S(1)} %copy-done.13, f32[4]{0:T(128)S(1)} %copy-done.14, f32[6,3,16,2048]{3,2,1,0:T(8,128)S(1)} %copy-done.3, f32[3,16,2048]{2,1,0:T(8,128)S(1)} %get-tuple-element.20.solute_ref, f32[16,6,16,128]{3,2,1,0:T(8,128)S(1)} %bitcast.6, ...), custom_call_target="tpu_custom_call" | custom-call | flops 20000000 | bytes 10000000 | tf_op jit(solution)/shard_map/second_step/pallas_call | solution.py:290
  152.2 1.1 solute_end.1
  (24 shorter events, 0.1 us)
Async XLA Ops:
  21.3 49.4 %copy-start = (f32[6,3,16,2048]{3,2,1,0:T(8,128)S(1)}, f32[6,3,16,2048]{3,2,1,0:T(8,128)}, u32[]{:S(2)}) copy-start(f32[6,3,16,2048]{3,2,1,0:T(8,128)} %noise_ref.3) | copy-start | bytes 7077892
  21.4 49.4 %copy-start.1 = (f32[3,16,2048]{2,1,0:T(8,128)S(1)}, f32[3,16,2048]{2,1,0:T(8,128)}, u32[]{:S(2)}) copy-start(f32[3,16,2048]{2,1,0:T(8,128)} %solute_ref.5) | copy-start | bytes 1179652
  21.4 49.4 %copy-start.13 = (s32[6]{0:T(128)S(1)}, s32[6]{0:T(128)}, u32[]{:S(2)}) copy-start(s32[6]{0:T(128)} %group_ref.3) | copy-start | bytes 76
  21.4 49.4 %copy-start.14 = (f32[4]{0:T(128)S(1)}, f32[4]{0:T(128)}, u32[]{:S(2)}) copy-start(f32[4]{0:T(128)} %mobility_ref.3) | copy-start | bytes 52
  48.6 22.1 %all-to-all-start.2 = ((f32[4,4,6,16,128]{4,3,2,1,0:T(8,128)}), f32[4,4,6,16,128]{4,3,2,1,0:T(8,128)S(1)}, u32[]{:S(2)}, u32[]{:S(2)}) async-start(f32[4,4,6,16,128]{4,3,2,1,0:T(8,128)} %broadcast_in_dim.9), calls=%async_computation.2 | async-start | bytes 1572864 | tf_op jit(solution)/shard_map/all_to_all | solution.py:334
  52.1 16.0 %collective-permute-start = (f32[27,2048]{1,0:T(8,128)}, f32[27,2048]{1,0:T(8,128)S(1)}, u32[]{:S(2)}, u32[]{:S(2)}) collective-permute-start(f32[27,2048]{1,0:T(8,128)} %get-tuple-element.15), channel_id=1, source_target_pairs={{0,16},{16,32},{32,48},{48,64},{64,80},{80,96},{96,112},{112,128},... | collective-permute-start | bytes 663560 | tf_op jit(solution)/shard_map/ppermute | solution.py:327
  54.1 16.0 %collective-permute-start.1 = (f32[27,2048]{1,0:T(8,128)}, f32[27,2048]{1,0:T(8,128)S(1)}, u32[]{:S(2)}, u32[]{:S(2)}) collective-permute-start(f32[27,2048]{1,0:T(8,128)} %get-tuple-element.16), channel_id=1, source_target_pairs={{16,0},{32,16},{48,32},{64,48},{80,64},{96,80},{112,96},{128,112},... | collective-permute-start | bytes 663560 | tf_op jit(solution)/shard_map/ppermute | solution.py:328
  68.2 0.7 copy-start.5
  70.0 0.7 copy-start.8
  70.8 1.0 copy-start.4
  71.8 0.9 copy-start.6
  72.7 0.9 copy-start.9
  77.3 1.4 copy-start.2
  78.7 0.7 copy-start.15
  79.4 0.7 copy-start.17
  93.9 27.3 %copy-start.18 = (f32[24,2048]{1,0:T(8,128)S(1)}, f32[24,2048]{1,0:T(8,128)}, u32[]{:S(2)}) copy-start(f32[24,2048]{1,0:T(8,128)} %copy-done.17) | copy-start | bytes 589828
  93.9 29.2 %copy-start.16 = (f32[24,2048]{1,0:T(8,128)S(1)}, f32[24,2048]{1,0:T(8,128)}, u32[]{:S(2)}) copy-start(f32[24,2048]{1,0:T(8,128)} %copy-done.15) | copy-start | bytes 589828
  93.9 40.7 %copy-start.7 = (f32[27,2048]{1,0:T(8,128)S(1)}, f32[27,2048]{1,0:T(8,128)}, u32[]{:S(2)}) copy-start(f32[27,2048]{1,0:T(8,128)} %copy-done.5) | copy-start | bytes 663556
  94.0 40.7 %copy-start.10 = (f32[27,2048]{1,0:T(8,128)S(1)}, f32[27,2048]{1,0:T(8,128)}, u32[]{:S(2)}) copy-start(f32[27,2048]{1,0:T(8,128)} %copy-done.8) | copy-start | bytes 663556
  117.7 19.2 %all-to-all-start.5 = ((f32[4,4,6,16,128]{4,3,2,1,0:T(8,128)}), f32[4,4,6,16,128]{4,3,2,1,0:T(8,128)S(1)}, u32[]{:S(2)}, u32[]{:S(2)}) async-start(f32[4,4,6,16,128]{4,3,2,1,0:T(8,128)} %broadcast_in_dim.11), calls=%async_computation.5 | async-start | bytes 1572864 | tf_op jit(solution)/shard_map/all_to_all | solution.py:334
  121.3 11.6 %collective-permute-start.2 = (f32[24,2048]{1,0:T(8,128)S(1)}, f32[24,2048]{1,0:T(8,128)S(1)}, u32[]{:S(2)}, u32[]{:S(2)}) collective-permute-start(f32[24,2048]{1,0:T(8,128)S(1)} %copy-done.18), channel_id=1, source_target_pairs={{0,16},{16,32},{32,48},{48,64},{64,80},{80,96},{96,112},{112,128},... | collective-permute-start | bytes 589832 | tf_op jit(solution)/shard_map/ppermute | solution.py:327
  123.2 11.5 %collective-permute-start.3 = (f32[24,2048]{1,0:T(8,128)S(1)}, f32[24,2048]{1,0:T(8,128)S(1)}, u32[]{:S(2)}, u32[]{:S(2)}) collective-permute-start(f32[24,2048]{1,0:T(8,128)S(1)} %copy-done.16), channel_id=1, source_target_pairs={{16,0},{32,16},{48,32},{64,48},{80,64},{96,80},{112,96},{128,112},... | collective-permute-start | bytes 589832 | tf_op jit(solution)/shard_map/ppermute | solution.py:328
  136.1 0.7 copy-start.11
  136.9 1.0 copy-start.12
  138.0 14.2 %collective-permute-start.4 = (f32[3,2048]{1,0:T(4,128)S(1)}, f32[3,2048]{1,0:T(4,128)S(1)}, u32[]{:S(2)}, u32[]{:S(2)}) collective-permute-start(f32[3,2048]{1,0:T(4,128)S(1)} %get-tuple-element.24), channel_id=1, source_target_pairs={{0,16},{16,32},{32,48},{48,64},{64,80},{80,96},{96,112},{112,128},... | collective-permute-start | bytes 73736 | tf_op jit(solution)/shard_map/ppermute | solution.py:327
  139.9 12.3 %collective-permute-start.5 = (f32[3,2048]{1,0:T(4,128)S(1)}, f32[3,2048]{1,0:T(4,128)S(1)}, u32[]{:S(2)}, u32[]{:S(2)}) collective-permute-start(f32[3,2048]{1,0:T(4,128)S(1)} %get-tuple-element.25), channel_id=1, source_target_pairs={{16,0},{32,16},{48,32},{64,48},{80,64},{96,80},{112,96},{128,112},... | collective-permute-start | bytes 73736 | tf_op jit(solution)/shard_map/ppermute | solution.py:328
  146.1 1.7 %copy-start.3 = (f32[6,3,16,2048]{3,2,1,0:T(8,128)S(1)}, f32[6,3,16,2048]{3,2,1,0:T(8,128)}, u32[]{:S(2)}) copy-start(f32[6,3,16,2048]{3,2,1,0:T(8,128)} %copy-done.2) | copy-start | bytes 7077892

commit v3 on v2

--- a/solution.py
+++ b/solution.py
@@ -27,6 +27,14 @@
 
 def shape(*dims):
     return jax.ShapeDtypeStruct(dims, F32)
+
+
+def hbm(*dims):
+    return pltpu.HBM(dims, F32)
+
+
+def from_hbm(*arrays):
+    return [pltpu.with_memory_space_constraint(array, pltpu.HBM) for array in arrays]
 
 
 def params(mib=16):
@@ -98,7 +106,7 @@
         ],
         compiler_params=params(60),
         name="first_sums",
-    )(first, noise, ids, solute)
+    )(first, *from_hbm(noise, ids, solute))
 
 
 def factors(sums_ref, solute_ref, base_ref, slope_ref):
@@ -130,7 +138,7 @@
 
 
 def first_step(
-    first_ref, group_ref, mobility_ref, noise_ref, ids_ref, solute_ref, sums_ref, above_ref, below_ref,
+    first_ref, group_ref, mobility_ref, noise_ref, ids_ref, solute_ref, sums_ref, bulk_ref, above_ref, below_ref,
     eta_ref, next_sums_ref, next_ref, prev_ref, base_ref, slope_ref,
 ):
     grain = pl.program_id(0)
@@ -139,13 +147,8 @@
     def _():
         factors(sums_ref, solute_ref, base_ref, slope_ref)
         for plane in range(PLANES):
-            row = GRAINS * PLANES + 2 * plane
             for block in range(BLOCKS):
-                columns = column_block(block)
-                two, four = sums_ref[block, plane], sums_ref[block, PLANES + plane]
-                bulk = solute_beta * (two * two - four)
-                prev_ref[row : row + 2, columns] = bulk[:2]
-                next_ref[row : row + 2, columns] = bulk[ROWS - 2 :]
+                next_sums_ref[block, 2 * PLANES + plane] = bulk_ref[plane]
 
     rate = time_step * mobility_ref[group_ref[grain]]
     planes = [
@@ -176,23 +179,76 @@
                 next_sums_ref[block, PLANES + plane] += fourth[:, column_block(block)]
 
 
-def call_first_step(first, groups, mobility, noise, ids, solute, sums, above, below):
-    edge = GRAINS * PLANES + 2 * PLANES
+def call_first_step(first, groups, mobility, noise, ids, solute, sums, bulk, above, below):
+    edge = GRAINS * PLANES
     grain_block = pl.BlockSpec((1, PLANES, ROWS, COLS), lambda i: (i, 0, 0, 0))
+    parts = (BLOCKS, 3 * PLANES, ROWS, LANES)
     return pl.pallas_call(
         first_step,
         grid=(GRAINS,),
         in_specs=[
             smem(), smem(), smem(), grain_block,
-            whole(*ids.shape), whole(*solute.shape), whole(*sums.shape),
+            whole(*ids.shape), whole(*solute.shape), whole(*sums.shape), whole(*bulk.shape),
             whole(*above.shape), whole(*below.shape),
         ],
-        out_specs=[grain_block, whole(*sums.shape), whole(edge, COLS), whole(edge, COLS)],
-        out_shape=[shape(*noise.shape), shape(*sums.shape), shape(edge, COLS), shape(edge, COLS)],
+        out_specs=[grain_block, whole(*parts), whole(edge, COLS), whole(edge, COLS)],
+        out_shape=[hbm(*noise.shape), shape(*parts), hbm(edge, COLS), hbm(edge, COLS)],
         scratch_shapes=[pltpu.VMEM(solute.shape, F32)] * 2,
         compiler_params=params(),
         name="first_step",
-    )(first, groups, mobility, noise, ids, solute, sums, above, below)
+    )(first, groups, mobility, *from_hbm(noise, ids, solute), sums, *from_hbm(bulk, above, below))
+
+
+def added(parts_ref, row):
+    values = [parts_ref[part, row] for part in range(parts_ref.shape[0])]
+    while len(values) > 1:
+        values = [left + right for left, right in zip(values[::2], values[1::2])]
+    return values[0]
+
+
+def first_owner(parts_ref, copies_ref, bulk_ref):
+    for plane in range(PLANES):
+        two, four = added(parts_ref, plane), added(parts_ref, PLANES + plane)
+        bulk_ref[plane] = solute_beta * (two * two - four)
+        for copy in range(copies_ref.shape[0]):
+            copies_ref[copy, plane] = two
+
+
+def call_first_owner(parts):
+    return pl.pallas_call(
+        first_owner,
+        out_shape=[hbm(BLOCKS, PLANES, ROWS, LANES), hbm(PLANES, ROWS, LANES)],
+        compiler_params=params(),
+        name="first_owner",
+    )(parts)
+
+
+def second_owner(parts_ref, eta_next_ref, eta_prev_ref, copies_ref, next_ref, prev_ref):
+    for plane in range(PLANES):
+        two, four = added(parts_ref, plane), added(parts_ref, PLANES + plane)
+        bulk = solute_beta * (two * two - four)
+        for copy in range(copies_ref.shape[0]):
+            copies_ref[copy, plane] = two
+            copies_ref[copy, PLANES + plane] = bulk
+    edge = eta_next_ref.shape[0]
+    next_ref[:edge] = eta_next_ref[...]
+    prev_ref[:edge] = eta_prev_ref[...]
+    for plane in range(PLANES):
+        row = edge + 2 * plane
+        for block in range(BLOCKS):
+            columns = column_block(block)
+            prev_ref[row : row + 2, columns] = parts_ref[block, 2 * PLANES + plane, :2]
+            next_ref[row : row + 2, columns] = parts_ref[block, 2 * PLANES + plane, ROWS - 2 :]
+
+
+def call_second_owner(parts, eta_next, eta_prev):
+    edge = eta_next.shape[0] + 2 * PLANES
+    return pl.pallas_call(
+        second_owner,
+        out_shape=[hbm(BLOCKS, 2 * PLANES, ROWS, LANES), hbm(edge, COLS), hbm(edge, COLS)],
+        compiler_params=params(),
+        name="second_owner",
+    )(parts, *from_hbm(eta_next, eta_prev))
 
 
 PAD = 8
@@ -208,7 +264,7 @@
 
 
 def solute_step(
-    solute_ref, sums_ref, above_ref, below_ref, mid_above_ref, mid_below_ref,
+    solute_ref, parts_ref, above_ref, below_ref, mid_above_ref, mid_below_ref,
     out_ref, part_ref, deep_ref, bulk_ref,
 ):
     for plane in range(PLANES):
@@ -223,8 +279,7 @@
         bulk_ref[plane, PAD - 2 : PAD] = mid_above_ref[row : row + 2, :]
         bulk_ref[plane, PAD + ROWS : PAD + ROWS + 2] = mid_below_ref[row : row + 2, :]
         for block in range(BLOCKS):
-            two, four = sums_ref[block, plane], sums_ref[block, PLANES + plane]
-            bulk_ref[plane, PAD : PAD + ROWS, column_block(block)] = solute_beta * (two * two - four)
+            bulk_ref[plane, PAD : PAD + ROWS, column_block(block)] = parts_ref[block, 2 * PLANES + plane]
     solute = [deep_ref[plane] for plane in range(PLANES)]
     potential = [
         2.0 * bulk_stiff * (solute[plane] - solute_mean) - bulk_ref[plane] - solute_kappa * lap
@@ -239,22 +294,21 @@
         part_ref[plane] = part[PAD : PAD + ROWS]
 
 
-def call_solute_step(solute, sums, above, below, mid_above, mid_below):
+def call_solute_step(solute, parts, above, below, mid_above, mid_below):
     return pl.pallas_call(
         solute_step,
-        out_shape=[shape(*solute.shape)] * 2,
+        out_shape=[hbm(*solute.shape)] * 2,
         scratch_shapes=[pltpu.VMEM((PLANES, DEEP, COLS), F32)] * 2,
         compiler_params=params(),
         name="solute_step",
-    )(solute, sums, above, below, mid_above, mid_below)
+    )(*from_hbm(solute), parts, *from_hbm(above, below, mid_above, mid_below))
 
 
 def second_potential(part_ref, sums_ref, out_ref, next_ref, prev_ref):
     for plane in range(PLANES):
         for block in range(BLOCKS):
             columns = column_block(block)
-            two, four = sums_ref[block, plane], sums_ref[block, PLANES + plane]
-            potential = part_ref[plane, :, columns] - solute_beta * (two * two - four)
+            potential = part_ref[plane, :, columns] - sums_ref[block, PLANES + plane]
             out_ref[plane, :, columns] = potential
             prev_ref[plane : plane + 1, columns] = potential[:1]
             next_ref[plane : plane + 1, columns] = potential[ROWS - 1 :]
@@ -266,7 +320,7 @@
         out_shape=[shape(*part.shape), shape(PLANES, COLS), shape(PLANES, COLS)],
         compiler_params=params(),
         name="second_potential",
-    )(part, sums)
+    )(*from_hbm(part), sums)
 
 
 def second_step(
@@ -300,7 +354,7 @@
         compiler_params=params(),
         cost_estimate=pl.CostEstimate(flops=20_000_000, bytes_accessed=10_000_000, transcendentals=0),
         name="second_step",
-    )(groups, mobility, eta, solute, sums, above, below)
+    )(groups, mobility, *from_hbm(eta, solute), sums, *from_hbm(above, below))
 
 
 def solute_end(solute_ref, potential_ref, above_ref, below_ref, out_ref):
@@ -320,7 +374,7 @@
         out_shape=shape(*solute.shape),
         compiler_params=params(),
         name="solute_end",
-    )(solute, potential, above, below)
+    )(*from_hbm(solute), potential, above, below)
 
 
 def exchange(to_next, to_prev, count):
@@ -329,17 +383,8 @@
     return above, below
 
 
-def spread(value, axis):
-    copies = jnp.broadcast_to(value[None], (lax.axis_size(axis),) + value.shape)
-    return lax.all_to_all(copies, axis, 0, 0, tiled=True)
-
-
-def total(sums):
-    along = lax.axis_size("x")
-    parts = sums.reshape((along, BLOCKS // along) + sums.shape[1:])
-    parts = jnp.sum(lax.all_to_all(parts, "x", 0, 0, tiled=True), 0)
-    parts = jnp.sum(spread(parts, "yh"), 0)
-    return spread(parts, "x").reshape(sums.shape)
+def dealt(blocks):
+    return lax.all_to_all(blocks, GRAIN, 0, 0, tiled=True)
 
 
 def shards(grain_ids, group_of, group_mobility, seed_noise, concentration):
@@ -347,16 +392,18 @@
     first = (lax.axis_index(GRAIN) * GRAINS).astype(jnp.int32).reshape(1)
     sums, to_next, to_prev = call_first_sums(first, seed_noise, grain_ids, concentration)
     above, below = exchange(to_next, to_prev, count)
-    sums = total(sums)
-    eta, next_sums, to_next, to_prev = call_first_step(
-        first, group_of, group_mobility, seed_noise, grain_ids, concentration, sums, above, below
+    copies, bulk = call_first_owner(dealt(sums))
+    eta, parts, eta_next, eta_prev = call_first_step(
+        first, group_of, group_mobility, seed_noise, grain_ids, concentration, dealt(copies), bulk, above, below
     )
+    parts = dealt(parts)
+    copies, to_next, to_prev = call_second_owner(parts, eta_next, eta_prev)
     mid_above, mid_below = exchange(to_next, to_prev, count)
-    next_sums = total(next_sums)
-    solute, part = call_solute_step(concentration, sums, above, below, mid_above, mid_below)
-    potential, to_next, to_prev = call_second_potential(part, next_sums)
+    sums = dealt(copies)
+    solute, part = call_solute_step(concentration, parts, above, below, mid_above, mid_below)
+    potential, to_next, to_prev = call_second_potential(part, sums)
     end_above, end_below = exchange(to_next, to_prev, count)
-    eta = call_second_step(group_of, group_mobility, eta, solute, next_sums, mid_above, mid_below)
+    eta = call_second_step(group_of, group_mobility, eta, solute, sums, mid_above, mid_below)
     solute = call_solute_end(solute, potential, end_above, end_below)
     return eta, solute
 

time: 154 us -> 158 us (1.026)
  the two profiles are of different devices: /device:TPU:8 before, /device:TPU:56 now
where the time goes in v3:
time: 158 us; the launch traced here: 157 us
  blocking collectives  57.6 us (36%)
  starting transfers between devices  47.7 us (30%)
  Pallas kernels  26.4 us (17%)
  waiting for transfers between devices  22 us (14%)
  local copies, waits for them, and re-layouts  2.15 us (1%)
    all_to_all x2, blocking collectives, dealt(): return lax.all_to_all(blocks, GRAIN, 0, 0, tiled=True)  57.6 us
    ppermute x3, starting transfers between devices, exchange(): lax.ppermute(to_prev, SPACE, [((i + 1) % count, i) for i in range(count)])  24.5 us
    ppermute x3, waiting for transfers between devices, exchange(): lax.ppermute(to_next, SPACE, [(i, (i + 1) % count) for i in range(count)])  22 us
    all_to_all x2, starting transfers between devices, dealt(): return lax.all_to_all(blocks, GRAIN, 0, 0, tiled=True)  17.5 us
    pallas_call x1, Pallas kernels, call_first_step(): pl.pallas_call(first_step, grid=(GRAINS,), in_specs=[smem(), smem(), smem...  6.78 us
    pallas_call x1, Pallas kernels, call_second_step(): pl.pallas_call(second_step, grid=(GRAINS,), in_specs=[smem(), smem(), gra...  6.07 us
    ppermute x3, starting transfers between devices, exchange(): lax.ppermute(to_next, SPACE, [(i, (i + 1) % count) for i in range(count)])  5.75 us
    pallas_call x1, Pallas kernels, call_first_sums(): pl.pallas_call(first_sums, grid=(COLS // width,), in_specs=[smem(), pl.Bl...  4 us
  transfers between devices with their start and end apart: 8, of which 2 were waited for; matrix products, arithmetic and copies ran while one was open for 0% of the time, Pallas kernels for 6%

profile of v3, /device:TPU:56, one launch (start us, length us, event | category | flops | bytes accessed | tf_op | source)
XLA Modules:
  0.0 156.6 jit_solution(14898668918584461578)
XLA Ops:
  0.6 4.0 %first_sums.1 = (f32[16,6,16,128]{3,2,1,0:T(8,128)}, f32[27,2048]{1,0:T(8,128)}, f32[27,2048]{1,0:T(8,128)}) custom-call(s32[1]{0:T(128)} %bitcast.first_ref, f32[6,3,16,2048]{3,2,1,0:T(8,128)} %noise_ref.3, s32[3,16,2048]{2,1,0:T(8,128)} %ids_ref.3, f32[3,16,2048]{2,1,0:T(8,128)} %solute_ref.5), custom_call_target="tpu_custom_call" | custom-call | tf_op jit(solution)/shard_map/first_sums/pallas_call | solution.py:88
  4.6 0.0 copy-start.7
  4.6 0.0 copy-start.6
  4.6 0.0 copy-start
  4.7 0.0 copy-start.1
  4.7 26.1 %all_to_all.20.parts_ref = f32[16,6,16,128]{3,2,1,0:T(8,128)S(1)} all-to-all(f32[16,6,16,128]{3,2,1,0:T(8,128)} %get-tuple-element.19), channel_id=1, replica_groups=mesh['yl'=2,'z'=8,'core'=2,'x'=4,'yh'=4] {'x','yh'}, dimensions={0} | all-to-all | bytes 1572864 | tf_op jit(solution)/shard_map/all_to_all | solution.py:387
  30.8 0.8 first_owner.1
  31.5 10.8 %all-to-all-start.1 = ((f32[16,3,16,128]{3,2,1,0:T(8,128)}), f32[16,3,16,128]{3,2,1,0:T(8,128)S(1)}, u32[]{:S(2)}, u32[]{:S(2)}) async-start(f32[16,3,16,128]{3,2,1,0:T(8,128)} %get-tuple-element.20), calls=%async_computation.1 | async-start | bytes 786432 | tf_op jit(solution)/shard_map/all_to_all | solution.py:387
  42.4 0.0 copy-done.7
  42.4 1.9 %collective-permute-start = (f32[27,2048]{1,0:T(8,128)S(1)}, f32[27,2048]{1,0:T(8,128)S(1)}, u32[]{:S(2)}, u32[]{:S(2)}) collective-permute-start(f32[27,2048]{1,0:T(8,128)S(1)} %copy-done.7), channel_id=1, source_target_pairs={{0,16},{16,32},{32,48},{48,64},{64,80},{80,96},{96,112},{112,128},... | collective-permute-start | bytes 663560 | tf_op jit(solution)/shard_map/ppermute | solution.py:381
  44.3 0.0 copy-done.6
  44.3 10.8 %collective-permute-start.1 = (f32[27,2048]{1,0:T(8,128)S(1)}, f32[27,2048]{1,0:T(8,128)S(1)}, u32[]{:S(2)}, u32[]{:S(2)}) collective-permute-start(f32[27,2048]{1,0:T(8,128)S(1)} %copy-done.6), channel_id=1, source_target_pairs={{16,0},{32,16},{48,32},{64,48},{80,64},{96,80},{112,96},{128,112},... | collective-permute-start | bytes 663560 | tf_op jit(solution)/shard_map/ppermute | solution.py:382
  55.1 7.7 %collective-permute-done.above_ref = f32[27,2048]{1,0:T(8,128)S(1)} collective-permute-done((f32[27,2048]{1,0:T(8,128)S(1)}, f32[27,2048]{1,0:T(8,128)S(1)}, u32[]{:S(2)}, u32[]{:S(2)}) %collective-permute-start) | collective-permute-done | bytes 221216 | tf_op jit(solution)/shard_map/ppermute | solution.py:381
  62.8 0.0 copy-start.2
  62.8 0.0 collective-permute-done.1.below_ref
  62.8 0.0 copy-start.3
  62.8 0.0 all-to-all-done.1.sums_ref
  62.8 0.7 copy-done.2
  63.5 0.1 copy-done.3
  63.6 0.0 copy-done
  63.6 0.0 copy-done.1
  63.6 6.8 %first_step.1 = (f32[6,3,16,2048]{3,2,1,0:T(8,128)}, f32[16,9,16,128]{3,2,1,0:T(8,128)S(1)}, f32[18,2048]{1,0:T(8,128)}, f32[18,2048]{1,0:T(8,128)}) custom-call(s32[1]{0:T(128)} %bitcast.first_ref, s32[6]{0:T(128)S(1)} %copy-done, f32[4]{0:T(128)S(1)} %copy-done.1, f32[6,3,16,2048]{3,2,1,0:T(8,128)} %noise_ref.3, s32[3,16,2048]{2,1,0:T(8,128)} %ids_ref.3, ...), custom_call_target="tpu_custom_call" | custom-call | tf_op jit(solution)/shard_map/first_step/pallas_call | solution.py:186
  70.4 31.5 %all_to_all.21.parts_ref = f32[16,9,16,128]{3,2,1,0:T(8,128)S(1)} all-to-all(f32[16,9,16,128]{3,2,1,0:T(8,128)S(1)} %get-tuple-element.25), channel_id=1, replica_groups=mesh['yl'=2,'z'=8,'core'=2,'x'=4,'yh'=4] {'x','yh'}, dimensions={0} | all-to-all | bytes 2359296 | tf_op jit(solution)/shard_map/all_to_all | solution.py:387
  101.9 2.1 %second_owner.1 = (f32[16,6,16,128]{3,2,1,0:T(8,128)}, f32[24,2048]{1,0:T(8,128)}, f32[24,2048]{1,0:T(8,128)}) custom-call(f32[16,9,16,128]{3,2,1,0:T(8,128)S(1)} %all_to_all.21.parts_ref, f32[18,2048]{1,0:T(8,128)} %get-tuple-element.26.eta_next_ref, f32[18,2048]{1,0:T(8,128)} %get-tuple-element.27.eta_prev_ref), custom_call_target="tpu_custom_call" | custom-call | tf_op jit(solution)/shard_map/second_owner/pallas_call | solution.py:246
  104.0 6.7 %all-to-all-start.3 = ((f32[16,6,16,128]{3,2,1,0:T(8,128)}), f32[16,6,16,128]{3,2,1,0:T(8,128)S(1)}, u32[]{:S(2)}, u32[]{:S(2)}) async-start(f32[16,6,16,128]{3,2,1,0:T(8,128)} %get-tuple-element.31), calls=%async_computation.3 | async-start | bytes 1572864 | tf_op jit(solution)/shard_map/all_to_all | solution.py:387
  110.7 1.9 %collective-permute-start.2 = (f32[24,2048]{1,0:T(8,128)}, f32[24,2048]{1,0:T(8,128)S(1)}, u32[]{:S(2)}, u32[]{:S(2)}) collective-permute-start(f32[24,2048]{1,0:T(8,128)} %get-tuple-element.28), channel_id=1, source_target_pairs={{0,16},{16,32},{32,48},{48,64},{64,80},{80,96},{96,112},{112,128},... | collective-permute-start | bytes 589832 | tf_op jit(solution)/shard_map/ppermute | solution.py:381
  112.6 8.0 %collective-permute-start.3 = (f32[24,2048]{1,0:T(8,128)}, f32[24,2048]{1,0:T(8,128)S(1)}, u32[]{:S(2)}, u32[]{:S(2)}) collective-permute-start(f32[24,2048]{1,0:T(8,128)} %get-tuple-element.29), channel_id=1, source_target_pairs={{16,0},{32,16},{48,32},{64,48},{80,64},{96,80},{112,96},{128,112},... | collective-permute-start | bytes 589832 | tf_op jit(solution)/shard_map/ppermute | solution.py:382
  120.6 14.3 %collective-permute-done.2.mid_above_ref.above_ref = f32[24,2048]{1,0:T(8,128)S(1)} collective-permute-done((f32[24,2048]{1,0:T(8,128)}, f32[24,2048]{1,0:T(8,128)S(1)}, u32[]{:S(2)}, u32[]{:S(2)}) %collective-permute-start.2) | collective-permute-done | bytes 196640 | tf_op jit(solution)/shard_map/ppermute | solution.py:381
  134.9 0.0 copy-start.4
  134.9 0.0 collective-permute-done.3.mid_below_ref.below_ref
  134.9 0.7 copy-done.4
  135.6 0.0 copy-start.5
  135.6 0.7 copy-done.5
  136.2 3.5 %solute_step.1 = (f32[3,16,2048]{2,1,0:T(8,128)}, f32[3,16,2048]{2,1,0:T(8,128)}) custom-call(f32[3,16,2048]{2,1,0:T(8,128)} %solute_ref.5, f32[16,9,16,128]{3,2,1,0:T(8,128)S(1)} %all_to_all.21.parts_ref, f32[27,2048]{1,0:T(8,128)} %copy-done.2, f32[27,2048]{1,0:T(8,128)} %copy-done.3, f32[24,2048]{1,0:T(8,128)} %copy-done.4, f32[24,2048]{1,0:T(8,128)} %copy-done.5), custom_call_target="tpu_custom_call" | custom-call | tf_op jit(solution)/shard_map/solute_step/pallas_call | solution.py:298
  139.7 0.0 all-to-all-done.3.sums_ref
  139.7 1.1 second_potential.1
  140.8 1.9 %collective-permute-start.4 = (f32[3,2048]{1,0:T(4,128)S(1)}, f32[3,2048]{1,0:T(4,128)S(1)}, u32[]{:S(2)}, u32[]{:S(2)}) collective-permute-start(f32[3,2048]{1,0:T(4,128)S(1)} %get-tuple-element.34), channel_id=1, source_target_pairs={{0,16},{16,32},{32,48},{48,64},{64,80},{80,96},{96,112},{112,128},... | collective-permute-start | bytes 73736 | tf_op jit(solution)/shard_map/ppermute | solution.py:381
  142.7 5.8 %collective-permute-start.5 = (f32[3,2048]{1,0:T(4,128)S(1)}, f32[3,2048]{1,0:T(4,128)S(1)}, u32[]{:S(2)}, u32[]{:S(2)}) collective-permute-start(f32[3,2048]{1,0:T(4,128)S(1)} %get-tuple-element.35), channel_id=1, source_target_pairs={{16,0},{32,16},{48,32},{64,48},{80,64},{96,80},{112,96},{128,112},... | collective-permute-start | bytes 73736 | tf_op jit(solution)/shard_map/ppermute | solution.py:382
  148.5 6.1 %second_step.1 = f32[6,3,16,2048]{3,2,1,0:T(8,128)} custom-call(s32[6]{0:T(128)S(1)} %copy-done, f32[4]{0:T(128)S(1)} %copy-done.1, f32[6,3,16,2048]{3,2,1,0:T(8,128)} %get-tuple-element.24.old_ref, f32[3,16,2048]{2,1,0:T(8,128)} %get-tuple-element.30.solute_ref, f32[16,6,16,128]{3,2,1,0:T(8,128)S(1)} %all-to-all-done.3.sums_ref, f32[24,2048]{1,0:T(8,128)} %copy-done.4, ...), custom_call_target="tpu_custom_call" | custom-call | flops 20000000 | bytes 10000000 | tf_op jit(solution)/shard_map/second_step/pallas_call | solution.py:344
  154.5 0.0 collective-permute-done.4.above_ref
  154.5 0.0 collective-permute-done.5.below_ref
  154.5 2.0 %solute_end.1 = f32[3,16,2048]{2,1,0:T(8,128)} custom-call(f32[3,16,2048]{2,1,0:T(8,128)} %get-tuple-element.30.solute_ref, f32[3,16,2048]{2,1,0:T(8,128)S(1)} %get-tuple-element.33.potential_ref, f32[3,2048]{1,0:T(4,128)S(1)} %collective-permute-done.4.above_ref, f32[3,2048]{1,0:T(4,128)S(1)} %collective-permute-done.5.below_ref), custom_call_target="tpu_custom_call" | custom-call | tf_op jit(solution)/shard_map/solute_end/pallas_call | solution.py:372
Async XLA Ops:
  4.6 37.7 %copy-start.7 = (f32[27,2048]{1,0:T(8,128)S(1)}, f32[27,2048]{1,0:T(8,128)}, u32[]{:S(2)}) copy-start(f32[27,2048]{1,0:T(8,128)} %get-tuple-element.22) | copy-start | bytes 663556
  4.6 39.6 %copy-start.6 = (f32[27,2048]{1,0:T(8,128)S(1)}, f32[27,2048]{1,0:T(8,128)}, u32[]{:S(2)}) copy-start(f32[27,2048]{1,0:T(8,128)} %get-tuple-element.23) | copy-start | bytes 663556
  4.6 58.9 %copy-start = (s32[6]{0:T(128)S(1)}, s32[6]{0:T(128)}, u32[]{:S(2)}) copy-start(s32[6]{0:T(128)} %group_ref.3) | copy-start | bytes 76
  4.7 58.9 %copy-start.1 = (f32[4]{0:T(128)S(1)}, f32[4]{0:T(128)}, u32[]{:S(2)}) copy-start(f32[4]{0:T(128)} %mobility_ref.3) | copy-start | bytes 52
  31.5 31.2 %all-to-all-start.1 = ((f32[16,3,16,128]{3,2,1,0:T(8,128)}), f32[16,3,16,128]{3,2,1,0:T(8,128)S(1)}, u32[]{:S(2)}, u32[]{:S(2)}) async-start(f32[16,3,16,128]{3,2,1,0:T(8,128)} %get-tuple-element.20), calls=%async_computation.1 | async-start | bytes 786432 | tf_op jit(solution)/shard_map/all_to_all | solution.py:387
  42.4 20.4 %collective-permute-start = (f32[27,2048]{1,0:T(8,128)S(1)}, f32[27,2048]{1,0:T(8,128)S(1)}, u32[]{:S(2)}, u32[]{:S(2)}) collective-permute-start(f32[27,2048]{1,0:T(8,128)S(1)} %copy-done.7), channel_id=1, source_target_pairs={{0,16},{16,32},{32,48},{48,64},{64,80},{80,96},{96,112},{112,128},... | collective-permute-start | bytes 663560 | tf_op jit(solution)/shard_map/ppermute | solution.py:381
  44.3 18.5 %collective-permute-start.1 = (f32[27,2048]{1,0:T(8,128)S(1)}, f32[27,2048]{1,0:T(8,128)S(1)}, u32[]{:S(2)}, u32[]{:S(2)}) collective-permute-start(f32[27,2048]{1,0:T(8,128)S(1)} %copy-done.6), channel_id=1, source_target_pairs={{16,0},{32,16},{48,32},{64,48},{80,64},{96,80},{112,96},{128,112},... | collective-permute-start | bytes 663560 | tf_op jit(solution)/shard_map/ppermute | solution.py:382
  62.8 0.7 copy-start.2
  62.8 0.8 copy-start.3
  104.0 35.7 %all-to-all-start.3 = ((f32[16,6,16,128]{3,2,1,0:T(8,128)}), f32[16,6,16,128]{3,2,1,0:T(8,128)S(1)}, u32[]{:S(2)}, u32[]{:S(2)}) async-start(f32[16,6,16,128]{3,2,1,0:T(8,128)} %get-tuple-element.31), calls=%async_computation.3 | async-start | bytes 1572864 | tf_op jit(solution)/shard_map/all_to_all | solution.py:387
  110.7 24.2 %collective-permute-start.2 = (f32[24,2048]{1,0:T(8,128)}, f32[24,2048]{1,0:T(8,128)S(1)}, u32[]{:S(2)}, u32[]{:S(2)}) collective-permute-start(f32[24,2048]{1,0:T(8,128)} %get-tuple-element.28), channel_id=1, source_target_pairs={{0,16},{16,32},{32,48},{48,64},{64,80},{80,96},{96,112},{112,128},... | collective-permute-start | bytes 589832 | tf_op jit(solution)/shard_map/ppermute | solution.py:381
  112.6 22.3 %collective-permute-start.3 = (f32[24,2048]{1,0:T(8,128)}, f32[24,2048]{1,0:T(8,128)S(1)}, u32[]{:S(2)}, u32[]{:S(2)}) collective-permute-start(f32[24,2048]{1,0:T(8,128)} %get-tuple-element.29), channel_id=1, source_target_pairs={{16,0},{32,16},{48,32},{64,48},{80,64},{96,80},{112,96},{128,112},... | collective-permute-start | bytes 589832 | tf_op jit(solution)/shard_map/ppermute | solution.py:382
  134.9 0.7 copy-start.4
  135.6 0.7 copy-start.5
  140.8 13.8 %collective-permute-start.4 = (f32[3,2048]{1,0:T(4,128)S(1)}, f32[3,2048]{1,0:T(4,128)S(1)}, u32[]{:S(2)}, u32[]{:S(2)}) collective-permute-start(f32[3,2048]{1,0:T(4,128)S(1)} %get-tuple-element.34), channel_id=1, source_target_pairs={{0,16},{16,32},{32,48},{48,64},{64,80},{80,96},{96,112},{112,128},... | collective-permute-start | bytes 73736 | tf_op jit(solution)/shard_map/ppermute | solution.py:381
  142.7 11.8 %collective-permute-start.5 = (f32[3,2048]{1,0:T(4,128)S(1)}, f32[3,2048]{1,0:T(4,128)S(1)}, u32[]{:S(2)}, u32[]{:S(2)}) collective-permute-start(f32[3,2048]{1,0:T(4,128)S(1)} %get-tuple-element.35), channel_id=1, source_target_pairs={{16,0},{32,16},{48,32},{64,48},{80,64},{96,80},{112,96},{128,112},... | collective-permute-start | bytes 73736 | tf_op jit(solution)/shard_map/ppermute | solution.py:382

commit v4 on v2

--- a/solution.py
+++ b/solution.py
@@ -27,6 +27,10 @@
 
 def shape(*dims):
     return jax.ShapeDtypeStruct(dims, F32)
+
+
+def hbm(*dims):
+    return pltpu.HBM(dims, F32)
 
 
 def params(mib=16):
@@ -131,7 +135,7 @@
 
 def first_step(
     first_ref, group_ref, mobility_ref, noise_ref, ids_ref, solute_ref, sums_ref, above_ref, below_ref,
-    eta_ref, next_sums_ref, next_ref, prev_ref, base_ref, slope_ref,
+    eta_ref, next_sums_ref, next_ref, prev_ref, bulk_ref, rows_above_ref, rows_below_ref, base_ref, slope_ref,
 ):
     grain = pl.program_id(0)
 
@@ -142,10 +146,12 @@
             row = GRAINS * PLANES + 2 * plane
             for block in range(BLOCKS):
                 columns = column_block(block)
-                two, four = sums_ref[block, plane], sums_ref[block, PLANES + plane]
-                bulk = solute_beta * (two * two - four)
+                bulk = sums_ref[block, PLANES + plane]
+                bulk_ref[plane, :, columns] = bulk
                 prev_ref[row : row + 2, columns] = bulk[:2]
                 next_ref[row : row + 2, columns] = bulk[ROWS - 2 :]
+        rows_above_ref[...] = above_ref[GRAINS * PLANES :]
+        rows_below_ref[...] = below_ref[GRAINS * PLANES :]
 
     rate = time_step * mobility_ref[group_ref[grain]]
     planes = [
@@ -187,8 +193,14 @@
             whole(*ids.shape), whole(*solute.shape), whole(*sums.shape),
             whole(*above.shape), whole(*below.shape),
         ],
-        out_specs=[grain_block, whole(*sums.shape), whole(edge, COLS), whole(edge, COLS)],
-        out_shape=[shape(*noise.shape), shape(*sums.shape), shape(edge, COLS), shape(edge, COLS)],
+        out_specs=[grain_block, whole(*sums.shape)]
+        + [whole(edge, COLS)] * 2
+        + [whole(*solute.shape)]
+        + [whole(3 * PLANES, COLS)] * 2,
+        out_shape=[hbm(*noise.shape), shape(*sums.shape)]
+        + [shape(edge, COLS)] * 2
+        + [hbm(*solute.shape)]
+        + [hbm(3 * PLANES, COLS)] * 2,
         scratch_shapes=[pltpu.VMEM(solute.shape, F32)] * 2,
         compiler_params=params(),
         name="first_step",
@@ -208,23 +220,21 @@
 
 
 def solute_step(
-    solute_ref, sums_ref, above_ref, below_ref, mid_above_ref, mid_below_ref,
+    solute_ref, middle_ref, above_ref, below_ref, mid_above_ref, mid_below_ref,
     out_ref, part_ref, deep_ref, bulk_ref,
 ):
     for plane in range(PLANES):
         for ref in (deep_ref, bulk_ref):
             ref[plane, :PAD] = jnp.zeros((PAD, COLS), F32)
             ref[plane, PAD + ROWS :] = jnp.zeros((PAD, COLS), F32)
-        row = GRAINS * PLANES + 3 * plane
+        row = 3 * plane
         deep_ref[plane, PAD - 3 : PAD] = above_ref[row : row + 3, :]
         deep_ref[plane, PAD : PAD + ROWS] = solute_ref[plane]
         deep_ref[plane, PAD + ROWS : PAD + ROWS + 3] = below_ref[row : row + 3, :]
         row = GRAINS * PLANES + 2 * plane
         bulk_ref[plane, PAD - 2 : PAD] = mid_above_ref[row : row + 2, :]
         bulk_ref[plane, PAD + ROWS : PAD + ROWS + 2] = mid_below_ref[row : row + 2, :]
-        for block in range(BLOCKS):
-            two, four = sums_ref[block, plane], sums_ref[block, PLANES + plane]
-            bulk_ref[plane, PAD : PAD + ROWS, column_block(block)] = solute_beta * (two * two - four)
+        bulk_ref[plane, PAD : PAD + ROWS] = middle_ref[plane]
     solute = [deep_ref[plane] for plane in range(PLANES)]
     potential = [
         2.0 * bulk_stiff * (solute[plane] - solute_mean) - bulk_ref[plane] - solute_kappa * lap
@@ -239,22 +249,21 @@
         part_ref[plane] = part[PAD : PAD + ROWS]
 
 
-def call_solute_step(solute, sums, above, below, mid_above, mid_below):
+def call_solute_step(solute, bulk, above, below, mid_above, mid_below):
     return pl.pallas_call(
         solute_step,
         out_shape=[shape(*solute.shape)] * 2,
         scratch_shapes=[pltpu.VMEM((PLANES, DEEP, COLS), F32)] * 2,
         compiler_params=params(),
         name="solute_step",
-    )(solute, sums, above, below, mid_above, mid_below)
+    )(solute, bulk, above, below, mid_above, mid_below)
 
 
 def second_potential(part_ref, sums_ref, out_ref, next_ref, prev_ref):
     for plane in range(PLANES):
         for block in range(BLOCKS):
             columns = column_block(block)
-            two, four = sums_ref[block, plane], sums_ref[block, PLANES + plane]
-            potential = part_ref[plane, :, columns] - solute_beta * (two * two - four)
+            potential = part_ref[plane, :, columns] - sums_ref[block, PLANES + plane]
             out_ref[plane, :, columns] = potential
             prev_ref[plane : plane + 1, columns] = potential[:1]
             next_ref[plane : plane + 1, columns] = potential[ROWS - 1 :]
@@ -329,34 +338,78 @@
     return above, below
 
 
-def spread(value, axis):
-    copies = jnp.broadcast_to(value[None], (lax.axis_size(axis),) + value.shape)
-    return lax.all_to_all(copies, axis, 0, 0, tiled=True)
-
-
-def total(sums):
+def added(parts_ref, index):
+    values = [parts_ref[(part,) + index] for part in range(parts_ref.shape[0])]
+    while len(values) > 1:
+        values = [left + right for left, right in zip(values[::2], values[1::2])]
+    return values[0]
+
+
+def add_parts(parts_ref, out_ref):
+    for block in range(out_ref.shape[0]):
+        for row in range(out_ref.shape[1]):
+            out_ref[block, row] = added(parts_ref, (block, row))
+
+
+def call_add_parts(parts):
+    return pl.pallas_call(
+        add_parts, out_shape=shape(*parts.shape[1:]), compiler_params=params(), name="add_parts"
+    )(parts)
+
+
+def owner(parts_ref, copies_ref):
+    for plane in range(PLANES):
+        two, four = added(parts_ref, (plane,)), added(parts_ref, (PLANES + plane,))
+        bulk = solute_beta * (two * two - four)
+        for copy in range(copies_ref.shape[0]):
+            copies_ref[copy, plane] = two
+            copies_ref[copy, PLANES + plane] = bulk
+
+
+def call_owner(parts):
+    return pl.pallas_call(
+        owner, out_shape=shape(*parts.shape), compiler_params=params(), name="owner"
+    )(parts)
+
+
+def copies(value_ref, out_ref):
+    for copy in range(out_ref.shape[0]):
+        out_ref[copy] = value_ref[...]
+
+
+def call_copies(value, count):
+    return pl.pallas_call(
+        copies, out_shape=shape(count, *value.shape), compiler_params=params(), name="copies"
+    )(value)
+
+
+def dealt(blocks, axis):
+    return lax.all_to_all(blocks, axis, 0, 0, tiled=True)
+
+
+def total(sums, to_next, to_prev):
+    count = lax.axis_size("yl") * lax.axis_size("z") * lax.axis_size("core")
     along = lax.axis_size("x")
-    parts = sums.reshape((along, BLOCKS // along) + sums.shape[1:])
-    parts = jnp.sum(lax.all_to_all(parts, "x", 0, 0, tiled=True), 0)
-    parts = jnp.sum(spread(parts, "yh"), 0)
-    return spread(parts, "x").reshape(sums.shape)
+    parts = dealt(sums.reshape((along, BLOCKS // along) + sums.shape[1:]), "x")
+    parts, above, below = lax.optimization_barrier((parts, *exchange(to_next, to_prev, count)))
+    parts = dealt(call_add_parts(parts), "yh")
+    parts = dealt(call_owner(parts), "yh")
+    return dealt(call_copies(parts, along), "x").reshape(sums.shape), above, below
 
 
 def shards(grain_ids, group_of, group_mobility, seed_noise, concentration):
     count = lax.axis_size("yl") * lax.axis_size("z") * lax.axis_size("core")
     first = (lax.axis_index(GRAIN) * GRAINS).astype(jnp.int32).reshape(1)
     sums, to_next, to_prev = call_first_sums(first, seed_noise, grain_ids, concentration)
-    above, below = exchange(to_next, to_prev, count)
-    sums = total(sums)
-    eta, next_sums, to_next, to_prev = call_first_step(
+    sums, above, below = total(sums, to_next, to_prev)
+    eta, sums, to_next, to_prev, bulk, rows_above, rows_below = call_first_step(
         first, group_of, group_mobility, seed_noise, grain_ids, concentration, sums, above, below
     )
-    mid_above, mid_below = exchange(to_next, to_prev, count)
-    next_sums = total(next_sums)
-    solute, part = call_solute_step(concentration, sums, above, below, mid_above, mid_below)
-    potential, to_next, to_prev = call_second_potential(part, next_sums)
+    sums, mid_above, mid_below = total(sums, to_next, to_prev)
+    solute, part = call_solute_step(concentration, bulk, rows_above, rows_below, mid_above, mid_below)
+    potential, to_next, to_prev = call_second_potential(part, sums)
     end_above, end_below = exchange(to_next, to_prev, count)
-    eta = call_second_step(group_of, group_mobility, eta, solute, next_sums, mid_above, mid_below)
+    eta = call_second_step(group_of, group_mobility, eta, solute, sums, mid_above, mid_below)
     solute = call_solute_end(solute, potential, end_above, end_below)
     return eta, solute
 

time: 154 us -> 146 us (0.948)
  the two profiles are of different devices: /device:TPU:8 before, /device:TPU:1 now
where the time goes in v4:
time: 146 us; the launch traced here: 145 us
  blocking collectives  58.5 us (40%)
  starting transfers between devices  50.3 us (34%)
  Pallas kernels  17.3 us (12%)
  waiting for transfers between devices  15.1 us (10%)
  local copies, waits for them, and re-layouts  3.12 us (2%)
    all_to_all x5, blocking collectives, dealt(): return lax.all_to_all(blocks, axis, 0, 0, tiled=True)  58.5 us
    ppermute x3, starting transfers between devices, exchange(): lax.ppermute(to_next, SPACE, [(i, (i + 1) % count) for i in range(count)])  28.7 us
    all_to_all x3, starting transfers between devices, dealt(): return lax.all_to_all(blocks, axis, 0, 0, tiled=True)  12.8 us
    ppermute x3, starting transfers between devices, exchange(): lax.ppermute(to_prev, SPACE, [((i + 1) % count, i) for i in range(count)])  8.77 us
    ppermute x3, waiting for transfers between devices, exchange(): lax.ppermute(to_prev, SPACE, [((i + 1) % count, i) for i in range(count)])  7.79 us
    all_to_all x3, waiting for transfers between devices, dealt(): return lax.all_to_all(blocks, axis, 0, 0, tiled=True)  6.82 us
    pallas_call x1, Pallas kernels, call_first_step(): pl.pallas_call(first_step, grid=(GRAINS,), in_specs=[smem(), smem(), smem...  5.39 us
    pallas_call x1, Pallas kernels, call_second_step(): pl.pallas_call(second_step, grid=(GRAINS,), in_specs=[smem(), smem(), gra...  4.21 us
  transfers between devices with their start and end apart: 9, of which 4 were waited for; matrix products, arithmetic and copies ran while one was open for 0% of the time, Pallas kernels for 4%

profile of v4, /device:TPU:1, one launch (start us, length us, event | category | flops | bytes accessed | tf_op | source)
XLA Modules:
  0.0 145.3 jit_solution(8708927091721585099)
XLA Ops:
  0.6 4.0 %first_sums.1 = (f32[16,6,16,128]{3,2,1,0:T(8,128)}, f32[27,2048]{1,0:T(8,128)}, f32[27,2048]{1,0:T(8,128)}) custom-call(s32[1]{0:T(128)} %bitcast.first_ref, f32[6,3,16,2048]{3,2,1,0:T(8,128)} %noise_ref.3, s32[3,16,2048]{2,1,0:T(8,128)} %ids_ref.3, f32[3,16,2048]{2,1,0:T(8,128)} %solute_ref.5), custom_call_target="tpu_custom_call" | custom-call | tf_op jit(solution)/shard_map/first_sums/pallas_call | solution.py:84
  4.6 4.8 %all-to-all-start = ((f32[4,4,6,16,128]{4,3,2,1,0:T(8,128)}), f32[4,4,6,16,128]{4,3,2,1,0:T(8,128)S(1)}, u32[]{:S(2)}, u32[]{:S(2)}) async-start(f32[4,4,6,16,128]{4,3,2,1,0:T(8,128)} %bitcast.8), calls=%async_computation | async-start | bytes 1572864 | tf_op jit(solution)/shard_map/all_to_all | solution.py:387
  9.5 4.8 %collective-permute-start = (f32[27,2048]{1,0:T(8,128)}, f32[27,2048]{1,0:T(8,128)S(1)}, u32[]{:S(2)}, u32[]{:S(2)}) collective-permute-start(f32[27,2048]{1,0:T(8,128)} %get-tuple-element.24), channel_id=1, source_target_pairs={{0,16},{16,32},{32,48},{48,64},{64,80},{80,96},{96,112},{112,128},... | collective-permute-start | bytes 663560 | tf_op jit(solution)/shard_map/ppermute | solution.py:336
  14.3 0.0 copy-start
  14.3 0.0 copy-start.1
  14.3 0.0 copy-start.11
  14.4 0.0 copy-start.12
  14.4 4.8 %collective-permute-start.1 = (f32[27,2048]{1,0:T(8,128)}, f32[27,2048]{1,0:T(8,128)S(1)}, u32[]{:S(2)}, u32[]{:S(2)}) collective-permute-start(f32[27,2048]{1,0:T(8,128)} %get-tuple-element.25), channel_id=1, source_target_pairs={{16,0},{32,16},{48,32},{64,48},{80,64},{96,80},{112,96},{128,112},... | collective-permute-start | bytes 663560 | tf_op jit(solution)/shard_map/ppermute | solution.py:337
  19.2 0.0 collective-permute-done.above_ref
  19.2 0.0 copy-start.5
  19.2 0.7 copy-done.5
  19.9 2.9 %collective-permute-done.1.below_ref = f32[27,2048]{1,0:T(8,128)S(1)} collective-permute-done((f32[27,2048]{1,0:T(8,128)}, f32[27,2048]{1,0:T(8,128)S(1)}, u32[]{:S(2)}, u32[]{:S(2)}) %collective-permute-start.1) | collective-permute-done | bytes 221216 | tf_op jit(solution)/shard_map/ppermute | solution.py:337
  22.8 0.7 copy-done.7
  23.5 0.0 all-to-all-done.parts_ref
  23.6 14.7 %all_to_all.40.parts_ref = f32[4,6,16,128]{3,2,1,0:T(8,128)S(1)} all-to-all(f32[4,6,16,128]{3,2,1,0:T(8,128)S(1)} %add_parts.2), channel_id=1, replica_groups=mesh['yl'=2,'z'=8,'core'=2,'x'=4,'yh'=4] {'yh'}, dimensions={0} | all-to-all | bytes 393216 | tf_op jit(solution)/shard_map/all_to_all | solution.py:387
  38.3 10.4 %all_to_all.41.value_ref = f32[4,6,16,128]{3,2,1,0:T(8,128)S(1)} all-to-all(f32[4,6,16,128]{3,2,1,0:T(8,128)S(1)} %owner.2), channel_id=1, replica_groups=mesh['yl'=2,'z'=8,'core'=2,'x'=4,'yh'=4] {'yh'}, dimensions={0} | all-to-all | bytes 393216 | tf_op jit(solution)/shard_map/all_to_all | solution.py:387
  48.7 0.1 copies.2
  48.7 12.7 %all_to_all.42 = f32[4,4,6,16,128]{4,3,2,1,0:T(8,128)S(1)} all-to-all(f32[4,4,6,16,128]{4,3,2,1,0:T(8,128)S(1)} %copies.2), channel_id=1, replica_groups=mesh['yl'=2,'z'=8,'core'=2,'x'=4,'yh'=4] {'x'}, dimensions={0} | all-to-all | bytes 1572864 | tf_op jit(solution)/shard_map/all_to_all | solution.py:387
  61.4 0.0 copy-done
  61.4 0.0 copy-done.1
  61.4 0.0 copy-done.12
  61.4 0.0 copy-done.3
  61.4 0.0 copy-done.6
  61.5 0.0 copy-done.8
  61.5 5.4 %first_step.1 = (f32[6,3,16,2048]{3,2,1,0:T(8,128)}, f32[16,6,16,128]{3,2,1,0:T(8,128)}, f32[24,2048]{1,0:T(8,128)S(1)}, f32[24,2048]{1,0:T(8,128)S(1)}, f32[3,1...) custom-call(s32[1]{0:T(128)} %bitcast.first_ref, s32[6]{0:T(128)S(1)} %copy-done.11, f32[4]{0:T(128)S(1)} %copy-done.12, ...), custom_call_target="tpu_custom_call" | custom-call | tf_op jit(solution)/shard_map/first_step/pallas_call | solution.py:188
  66.9 3.5 %all-to-all-start.4 = ((f32[4,4,6,16,128]{4,3,2,1,0:T(8,128)}), f32[4,4,6,16,128]{4,3,2,1,0:T(8,128)S(1)}, u32[]{:S(2)}, u32[]{:S(2)}) async-start(f32[4,4,6,16,128]{4,3,2,1,0:T(8,128)} %bitcast.3), calls=%async_computation.4 | async-start | bytes 1572864 | tf_op jit(solution)/shard_map/all_to_all | solution.py:387
  70.4 11.6 %collective-permute-start.2 = (f32[24,2048]{1,0:T(8,128)S(1)}, f32[24,2048]{1,0:T(8,128)S(1)}, u32[]{:S(2)}, u32[]{:S(2)}) collective-permute-start(f32[24,2048]{1,0:T(8,128)S(1)} %get-tuple-element.34), channel_id=1, source_target_pairs={{0,16},{16,32},{32,48},{48,64},{64,80},{80,96},{96,112},{112,128},... | collective-permute-start | bytes 589832 | tf_op jit(solution)/shard_map/ppermute | solution.py:336
  82.0 0.0 copy-start.4
  82.0 2.1 %collective-permute-start.3 = (f32[24,2048]{1,0:T(8,128)S(1)}, f32[24,2048]{1,0:T(8,128)S(1)}, u32[]{:S(2)}, u32[]{:S(2)}) collective-permute-start(f32[24,2048]{1,0:T(8,128)S(1)} %get-tuple-element.35), channel_id=1, source_target_pairs={{16,0},{32,16},{48,32},{64,48},{80,64},{96,80},{112,96},{128,112},... | collective-permute-start | bytes 589832 | tf_op jit(solution)/shard_map/ppermute | solution.py:337
  84.1 0.5 collective-permute-done.2.mid_above_ref.above_ref
  84.6 4.9 %collective-permute-done.3.mid_below_ref.below_ref = f32[24,2048]{1,0:T(8,128)S(1)} collective-permute-done((f32[24,2048]{1,0:T(8,128)S(1)}, f32[24,2048]{1,0:T(8,128)S(1)}, u32[]{:S(2)}, u32[]{:S(2)}) %collective-permute-start.3) | collective-permute-done | bytes 196640 | tf_op jit(solution)/shard_map/ppermute | solution.py:337
  89.4 0.0 all-to-all-done.4.parts_ref
  89.5 10.5 %all_to_all.43.parts_ref = f32[4,6,16,128]{3,2,1,0:T(8,128)S(1)} all-to-all(f32[4,6,16,128]{3,2,1,0:T(8,128)S(1)} %add_parts.3), channel_id=1, replica_groups=mesh['yl'=2,'z'=8,'core'=2,'x'=4,'yh'=4] {'yh'}, dimensions={0} | all-to-all | bytes 393216 | tf_op jit(solution)/shard_map/all_to_all | solution.py:387
  100.0 10.3 %all_to_all.44.value_ref = f32[4,6,16,128]{3,2,1,0:T(8,128)S(1)} all-to-all(f32[4,6,16,128]{3,2,1,0:T(8,128)S(1)} %owner.3), channel_id=1, replica_groups=mesh['yl'=2,'z'=8,'core'=2,'x'=4,'yh'=4] {'yh'}, dimensions={0} | all-to-all | bytes 393216 | tf_op jit(solution)/shard_map/all_to_all | solution.py:387
  110.3 0.9 copies.3
  111.2 4.5 %all-to-all-start.7 = ((f32[4,4,6,16,128]{4,3,2,1,0:T(8,128)}), f32[4,4,6,16,128]{4,3,2,1,0:T(8,128)S(1)}, u32[]{:S(2)}, u32[]{:S(2)}) async-start(f32[4,4,6,16,128]{4,3,2,1,0:T(8,128)} %copies.3), calls=%async_computation.7 | async-start | bytes 1572864 | tf_op jit(solution)/shard_map/all_to_all | solution.py:387
  115.7 0.0 copy-done.9
  115.7 1.5 %solute_step.1 = (f32[3,16,2048]{2,1,0:T(8,128)S(1)}, f32[3,16,2048]{2,1,0:T(8,128)S(1)}) custom-call(f32[3,16,2048]{2,1,0:T(8,128)S(1)} %copy-done.1, f32[3,16,2048]{2,1,0:T(8,128)S(1)} %copy-done.4, f32[9,2048]{1,0:T(8,128)S(1)} %copy-done.9, f32[9,2048]{1,0:T(8,128)S(1)} %copy-done.10, f32[24,2048]{1,0:T(8,128)S(1)} %collective-permute-done.2.mid_above_ref.above_ref, ...), custom_call_target="tpu_custom_call" | custom-call | tf_op jit(solution)/shard_map/solute_step/pallas_call | solution.py:253
  117.2 6.8 %all-to-all-done.7 = f32[4,4,6,16,128]{4,3,2,1,0:T(8,128)S(1)} async-done(((f32[4,4,6,16,128]{4,3,2,1,0:T(8,128)}), f32[4,4,6,16,128]{4,3,2,1,0:T(8,128)S(1)}, u32[]{:S(2)}, u32[]{:S(2)}) %all-to-all-start.7) | async-done | bytes 786464 | tf_op jit(solution)/shard_map/all_to_all | solution.py:387
  124.0 0.1 second_potential.1
  124.1 12.3 %collective-permute-start.4 = (f32[3,2048]{1,0:T(4,128)S(1)}, f32[3,2048]{1,0:T(4,128)S(1)}, u32[]{:S(2)}, u32[]{:S(2)}) collective-permute-start(f32[3,2048]{1,0:T(4,128)S(1)} %get-tuple-element.42), channel_id=1, source_target_pairs={{0,16},{16,32},{32,48},{48,64},{64,80},{80,96},{96,112},{112,128},... | collective-permute-start | bytes 73736 | tf_op jit(solution)/shard_map/ppermute | solution.py:336
  136.4 1.9 %collective-permute-start.5 = (f32[3,2048]{1,0:T(4,128)S(1)}, f32[3,2048]{1,0:T(4,128)S(1)}, u32[]{:S(2)}, u32[]{:S(2)}) collective-permute-start(f32[3,2048]{1,0:T(4,128)S(1)} %get-tuple-element.43), channel_id=1, source_target_pairs={{16,0},{32,16},{48,32},{64,48},{80,64},{96,80},{112,96},{128,112},... | collective-permute-start | bytes 73736 | tf_op jit(solution)/shard_map/ppermute | solution.py:337
  138.3 0.0 copy-start.2
  138.3 1.7 %copy-done.2 = f32[6,3,16,2048]{3,2,1,0:T(8,128)S(1)} copy-done((f32[6,3,16,2048]{3,2,1,0:T(8,128)S(1)}, f32[6,3,16,2048]{3,2,1,0:T(8,128)}, u32[]{:S(2)}) %copy-start.2) | copy-done | bytes 2359320
  140.0 4.2 %second_step.1 = f32[6,3,16,2048]{3,2,1,0:T(8,128)} custom-call(s32[6]{0:T(128)S(1)} %copy-done.11, f32[4]{0:T(128)S(1)} %copy-done.12, f32[6,3,16,2048]{3,2,1,0:T(8,128)S(1)} %copy-done.2, f32[3,16,2048]{2,1,0:T(8,128)S(1)} %get-tuple-element.38.solute_ref, f32[16,6,16,128]{3,2,1,0:T(8,128)S(1)} %bitcast.6, ...), custom_call_target="tpu_custom_call" | custom-call | flops 20000000 | bytes 10000000 | tf_op jit(solution)/shard_map/second_step/pallas_call | solution.py:299
  144.2 0.0 collective-permute-done.4.above_ref
  144.2 0.0 collective-permute-done.5.below_ref
  144.2 1.1 solute_end.1
  (13 shorter events, 0.1 us)
Async XLA Ops:
  4.6 18.9 %all-to-all-start = ((f32[4,4,6,16,128]{4,3,2,1,0:T(8,128)}), f32[4,4,6,16,128]{4,3,2,1,0:T(8,128)S(1)}, u32[]{:S(2)}, u32[]{:S(2)}) async-start(f32[4,4,6,16,128]{4,3,2,1,0:T(8,128)} %bitcast.8), calls=%async_computation | async-start | bytes 1572864 | tf_op jit(solution)/shard_map/all_to_all | solution.py:387
  9.5 9.7 %collective-permute-start = (f32[27,2048]{1,0:T(8,128)}, f32[27,2048]{1,0:T(8,128)S(1)}, u32[]{:S(2)}, u32[]{:S(2)}) collective-permute-start(f32[27,2048]{1,0:T(8,128)} %get-tuple-element.24), channel_id=1, source_target_pairs={{0,16},{16,32},{32,48},{48,64},{64,80},{80,96},{96,112},{112,128},... | collective-permute-start | bytes 663560 | tf_op jit(solution)/shard_map/ppermute | solution.py:336
  14.3 47.1 %copy-start = (f32[6,3,16,2048]{3,2,1,0:T(8,128)S(1)}, f32[6,3,16,2048]{3,2,1,0:T(8,128)}, u32[]{:S(2)}) copy-start(f32[6,3,16,2048]{3,2,1,0:T(8,128)} %noise_ref.3) | copy-start | bytes 7077892
  14.3 47.1 %copy-start.1 = (f32[3,16,2048]{2,1,0:T(8,128)S(1)}, f32[3,16,2048]{2,1,0:T(8,128)}, u32[]{:S(2)}) copy-start(f32[3,16,2048]{2,1,0:T(8,128)} %solute_ref.5) | copy-start | bytes 1179652
  14.3 47.1 %copy-start.11 = (s32[6]{0:T(128)S(1)}, s32[6]{0:T(128)}, u32[]{:S(2)}) copy-start(s32[6]{0:T(128)} %group_ref.3) | copy-start | bytes 76
  14.4 47.1 %copy-start.12 = (f32[4]{0:T(128)S(1)}, f32[4]{0:T(128)}, u32[]{:S(2)}) copy-start(f32[4]{0:T(128)} %mobility_ref.3) | copy-start | bytes 52
  14.4 8.5 %collective-permute-start.1 = (f32[27,2048]{1,0:T(8,128)}, f32[27,2048]{1,0:T(8,128)S(1)}, u32[]{:S(2)}, u32[]{:S(2)}) collective-permute-start(f32[27,2048]{1,0:T(8,128)} %get-tuple-element.25), channel_id=1, source_target_pairs={{16,0},{32,16},{48,32},{64,48},{80,64},{96,80},{112,96},{128,112},... | collective-permute-start | bytes 663560 | tf_op jit(solution)/shard_map/ppermute | solution.py:337
  19.2 0.7 copy-start.5
  22.8 0.7 copy-start.7
  23.5 37.9 %copy-start.3 = (s32[3,16,2048]{2,1,0:T(8,128)S(1)}, s32[3,16,2048]{2,1,0:T(8,128)}, u32[]{:S(2)}) copy-start(s32[3,16,2048]{2,1,0:T(8,128)} %ids_ref.3) | copy-start | bytes 1179652
  23.5 37.9 %copy-start.6 = (f32[27,2048]{1,0:T(8,128)S(1)}, f32[27,2048]{1,0:T(8,128)}, u32[]{:S(2)}) copy-start(f32[27,2048]{1,0:T(8,128)} %copy-done.5) | copy-start | bytes 663556
  23.5 37.9 %copy-start.8 = (f32[27,2048]{1,0:T(8,128)S(1)}, f32[27,2048]{1,0:T(8,128)}, u32[]{:S(2)}) copy-start(f32[27,2048]{1,0:T(8,128)} %copy-done.7) | copy-start | bytes 663556
  66.9 22.6 %all-to-all-start.4 = ((f32[4,4,6,16,128]{4,3,2,1,0:T(8,128)}), f32[4,4,6,16,128]{4,3,2,1,0:T(8,128)S(1)}, u32[]{:S(2)}, u32[]{:S(2)}) async-start(f32[4,4,6,16,128]{4,3,2,1,0:T(8,128)} %bitcast.3), calls=%async_computation.4 | async-start | bytes 1572864 | tf_op jit(solution)/shard_map/all_to_all | solution.py:387
  70.4 14.2 %collective-permute-start.2 = (f32[24,2048]{1,0:T(8,128)S(1)}, f32[24,2048]{1,0:T(8,128)S(1)}, u32[]{:S(2)}, u32[]{:S(2)}) collective-permute-start(f32[24,2048]{1,0:T(8,128)S(1)} %get-tuple-element.34), channel_id=1, source_target_pairs={{0,16},{16,32},{32,48},{48,64},{64,80},{80,96},{96,112},{112,128},... | collective-permute-start | bytes 589832 | tf_op jit(solution)/shard_map/ppermute | solution.py:336
  82.0 33.7 %copy-start.4 = (f32[3,16,2048]{2,1,0:T(8,128)S(1)}, f32[3,16,2048]{2,1,0:T(8,128)}, u32[]{:S(2)}) copy-start(f32[3,16,2048]{2,1,0:T(8,128)} %get-tuple-element.30.middle_ref) | copy-start | bytes 1179652
  82.0 33.7 %copy-start.9 = (f32[9,2048]{1,0:T(8,128)S(1)}, f32[9,2048]{1,0:T(8,128)}, u32[]{:S(2)}) copy-start(f32[9,2048]{1,0:T(8,128)} %get-tuple-element.31.above_ref) | copy-start | bytes 221188
  82.0 33.7 %copy-start.10 = (f32[9,2048]{1,0:T(8,128)S(1)}, f32[9,2048]{1,0:T(8,128)}, u32[]{:S(2)}) copy-start(f32[9,2048]{1,0:T(8,128)} %get-tuple-element.32.below_ref) | copy-start | bytes 221188
  82.0 7.4 %collective-permute-start.3 = (f32[24,2048]{1,0:T(8,128)S(1)}, f32[24,2048]{1,0:T(8,128)S(1)}, u32[]{:S(2)}, u32[]{:S(2)}) collective-permute-start(f32[24,2048]{1,0:T(8,128)S(1)} %get-tuple-element.35), channel_id=1, source_target_pairs={{16,0},{32,16},{48,32},{64,48},{80,64},{96,80},{112,96},{128,112},... | collective-permute-start | bytes 589832 | tf_op jit(solution)/shard_map/ppermute | solution.py:337
  111.2 12.8 %all-to-all-start.7 = ((f32[4,4,6,16,128]{4,3,2,1,0:T(8,128)}), f32[4,4,6,16,128]{4,3,2,1,0:T(8,128)S(1)}, u32[]{:S(2)}, u32[]{:S(2)}) async-start(f32[4,4,6,16,128]{4,3,2,1,0:T(8,128)} %copies.3), calls=%async_computation.7 | async-start | bytes 1572864 | tf_op jit(solution)/shard_map/all_to_all | solution.py:387
  124.1 20.1 %collective-permute-start.4 = (f32[3,2048]{1,0:T(4,128)S(1)}, f32[3,2048]{1,0:T(4,128)S(1)}, u32[]{:S(2)}, u32[]{:S(2)}) collective-permute-start(f32[3,2048]{1,0:T(4,128)S(1)} %get-tuple-element.42), channel_id=1, source_target_pairs={{0,16},{16,32},{32,48},{48,64},{64,80},{80,96},{96,112},{112,128},... | collective-permute-start | bytes 73736 | tf_op jit(solution)/shard_map/ppermute | solution.py:336
  136.4 7.8 %collective-permute-start.5 = (f32[3,2048]{1,0:T(4,128)S(1)}, f32[3,2048]{1,0:T(4,128)S(1)}, u32[]{:S(2)}, u32[]{:S(2)}) collective-permute-start(f32[3,2048]{1,0:T(4,128)S(1)} %get-tuple-element.43), channel_id=1, source_target_pairs={{16,0},{32,16},{48,32},{64,48},{80,64},{96,80},{112,96},{128,112},... | collective-permute-start | bytes 73736 | tf_op jit(solution)/shard_map/ppermute | solution.py:337
  138.3 1.7 %copy-start.2 = (f32[6,3,16,2048]{3,2,1,0:T(8,128)S(1)}, f32[6,3,16,2048]{3,2,1,0:T(8,128)}, u32[]{:S(2)}) copy-start(f32[6,3,16,2048]{3,2,1,0:T(8,128)} %get-tuple-element.29.old_ref) | copy-start | bytes 7077892

commit v5 on v4

--- a/solution.py
+++ b/solution.py
@@ -31,6 +31,10 @@
 
 def hbm(*dims):
     return pltpu.HBM(dims, F32)
+
+
+def from_hbm(*arrays):
+    return [pltpu.with_memory_space_constraint(array, pltpu.HBM) for array in arrays]
 
 
 def params(mib=16):
@@ -135,7 +139,7 @@
 
 def first_step(
     first_ref, group_ref, mobility_ref, noise_ref, ids_ref, solute_ref, sums_ref, above_ref, below_ref,
-    eta_ref, next_sums_ref, next_ref, prev_ref, bulk_ref, rows_above_ref, rows_below_ref, base_ref, slope_ref,
+    eta_ref, next_sums_ref, next_ref, prev_ref, bulk_ref, base_ref, slope_ref,
 ):
     grain = pl.program_id(0)
 
@@ -150,8 +154,6 @@
                 bulk_ref[plane, :, columns] = bulk
                 prev_ref[row : row + 2, columns] = bulk[:2]
                 next_ref[row : row + 2, columns] = bulk[ROWS - 2 :]
-        rows_above_ref[...] = above_ref[GRAINS * PLANES :]
-        rows_below_ref[...] = below_ref[GRAINS * PLANES :]
 
     rate = time_step * mobility_ref[group_ref[grain]]
     planes = [
@@ -195,16 +197,14 @@
         ],
         out_specs=[grain_block, whole(*sums.shape)]
         + [whole(edge, COLS)] * 2
-        + [whole(*solute.shape)]
-        + [whole(3 * PLANES, COLS)] * 2,
+        + [whole(*solute.shape)],
         out_shape=[hbm(*noise.shape), shape(*sums.shape)]
         + [shape(edge, COLS)] * 2
-        + [hbm(*solute.shape)]
-        + [hbm(3 * PLANES, COLS)] * 2,
+        + [hbm(*solute.shape)],
         scratch_shapes=[pltpu.VMEM(solute.shape, F32)] * 2,
         compiler_params=params(),
         name="first_step",
-    )(first, groups, mobility, noise, ids, solute, sums, above, below)
+    )(first, groups, mobility, *from_hbm(noise, ids, solute), sums, *from_hbm(above, below))
 
 
 PAD = 8
@@ -221,13 +221,13 @@
 
 def solute_step(
     solute_ref, middle_ref, above_ref, below_ref, mid_above_ref, mid_below_ref,
-    out_ref, part_ref, deep_ref, bulk_ref,
+    out_ref, part_ref, ends_ref, deep_ref, bulk_ref,
 ):
     for plane in range(PLANES):
         for ref in (deep_ref, bulk_ref):
             ref[plane, :PAD] = jnp.zeros((PAD, COLS), F32)
             ref[plane, PAD + ROWS :] = jnp.zeros((PAD, COLS), F32)
-        row = 3 * plane
+        row = GRAINS * PLANES + 3 * plane
         deep_ref[plane, PAD - 3 : PAD] = above_ref[row : row + 3, :]
         deep_ref[plane, PAD : PAD + ROWS] = solute_ref[plane]
         deep_ref[plane, PAD + ROWS : PAD + ROWS + 3] = below_ref[row : row + 3, :]
@@ -247,35 +247,40 @@
         part = 2.0 * bulk_stiff * (moved[plane] - solute_mean) - solute_kappa * lap
         out_ref[plane] = moved[plane][PAD : PAD + ROWS]
         part_ref[plane] = part[PAD : PAD + ROWS]
+        ends_ref[plane : plane + 1, :] = part[PAD : PAD + 1]
+        ends_ref[PLANES + plane : PLANES + plane + 1, :] = part[PAD + ROWS - 1 : PAD + ROWS]
 
 
 def call_solute_step(solute, bulk, above, below, mid_above, mid_below):
     return pl.pallas_call(
         solute_step,
-        out_shape=[shape(*solute.shape)] * 2,
+        out_shape=[hbm(*solute.shape)] * 2 + [hbm(2 * PLANES, COLS)],
         scratch_shapes=[pltpu.VMEM((PLANES, DEEP, COLS), F32)] * 2,
         compiler_params=params(),
         name="solute_step",
-    )(solute, bulk, above, below, mid_above, mid_below)
-
-
-def second_potential(part_ref, sums_ref, out_ref, next_ref, prev_ref):
-    for plane in range(PLANES):
+    )(*from_hbm(solute, bulk, above, below, mid_above, mid_below))
+
+
+def end_rows(core_ref, ends_ref, sums_ref, inner_ref, outer_ref):
+    for plane in range(PLANES):
+        row = slice(plane, plane + 1)
         for block in range(BLOCKS):
             columns = column_block(block)
-            potential = part_ref[plane, :, columns] - sums_ref[block, PLANES + plane]
-            out_ref[plane, :, columns] = potential
-            prev_ref[plane : plane + 1, columns] = potential[:1]
-            next_ref[plane : plane + 1, columns] = potential[ROWS - 1 :]
-
-
-def call_second_potential(part, sums):
-    return pl.pallas_call(
-        second_potential,
-        out_shape=[shape(*part.shape), shape(PLANES, COLS), shape(PLANES, COLS)],
+            bulk = sums_ref[block, PLANES + plane]
+            top = ends_ref[plane : plane + 1, columns] - bulk[:1]
+            bottom = ends_ref[PLANES + plane : PLANES + plane + 1, columns] - bulk[ROWS - 1 :]
+            inner_ref[row, columns] = jnp.where(core_ref[0] == 0, bottom, top)
+            outer_ref[row, columns] = jnp.where(core_ref[0] == 0, top, bottom)
+
+
+def call_end_rows(core, ends, sums):
+    return pl.pallas_call(
+        end_rows,
+        in_specs=[smem(), whole(*ends.shape), whole(*sums.shape)],
+        out_shape=[shape(PLANES, COLS)] * 2,
         compiler_params=params(),
-        name="second_potential",
-    )(part, sums)
+        name="end_rows",
+    )(core, ends, sums)
 
 
 def second_step(
@@ -309,27 +314,42 @@
         compiler_params=params(),
         cost_estimate=pl.CostEstimate(flops=20_000_000, bytes_accessed=10_000_000, transcendentals=0),
         name="second_step",
-    )(groups, mobility, eta, solute, sums, above, below)
-
-
-def solute_end(solute_ref, potential_ref, above_ref, below_ref, out_ref):
+    )(groups, mobility, *from_hbm(eta, solute), sums, *from_hbm(above, below))
+
+
+def solute_end(core_ref, solute_ref, part_ref, sums_ref, inner_ref, outer_ref, out_ref, potential_ref):
     rows = lax.broadcasted_iota(jnp.int32, (ROWS, COLS), 0)
+    first_core = core_ref[0] == 0
+    for plane in range(PLANES):
+        for block in range(BLOCKS):
+            columns = column_block(block)
+            potential_ref[plane, :, columns] = part_ref[plane, :, columns] - sums_ref[block, PLANES + plane]
     planes = [potential_ref[plane] for plane in range(PLANES)]
     for plane, across in enumerate(beside(planes)):
         value = planes[plane]
-        up = jnp.where(rows == 0, above_ref[plane : plane + 1, :], pltpu.roll(value, 1, 0))
-        down = jnp.where(rows == ROWS - 1, below_ref[plane : plane + 1, :], pltpu.roll(value, ROWS - 1, 0))
+        inner, outer = inner_ref[plane : plane + 1, :], outer_ref[plane : plane + 1, :]
+        above, below = jnp.where(first_core, outer, inner), jnp.where(first_core, inner, outer)
+        up = jnp.where(rows == 0, above, pltpu.roll(value, 1, 0))
+        down = jnp.where(rows == ROWS - 1, below, pltpu.roll(value, ROWS - 1, 0))
         lap = up + down + along_columns(value) + across - 6.0 * value
         out_ref[plane] = solute_ref[plane] + time_step * solute_mobility * lap
 
 
-def call_solute_end(solute, potential, above, below):
+def call_solute_end(core, solute, part, sums, inner, outer):
     return pl.pallas_call(
         solute_end,
+        in_specs=[smem()] + [whole(*array.shape) for array in (solute, part, sums, inner, outer)],
         out_shape=shape(*solute.shape),
+        scratch_shapes=[pltpu.VMEM(solute.shape, F32)],
         compiler_params=params(),
         name="solute_end",
-    )(solute, potential, above, below)
+    )(core, solute, part, sums, inner, outer)
+
+
+def swapped(inner, outer, count):
+    inner = lax.ppermute(inner, SPACE, [(i, i ^ 1) for i in range(count)])
+    outer = lax.ppermute(outer, SPACE, [(i, (i + 2 * (i % 2) - 1) % count) for i in range(count)])
+    return inner, outer
 
 
 def exchange(to_next, to_prev, count):
@@ -368,49 +388,36 @@
 
 def call_owner(parts):
     return pl.pallas_call(
-        owner, out_shape=shape(*parts.shape), compiler_params=params(), name="owner"
+        owner, out_shape=hbm(BLOCKS, *parts.shape[1:]), compiler_params=params(), name="owner"
     )(parts)
-
-
-def copies(value_ref, out_ref):
-    for copy in range(out_ref.shape[0]):
-        out_ref[copy] = value_ref[...]
-
-
-def call_copies(value, count):
-    return pl.pallas_call(
-        copies, out_shape=shape(count, *value.shape), compiler_params=params(), name="copies"
-    )(value)
 
 
 def dealt(blocks, axis):
     return lax.all_to_all(blocks, axis, 0, 0, tiled=True)
 
 
-def total(sums, to_next, to_prev):
-    count = lax.axis_size("yl") * lax.axis_size("z") * lax.axis_size("core")
+def total(sums):
     along = lax.axis_size("x")
     parts = dealt(sums.reshape((along, BLOCKS // along) + sums.shape[1:]), "x")
-    parts, above, below = lax.optimization_barrier((parts, *exchange(to_next, to_prev, count)))
     parts = dealt(call_add_parts(parts), "yh")
-    parts = dealt(call_owner(parts), "yh")
-    return dealt(call_copies(parts, along), "x").reshape(sums.shape), above, below
+    return dealt(call_owner(parts), GRAIN)
 
 
 def shards(grain_ids, group_of, group_mobility, seed_noise, concentration):
     count = lax.axis_size("yl") * lax.axis_size("z") * lax.axis_size("core")
     first = (lax.axis_index(GRAIN) * GRAINS).astype(jnp.int32).reshape(1)
+    core = lax.axis_index("core").astype(jnp.int32).reshape(1)
     sums, to_next, to_prev = call_first_sums(first, seed_noise, grain_ids, concentration)
-    sums, above, below = total(sums, to_next, to_prev)
-    eta, sums, to_next, to_prev, bulk, rows_above, rows_below = call_first_step(
-        first, group_of, group_mobility, seed_noise, grain_ids, concentration, sums, above, below
+    above, below = exchange(to_next, to_prev, count)
+    eta, sums, to_next, to_prev, bulk = call_first_step(
+        first, group_of, group_mobility, seed_noise, grain_ids, concentration, total(sums), above, below
     )
-    sums, mid_above, mid_below = total(sums, to_next, to_prev)
-    solute, part = call_solute_step(concentration, bulk, rows_above, rows_below, mid_above, mid_below)
-    potential, to_next, to_prev = call_second_potential(part, sums)
-    end_above, end_below = exchange(to_next, to_prev, count)
+    mid_above, mid_below = exchange(to_next, to_prev, count)
+    sums = total(sums)
+    solute, part, ends = call_solute_step(concentration, bulk, above, below, mid_above, mid_below)
+    inner, outer = swapped(*call_end_rows(core, ends, sums), count)
     eta = call_second_step(group_of, group_mobility, eta, solute, sums, mid_above, mid_below)
-    solute = call_solute_end(solute, potential, end_above, end_below)
+    solute = call_solute_end(core, solute, part, sums, inner, outer)
     return eta, solute
 
 

time: 146 us -> 151 us (1.034)
  starting transfers between devices: 50.3 us -> 58.2 us
  Pallas kernels: 17.3 us -> 23.7 us
  blocking collectives: 58.5 us -> 52.6 us
  waiting for transfers between devices: 15.1 us -> 13 us
  local copies, waits for them, and re-layouts: 3.12 us -> 1.54 us
    ppermute x0 -> x2, starting transfers between devices: none -> 18 us  [the longest x1 16.1 us: swapped(): inner = lax.ppermute(inner, SPACE, [(i, i ^ 1) for i in range(count)])]
    ppermute x3 -> x2, starting transfers between devices: 28.7 us -> 17.3 us  [exchange(): lax.ppermute(to_next, SPACE, [(i, (i + 1) % count) for i in range(count)])]
    ppermute x3 -> x2, starting transfers between devices: 8.77 us -> 15.7 us  [exchange(): lax.ppermute(to_prev, SPACE, [((i + 1) % count, i) for i in range(count)])]
    all_to_all x5 -> x4, blocking collectives: 58.5 us -> 52.6 us  [dealt(): return lax.all_to_all(blocks, axis, 0, 0, tiled=True)]
    all_to_all x3 -> x2, starting transfers between devices: 12.8 us -> 7.23 us  [dealt(): return lax.all_to_all(blocks, axis, 0, 0, tiled=True)]
    pallas_call x7 -> x5, Pallas kernels: 3.66 us -> 6.66 us  [the longest x1 3.59 us: call_solute_step(): pl.pallas_call(solute_step, out_shape=[hbm(*solute.shape)] * 2 + [hbm(2 *...]
    ppermute x3 -> x2, waiting for transfers between devices: 7.79 us -> 5.72 us  [exchange(): lax.ppermute(to_prev, SPACE, [((i + 1) % count, i) for i in range(count)])]
    pallas_call x1, Pallas kernels: 4.21 us -> 6.13 us  [call_second_step(): pl.pallas_call(second_step, grid=(GRAINS,), in_specs=[smem(), smem(), gra...]
  transfers between devices with their start and end apart: 9 -> 8, of which waited for: 4 -> 4; matrix products, arithmetic and copies ran while one was open for 0% -> 0% of each run, Pallas kernels for 4% -> 6%
where the time goes in v5:
time: 151 us; the launch traced here: 150 us
  starting transfers between devices  58.2 us (39%)
  blocking collectives  52.6 us (35%)
  Pallas kernels  23.7 us (16%)
  waiting for transfers between devices  13 us (9%)
  local copies, waits for them, and re-layouts  1.54 us (1%)
    all_to_all x4, blocking collectives, dealt(): return lax.all_to_all(blocks, axis, 0, 0, tiled=True)  52.6 us
    ppermute x2, starting transfers between devices, exchange(): lax.ppermute(to_next, SPACE, [(i, (i + 1) % count) for i in range(count)])  17.3 us
    ppermute x1, starting transfers between devices, swapped(): inner = lax.ppermute(inner, SPACE, [(i, i ^ 1) for i in range(count)])  16.1 us
    ppermute x2, starting transfers between devices, exchange(): lax.ppermute(to_prev, SPACE, [((i + 1) % count, i) for i in range(count)])  15.7 us
    all_to_all x2, starting transfers between devices, dealt(): return lax.all_to_all(blocks, axis, 0, 0, tiled=True)  7.23 us
    pallas_call x1, Pallas kernels, call_first_step(): pl.pallas_call(first_step, grid=(GRAINS,), in_specs=[smem(), smem(), smem...  6.81 us
    pallas_call x1, Pallas kernels, call_second_step(): pl.pallas_call(second_step, grid=(GRAINS,), in_specs=[smem(), smem(), gra...  6.13 us
    all_to_all x2, waiting for transfers between devices, dealt(): return lax.all_to_all(blocks, axis, 0, 0, tiled=True)  5.88 us
  transfers between devices with their start and end apart: 8, of which 4 were waited for; matrix products, arithmetic and copies ran while one was open for 0% of the time, Pallas kernels for 6%

profile of v5, /device:TPU:1, one launch (start us, length us, event | category | flops | bytes accessed | tf_op | source)
XLA Modules:
  0.0 149.8 jit_solution(316805215714474709)
XLA Ops:
  0.6 4.0 %first_sums.1 = (f32[16,6,16,128]{3,2,1,0:T(8,128)}, f32[27,2048]{1,0:T(8,128)}, f32[27,2048]{1,0:T(8,128)}) custom-call(s32[1]{0:T(128)} %bitcast.first_ref, f32[6,3,16,2048]{3,2,1,0:T(8,128)} %noise_ref.3, s32[3,16,2048]{2,1,0:T(8,128)} %ids_ref.3, f32[3,16,2048]{2,1,0:T(8,128)} %solute_ref.5), custom_call_target="tpu_custom_call" | custom-call | tf_op jit(solution)/shard_map/first_sums/pallas_call | solution.py:88
  4.6 13.2 %all_to_all.30.parts_ref = f32[4,4,6,16,128]{4,3,2,1,0:T(8,128)S(1)} all-to-all(f32[4,4,6,16,128]{4,3,2,1,0:T(8,128)} %bitcast.5), channel_id=1, replica_groups=mesh['yl'=2,'z'=8,'core'=2,'x'=4,'yh'=4] {'x'}, dimensions={0} | all-to-all | bytes 1572864 | tf_op jit(solution)/shard_map/all_to_all | solution.py:396
  17.8 0.0 copy-start.10
  17.8 0.0 copy-start.3
  17.8 0.0 copy-start.4
  17.9 17.7 %all_to_all.31.parts_ref = f32[4,6,16,128]{3,2,1,0:T(8,128)S(1)} all-to-all(f32[4,6,16,128]{3,2,1,0:T(8,128)S(1)} %add_parts.2), channel_id=1, replica_groups=mesh['yl'=2,'z'=8,'core'=2,'x'=4,'yh'=4] {'yh'}, dimensions={0} | all-to-all | bytes 393216 | tf_op jit(solution)/shard_map/all_to_all | solution.py:396
  35.6 1.0 owner.2
  36.6 3.6 %all-to-all-start.2 = ((f32[16,6,16,128]{3,2,1,0:T(8,128)}), f32[16,6,16,128]{3,2,1,0:T(8,128)S(1)}, u32[]{:S(2)}, u32[]{:S(2)}) async-start(f32[16,6,16,128]{3,2,1,0:T(8,128)} %owner.2), calls=%async_computation.2 | async-start | bytes 1572864 | tf_op jit(solution)/shard_map/all_to_all | solution.py:396
  40.2 0.0 copy-done.10
  40.2 7.3 %collective-permute-start = (f32[27,2048]{1,0:T(8,128)S(1)}, f32[27,2048]{1,0:T(8,128)S(1)}, u32[]{:S(2)}, u32[]{:S(2)}) collective-permute-start(f32[27,2048]{1,0:T(8,128)S(1)} %copy-done.10), channel_id=1, source_target_pairs={{0,16},{16,32},{32,48},{48,64},{64,80},{80,96},{96,112},{112,128},... | collective-permute-start | bytes 663560 | tf_op jit(solution)/shard_map/ppermute | solution.py:356
  47.5 0.0 copy-done.9
  47.5 1.9 %collective-permute-start.1 = (f32[27,2048]{1,0:T(8,128)S(1)}, f32[27,2048]{1,0:T(8,128)S(1)}, u32[]{:S(2)}, u32[]{:S(2)}) collective-permute-start(f32[27,2048]{1,0:T(8,128)S(1)} %copy-done.9), channel_id=1, source_target_pairs={{16,0},{32,16},{48,32},{64,48},{80,64},{96,80},{112,96},{128,112},... | collective-permute-start | bytes 663560 | tf_op jit(solution)/shard_map/ppermute | solution.py:357
  49.5 1.4 collective-permute-done.above_ref
  50.8 0.0 copy-start.5
  50.8 4.7 %collective-permute-done.1.below_ref = f32[27,2048]{1,0:T(8,128)S(1)} collective-permute-done((f32[27,2048]{1,0:T(8,128)S(1)}, f32[27,2048]{1,0:T(8,128)S(1)}, u32[]{:S(2)}, u32[]{:S(2)}) %collective-permute-start.1) | collective-permute-done | bytes 221216 | tf_op jit(solution)/shard_map/ppermute | solution.py:357
  55.5 0.0 copy-start.6
  55.5 5.9 %all-to-all-done.2.sums_ref = f32[16,6,16,128]{3,2,1,0:T(8,128)S(1)} async-done(((f32[16,6,16,128]{3,2,1,0:T(8,128)}), f32[16,6,16,128]{3,2,1,0:T(8,128)S(1)}, u32[]{:S(2)}, u32[]{:S(2)}) %all-to-all-start.2) | async-done | bytes 786464 | tf_op jit(solution)/shard_map/all_to_all | solution.py:396
  61.4 0.0 copy-done.5
  61.4 0.0 copy-done.6
  61.4 0.0 copy-done.3
  61.4 0.0 copy-done.4
  61.4 6.8 %first_step.1 = (f32[6,3,16,2048]{3,2,1,0:T(8,128)}, f32[16,6,16,128]{3,2,1,0:T(8,128)S(1)}, f32[24,2048]{1,0:T(8,128)S(1)}, f32[24,2048]{1,0:T(8,128)S(1)}, f32[3,16,2048]{2,1,0:T(8,128)}) custom-call(s32[1]{0:T(128)} %bitcast.first_ref, s32[6]{0:T(128)S(1)} %copy-done.3, f32[4]{0:T(128)S(1)} %copy-done.4, f32[6,3,16,2048]{3,2,1,0:T(8,128)} %noise_ref.3, ...), custom_call_target="tpu_custom_call" | custom-call | tf_op jit(solution)/shard_map/first_step/pallas_call | solution.py:190
  68.2 10.7 %all_to_all.32.parts_ref = f32[4,4,6,16,128]{4,3,2,1,0:T(8,128)S(1)} all-to-all(f32[4,4,6,16,128]{4,3,2,1,0:T(8,128)S(1)} %bitcast.4), channel_id=1, replica_groups=mesh['yl'=2,'z'=8,'core'=2,'x'=4,'yh'=4] {'x'}, dimensions={0} | all-to-all | bytes 1572864 | tf_op jit(solution)/shard_map/all_to_all | solution.py:396
  79.0 11.0 %all_to_all.33.parts_ref = f32[4,6,16,128]{3,2,1,0:T(8,128)S(1)} all-to-all(f32[4,6,16,128]{3,2,1,0:T(8,128)S(1)} %add_parts.3), channel_id=1, replica_groups=mesh['yl'=2,'z'=8,'core'=2,'x'=4,'yh'=4] {'yh'}, dimensions={0} | all-to-all | bytes 393216 | tf_op jit(solution)/shard_map/all_to_all | solution.py:396
  90.0 1.0 owner.3
  91.0 3.6 %all-to-all-start.5 = ((f32[16,6,16,128]{3,2,1,0:T(8,128)}), f32[16,6,16,128]{3,2,1,0:T(8,128)S(1)}, u32[]{:S(2)}, u32[]{:S(2)}) async-start(f32[16,6,16,128]{3,2,1,0:T(8,128)} %owner.3), calls=%async_computation.5 | async-start | bytes 1572864 | tf_op jit(solution)/shard_map/all_to_all | solution.py:396
  94.6 10.0 %collective-permute-start.2 = (f32[24,2048]{1,0:T(8,128)S(1)}, f32[24,2048]{1,0:T(8,128)S(1)}, u32[]{:S(2)}, u32[]{:S(2)}) collective-permute-start(f32[24,2048]{1,0:T(8,128)S(1)} %get-tuple-element.20), channel_id=1, source_target_pairs={{0,16},{16,32},{32,48},{48,64},{64,80},{80,96},{96,112},{112,128},... | collective-permute-start | bytes 589832 | tf_op jit(solution)/shard_map/ppermute | solution.py:356
  104.6 13.8 %collective-permute-start.3 = (f32[24,2048]{1,0:T(8,128)S(1)}, f32[24,2048]{1,0:T(8,128)S(1)}, u32[]{:S(2)}, u32[]{:S(2)}) collective-permute-start(f32[24,2048]{1,0:T(8,128)S(1)} %get-tuple-element.21), channel_id=1, source_target_pairs={{16,0},{32,16},{48,32},{64,48},{80,64},{96,80},{112,96},{128,112},... | collective-permute-start | bytes 589832 | tf_op jit(solution)/shard_map/ppermute | solution.py:357
  118.4 0.0 collective-permute-done.2.mid_above_ref.above_ref
  118.4 0.0 copy-start.7
  118.4 1.0 collective-permute-done.3.mid_below_ref.below_ref
  119.4 0.0 copy-start.8
  119.4 0.0 copy-done.7
  119.4 0.7 copy-done.8
  120.1 3.6 %solute_step.1 = (f32[3,16,2048]{2,1,0:T(8,128)}, f32[3,16,2048]{2,1,0:T(8,128)}, f32[6,2048]{1,0:T(8,128)}) custom-call(f32[3,16,2048]{2,1,0:T(8,128)} %solute_ref.5, f32[3,16,2048]{2,1,0:T(8,128)} %get-tuple-element.19.middle_ref, f32[27,2048]{1,0:T(8,128)} %copy-done.5, f32[27,2048]{1,0:T(8,128)} %copy-done.6, f32[24,2048]{1,0:T(8,128)} %copy-done.7, ...), custom_call_target="tpu_custom_call" | custom-call | tf_op jit(solution)/shard_map/solute_step/pallas_call | solution.py:255
  123.7 0.0 all-to-all-done.5.sums_ref
  123.7 0.8 copy-done.2
  124.5 0.1 end_rows.1
  124.6 16.1 %collective-permute-start.4 = (f32[3,2048]{1,0:T(4,128)S(1)}, f32[3,2048]{1,0:T(4,128)S(1)}, u32[]{:S(2)}, u32[]{:S(2)}) collective-permute-start(f32[3,2048]{1,0:T(4,128)S(1)} %get-tuple-element.26), channel_id=1, source_target_pairs={{0,16},{16,0},{32,48},{48,32},{64,80},{80,64},{96,112},{112,96},{1... | collective-permute-start | bytes 73736 | tf_op jit(solution)/shard_map/ppermute | solution.py:350
  140.7 1.9 %collective-permute-start.5 = (f32[3,2048]{1,0:T(4,128)S(1)}, f32[3,2048]{1,0:T(4,128)S(1)}, u32[]{:S(2)}, u32[]{:S(2)}) collective-permute-start(f32[3,2048]{1,0:T(4,128)S(1)} %get-tuple-element.27), channel_id=1, source_target_pairs={{0,496},{16,32},{32,16},{48,64},{64,48},{80,96},{96,80},{112,128},... | collective-permute-start | bytes 73736 | tf_op jit(solution)/shard_map/ppermute | solution.py:351
  142.6 0.0 copy-start
  142.6 0.0 copy-start.1
  142.6 6.1 %second_step.1 = f32[6,3,16,2048]{3,2,1,0:T(8,128)} custom-call(s32[6]{0:T(128)S(1)} %copy-done.3, f32[4]{0:T(128)S(1)} %copy-done.4, f32[6,3,16,2048]{3,2,1,0:T(8,128)} %get-tuple-element.18.old_ref, f32[3,16,2048]{2,1,0:T(8,128)} %get-tuple-element.22.solute_ref, f32[16,6,16,128]{3,2,1,0:T(8,128)S(1)} %all-to-all-done.5.sums_ref, f32[24,2048]{1,0:T(8,128)} %copy-done.7, ...), custom_call_target="tpu_custom_call" | custom-call | flops 20000000 | bytes 10000000 | tf_op jit(solution)/shard_map/second_step/pallas_call | solution.py:304
  148.8 0.0 collective-permute-done.4.inner_ref
  148.8 0.0 collective-permute-done.5.outer_ref
  148.8 0.0 copy-done
  148.8 0.0 copy-done.1
  148.8 1.1 solute_end.1
  (4 shorter events, 0.1 us)
Async XLA Ops:
  17.8 22.4 %copy-start.10 = (f32[27,2048]{1,0:T(8,128)S(1)}, f32[27,2048]{1,0:T(8,128)}, u32[]{:S(2)}) copy-start(f32[27,2048]{1,0:T(8,128)} %get-tuple-element.16) | copy-start | bytes 663556
  17.8 29.7 %copy-start.9 = (f32[27,2048]{1,0:T(8,128)S(1)}, f32[27,2048]{1,0:T(8,128)}, u32[]{:S(2)}) copy-start(f32[27,2048]{1,0:T(8,128)} %get-tuple-element.17) | copy-start | bytes 663556
  17.8 43.6 %copy-start.3 = (s32[6]{0:T(128)S(1)}, s32[6]{0:T(128)}, u32[]{:S(2)}) copy-start(s32[6]{0:T(128)} %group_ref.3) | copy-start | bytes 76
  17.8 43.6 %copy-start.4 = (f32[4]{0:T(128)S(1)}, f32[4]{0:T(128)}, u32[]{:S(2)}) copy-start(f32[4]{0:T(128)} %mobility_ref.3) | copy-start | bytes 52
  36.6 24.8 %all-to-all-start.2 = ((f32[16,6,16,128]{3,2,1,0:T(8,128)}), f32[16,6,16,128]{3,2,1,0:T(8,128)S(1)}, u32[]{:S(2)}, u32[]{:S(2)}) async-start(f32[16,6,16,128]{3,2,1,0:T(8,128)} %owner.2), calls=%async_computation.2 | async-start | bytes 1572864 | tf_op jit(solution)/shard_map/all_to_all | solution.py:396
  40.2 10.6 %collective-permute-start = (f32[27,2048]{1,0:T(8,128)S(1)}, f32[27,2048]{1,0:T(8,128)S(1)}, u32[]{:S(2)}, u32[]{:S(2)}) collective-permute-start(f32[27,2048]{1,0:T(8,128)S(1)} %copy-done.10), channel_id=1, source_target_pairs={{0,16},{16,32},{32,48},{48,64},{64,80},{80,96},{96,112},{112,128},... | collective-permute-start | bytes 663560 | tf_op jit(solution)/shard_map/ppermute | solution.py:356
  47.5 8.0 %collective-permute-start.1 = (f32[27,2048]{1,0:T(8,128)S(1)}, f32[27,2048]{1,0:T(8,128)S(1)}, u32[]{:S(2)}, u32[]{:S(2)}) collective-permute-start(f32[27,2048]{1,0:T(8,128)S(1)} %copy-done.9), channel_id=1, source_target_pairs={{16,0},{32,16},{48,32},{64,48},{80,64},{96,80},{112,96},{128,112},... | collective-permute-start | bytes 663560 | tf_op jit(solution)/shard_map/ppermute | solution.py:357
  50.8 10.6 %copy-start.5 = (f32[27,2048]{1,0:T(8,128)}, f32[27,2048]{1,0:T(8,128)S(1)}, u32[]{:S(2)}) copy-start(f32[27,2048]{1,0:T(8,128)S(1)} %collective-permute-done.above_ref) | copy-start | bytes 663556
  55.5 5.9 %copy-start.6 = (f32[27,2048]{1,0:T(8,128)}, f32[27,2048]{1,0:T(8,128)S(1)}, u32[]{:S(2)}) copy-start(f32[27,2048]{1,0:T(8,128)S(1)} %collective-permute-done.1.below_ref) | copy-start | bytes 663556
  91.0 32.7 %all-to-all-start.5 = ((f32[16,6,16,128]{3,2,1,0:T(8,128)}), f32[16,6,16,128]{3,2,1,0:T(8,128)S(1)}, u32[]{:S(2)}, u32[]{:S(2)}) async-start(f32[16,6,16,128]{3,2,1,0:T(8,128)} %owner.3), calls=%async_computation.5 | async-start | bytes 1572864 | tf_op jit(solution)/shard_map/all_to_all | solution.py:396
  94.6 23.8 %collective-permute-start.2 = (f32[24,2048]{1,0:T(8,128)S(1)}, f32[24,2048]{1,0:T(8,128)S(1)}, u32[]{:S(2)}, u32[]{:S(2)}) collective-permute-start(f32[24,2048]{1,0:T(8,128)S(1)} %get-tuple-element.20), channel_id=1, source_target_pairs={{0,16},{16,32},{32,48},{48,64},{64,80},{80,96},{96,112},{112,128},... | collective-permute-start | bytes 589832 | tf_op jit(solution)/shard_map/ppermute | solution.py:356
  104.6 14.8 %collective-permute-start.3 = (f32[24,2048]{1,0:T(8,128)S(1)}, f32[24,2048]{1,0:T(8,128)S(1)}, u32[]{:S(2)}, u32[]{:S(2)}) collective-permute-start(f32[24,2048]{1,0:T(8,128)S(1)} %get-tuple-element.21), channel_id=1, source_target_pairs={{16,0},{32,16},{48,32},{64,48},{80,64},{96,80},{112,96},{128,112},... | collective-permute-start | bytes 589832 | tf_op jit(solution)/shard_map/ppermute | solution.py:357
  118.4 1.0 copy-start.7
  119.4 0.7 copy-start.8
  123.7 0.8 copy-start.2
  124.6 24.2 %collective-permute-start.4 = (f32[3,2048]{1,0:T(4,128)S(1)}, f32[3,2048]{1,0:T(4,128)S(1)}, u32[]{:S(2)}, u32[]{:S(2)}) collective-permute-start(f32[3,2048]{1,0:T(4,128)S(1)} %get-tuple-element.26), channel_id=1, source_target_pairs={{0,16},{16,0},{32,48},{48,32},{64,80},{80,64},{96,112},{112,96},{1... | collective-permute-start | bytes 73736 | tf_op jit(solution)/shard_map/ppermute | solution.py:350
  140.7 8.1 %collective-permute-start.5 = (f32[3,2048]{1,0:T(4,128)S(1)}, f32[3,2048]{1,0:T(4,128)S(1)}, u32[]{:S(2)}, u32[]{:S(2)}) collective-permute-start(f32[3,2048]{1,0:T(4,128)S(1)} %get-tuple-element.27), channel_id=1, source_target_pairs={{0,496},{16,32},{32,16},{48,64},{64,48},{80,96},{96,80},{112,128},... | collective-permute-start | bytes 73736 | tf_op jit(solution)/shard_map/ppermute | solution.py:351
  142.6 6.2 %copy-start = (f32[3,16,2048]{2,1,0:T(8,128)S(1)}, f32[3,16,2048]{2,1,0:T(8,128)}, u32[]{:S(2)}) copy-start(f32[3,16,2048]{2,1,0:T(8,128)} %get-tuple-element.22.solute_ref) | copy-start | bytes 1179652
  142.6 6.2 %copy-start.1 = (f32[3,16,2048]{2,1,0:T(8,128)S(1)}, f32[3,16,2048]{2,1,0:T(8,128)}, u32[]{:S(2)}) copy-start(f32[3,16,2048]{2,1,0:T(8,128)} %get-tuple-element.24.part_ref) | copy-start | bytes 1179652

commit v6 on v5

--- a/solution.py
+++ b/solution.py
@@ -61,28 +61,31 @@
     return slice(block * LANES, (block + 1) * LANES)
 
 
-def first_sums(first_ref, noise_ref, ids_ref, solute_ref, sums_ref, next_ref, prev_ref):
+def first_sums(first_ref, core_ref, noise_ref, more_ref, ids_ref, solute_ref, sums_ref, inner_ref, outer_ref):
+    first_core = core_ref[0] == 0
+    half = noise_ref.shape[0]
     for plane in range(PLANES):
         ids = ids_ref[plane]
         two = four = None
         for grain in range(GRAINS):
             seed = jnp.where(ids == first_ref[0] + grain, 0.9, 0.0).astype(F32)
-            eta = seed + noise_ref[grain, plane]
-            row = grain * PLANES + plane
-            prev_ref[row : row + 1, :] = eta[:1]
-            next_ref[row : row + 1, :] = eta[ROWS - 1 :]
+            eta = seed + (noise_ref[grain, plane] if grain < half else more_ref[grain - half, plane])
+            row = slice(grain * PLANES + plane, grain * PLANES + plane + 1)
+            inner_ref[row, :] = jnp.where(first_core, eta[ROWS - 1 :], eta[:1])
+            outer_ref[row, :] = jnp.where(first_core, eta[:1], eta[ROWS - 1 :])
             square = eta * eta
             two = square if two is None else two + square
             four = square * square if four is None else four + square * square
         for block in range(sums_ref.shape[0]):
             sums_ref[block, plane] = two[:, column_block(block)]
             sums_ref[block, PLANES + plane] = four[:, column_block(block)]
-        row = GRAINS * PLANES + 3 * plane
-        prev_ref[row : row + 3, :] = solute_ref[plane, :3]
-        next_ref[row : row + 3, :] = solute_ref[plane, ROWS - 3 :]
-
-
-def call_first_sums(first, noise, ids, solute):
+        row = slice(GRAINS * PLANES + 3 * plane, GRAINS * PLANES + 3 * plane + 3)
+        top, bottom = solute_ref[plane, :3], solute_ref[plane, ROWS - 3 :]
+        inner_ref[row, :] = jnp.where(first_core, bottom, top)
+        outer_ref[row, :] = jnp.where(first_core, top, bottom)
+
+
+def call_first_sums(first, core, noise, ids, solute):
     width = 512
     edge = GRAINS * PLANES + 3 * PLANES
     return pl.pallas_call(
@@ -90,7 +93,9 @@
         grid=(COLS // width,),
         in_specs=[
             smem(),
-            pl.BlockSpec((GRAINS, PLANES, ROWS, width), lambda i: (0, 0, 0, i)),
+            smem(),
+            pl.BlockSpec((GRAINS // 2, PLANES, ROWS, width), lambda i: (0, 0, 0, i)),
+            pl.BlockSpec((GRAINS // 2, PLANES, ROWS, width), lambda i: (1, 0, 0, i)),
             pl.BlockSpec((PLANES, ROWS, width), lambda i: (0, 0, i)),
             pl.BlockSpec((PLANES, ROWS, width), lambda i: (0, 0, i)),
         ],
@@ -106,7 +111,7 @@
         ],
         compiler_params=params(60),
         name="first_sums",
-    )(first, noise, ids, solute)
+    )(first, core, noise, noise, ids, solute)
 
 
 def factors(sums_ref, solute_ref, base_ref, slope_ref):
@@ -133,15 +138,22 @@
     return out
 
 
-def halo_rows(ref, grain):
-    return [ref[pl.ds(grain * PLANES + plane, 1), :] for plane in range(PLANES)]
+def halo_rows(core_ref, inner_ref, outer_ref, grain):
+    above, below = [], []
+    for plane in range(PLANES):
+        row = pl.ds(grain * PLANES + plane, 1)
+        inner, outer = inner_ref[row, :], outer_ref[row, :]
+        above.append(jnp.where(core_ref[0] == 0, outer, inner))
+        below.append(jnp.where(core_ref[0] == 0, inner, outer))
+    return above, below
 
 
 def first_step(
-    first_ref, group_ref, mobility_ref, noise_ref, ids_ref, solute_ref, sums_ref, above_ref, below_ref,
-    eta_ref, next_sums_ref, next_ref, prev_ref, bulk_ref, base_ref, slope_ref,
+    first_ref, core_ref, group_ref, mobility_ref, noise_ref, ids_ref, solute_ref, sums_ref, inner_ref, outer_ref,
+    eta_ref, next_sums_ref, next_inner_ref, next_outer_ref, bulk_ref, base_ref, slope_ref,
 ):
     grain = pl.program_id(0)
+    first_core = core_ref[0] == 0
 
     @pl.when(grain == 0)
     def _():
@@ -152,21 +164,21 @@
                 columns = column_block(block)
                 bulk = sums_ref[block, PLANES + plane]
                 bulk_ref[plane, :, columns] = bulk
-                prev_ref[row : row + 2, columns] = bulk[:2]
-                next_ref[row : row + 2, columns] = bulk[ROWS - 2 :]
+                next_inner_ref[row : row + 2, columns] = jnp.where(first_core, bulk[ROWS - 2 :], bulk[:2])
+                next_outer_ref[row : row + 2, columns] = jnp.where(first_core, bulk[:2], bulk[ROWS - 2 :])
 
     rate = time_step * mobility_ref[group_ref[grain]]
     planes = [
         jnp.where(ids_ref[plane] == first_ref[0] + grain, 0.9, 0.0).astype(F32) + noise_ref[0, plane]
         for plane in range(PLANES)
     ]
-    out = stepped(planes, halo_rows(above_ref, grain), halo_rows(below_ref, grain), rate, base_ref, slope_ref)
+    out = stepped(planes, *halo_rows(core_ref, inner_ref, outer_ref, grain), rate, base_ref, slope_ref)
     for plane in range(PLANES):
         eta = out[plane]
         eta_ref[0, plane] = eta
         row = pl.ds(grain * PLANES + plane, 1)
-        prev_ref[row, :] = eta[:1]
-        next_ref[row, :] = eta[ROWS - 1 :]
+        next_inner_ref[row, :] = jnp.where(first_core, eta[ROWS - 1 :], eta[:1])
+        next_outer_ref[row, :] = jnp.where(first_core, eta[:1], eta[ROWS - 1 :])
     for plane in range(PLANES):
         square = out[plane] * out[plane]
         fourth = square * square
@@ -184,16 +196,16 @@
                 next_sums_ref[block, PLANES + plane] += fourth[:, column_block(block)]
 
 
-def call_first_step(first, groups, mobility, noise, ids, solute, sums, above, below):
+def call_first_step(first, core, groups, mobility, noise, ids, solute, sums, inner, outer):
     edge = GRAINS * PLANES + 2 * PLANES
     grain_block = pl.BlockSpec((1, PLANES, ROWS, COLS), lambda i: (i, 0, 0, 0))
     return pl.pallas_call(
         first_step,
         grid=(GRAINS,),
         in_specs=[
-            smem(), smem(), smem(), grain_block,
+            smem(), smem(), smem(), smem(), grain_block,
             whole(*ids.shape), whole(*solute.shape), whole(*sums.shape),
-            whole(*above.shape), whole(*below.shape),
+            whole(*inner.shape), whole(*outer.shape),
         ],
         out_specs=[grain_block, whole(*sums.shape)]
         + [whole(edge, COLS)] * 2
@@ -204,7 +216,7 @@
         scratch_shapes=[pltpu.VMEM(solute.shape, F32)] * 2,
         compiler_params=params(),
         name="first_step",
-    )(first, groups, mobility, *from_hbm(noise, ids, solute), sums, *from_hbm(above, below))
+    )(first, core, groups, mobility, noise, ids, solute, sums, *from_hbm(inner, outer))
 
 
 PAD = 8
@@ -220,20 +232,27 @@
 
 
 def solute_step(
-    solute_ref, middle_ref, above_ref, below_ref, mid_above_ref, mid_below_ref,
+    core_ref, solute_ref, middle_ref, inner_ref, outer_ref, mid_inner_ref, mid_outer_ref,
     out_ref, part_ref, ends_ref, deep_ref, bulk_ref,
 ):
+    first_core = core_ref[0] == 0
+
+    def sides(inner, outer):
+        return jnp.where(first_core, outer, inner), jnp.where(first_core, inner, outer)
+
     for plane in range(PLANES):
         for ref in (deep_ref, bulk_ref):
             ref[plane, :PAD] = jnp.zeros((PAD, COLS), F32)
             ref[plane, PAD + ROWS :] = jnp.zeros((PAD, COLS), F32)
         row = GRAINS * PLANES + 3 * plane
-        deep_ref[plane, PAD - 3 : PAD] = above_ref[row : row + 3, :]
+        above, below = sides(inner_ref[row : row + 3, :], outer_ref[row : row + 3, :])
+        deep_ref[plane, PAD - 3 : PAD] = above
         deep_ref[plane, PAD : PAD + ROWS] = solute_ref[plane]
-        deep_ref[plane, PAD + ROWS : PAD + ROWS + 3] = below_ref[row : row + 3, :]
+        deep_ref[plane, PAD + ROWS : PAD + ROWS + 3] = below
         row = GRAINS * PLANES + 2 * plane
-        bulk_ref[plane, PAD - 2 : PAD] = mid_above_ref[row : row + 2, :]
-        bulk_ref[plane, PAD + ROWS : PAD + ROWS + 2] = mid_below_ref[row : row + 2, :]
+        above, below = sides(mid_inner_ref[row : row + 2, :], mid_outer_ref[row : row + 2, :])
+        bulk_ref[plane, PAD - 2 : PAD] = above
+        bulk_ref[plane, PAD + ROWS : PAD + ROWS + 2] = below
         bulk_ref[plane, PAD : PAD + ROWS] = middle_ref[plane]
     solute = [deep_ref[plane] for plane in range(PLANES)]
     potential = [
@@ -251,14 +270,16 @@
         ends_ref[PLANES + plane : PLANES + plane + 1, :] = part[PAD + ROWS - 1 : PAD + ROWS]
 
 
-def call_solute_step(solute, bulk, above, below, mid_above, mid_below):
+def call_solute_step(core, *arrays):
+    solute = arrays[0]
     return pl.pallas_call(
         solute_step,
+        in_specs=[smem()] + [whole(*array.shape) for array in arrays],
         out_shape=[hbm(*solute.shape)] * 2 + [hbm(2 * PLANES, COLS)],
         scratch_shapes=[pltpu.VMEM((PLANES, DEEP, COLS), F32)] * 2,
         compiler_params=params(),
         name="solute_step",
-    )(*from_hbm(solute, bulk, above, below, mid_above, mid_below))
+    )(core, *from_hbm(*arrays))
 
 
 def end_rows(core_ref, ends_ref, sums_ref, inner_ref, outer_ref):
@@ -284,7 +305,7 @@
 
 
 def second_step(
-    group_ref, mobility_ref, old_ref, solute_ref, sums_ref, above_ref, below_ref, eta_ref, base_ref, slope_ref
+    core_ref, group_ref, mobility_ref, old_ref, solute_ref, sums_ref, inner_ref, outer_ref, eta_ref, base_ref, slope_ref
 ):
     grain = pl.program_id(0)
 
@@ -294,19 +315,19 @@
 
     rate = time_step * mobility_ref[group_ref[grain]]
     planes = [old_ref[0, plane] for plane in range(PLANES)]
-    out = stepped(planes, halo_rows(above_ref, grain), halo_rows(below_ref, grain), rate, base_ref, slope_ref)
+    out = stepped(planes, *halo_rows(core_ref, inner_ref, outer_ref, grain), rate, base_ref, slope_ref)
     for plane in range(PLANES):
         eta_ref[0, plane] = out[plane]
 
 
-def call_second_step(groups, mobility, eta, solute, sums, above, below):
+def call_second_step(core, groups, mobility, eta, solute, sums, inner, outer):
     grain_block = pl.BlockSpec((1, PLANES, ROWS, COLS), lambda i: (i, 0, 0, 0))
     return pl.pallas_call(
         second_step,
         grid=(GRAINS,),
         in_specs=[
-            smem(), smem(), grain_block, whole(*solute.shape), whole(*sums.shape),
-            whole(*above.shape), whole(*below.shape),
+            smem(), smem(), smem(), grain_block, whole(*solute.shape), whole(*sums.shape),
+            whole(*inner.shape), whole(*outer.shape),
         ],
         out_specs=grain_block,
         out_shape=shape(*eta.shape),
@@ -314,7 +335,7 @@
         compiler_params=params(),
         cost_estimate=pl.CostEstimate(flops=20_000_000, bytes_accessed=10_000_000, transcendentals=0),
         name="second_step",
-    )(groups, mobility, *from_hbm(eta, solute), sums, *from_hbm(above, below))
+    )(core, groups, mobility, eta, solute, sums, inner, outer)
 
 
 def solute_end(core_ref, solute_ref, part_ref, sums_ref, inner_ref, outer_ref, out_ref, potential_ref):
@@ -352,12 +373,6 @@
     return inner, outer
 
 
-def exchange(to_next, to_prev, count):
-    above = lax.ppermute(to_next, SPACE, [(i, (i + 1) % count) for i in range(count)])
-    below = lax.ppermute(to_prev, SPACE, [((i + 1) % count, i) for i in range(count)])
-    return above, below
-
-
 def added(parts_ref, index):
     values = [parts_ref[(part,) + index] for part in range(parts_ref.shape[0])]
     while len(values) > 1:
@@ -388,35 +403,48 @@
 
 def call_owner(parts):
     return pl.pallas_call(
-        owner, out_shape=hbm(BLOCKS, *parts.shape[1:]), compiler_params=params(), name="owner"
+        owner, out_shape=shape(*parts.shape), compiler_params=params(), name="owner"
     )(parts)
+
+
+def copies(value_ref, out_ref):
+    for copy in range(out_ref.shape[0]):
+        out_ref[copy] = value_ref[...]
+
+
+def call_copies(value, count):
+    return pl.pallas_call(
+        copies, out_shape=shape(count, *value.shape), compiler_params=params(), name="copies"
+    )(value)
 
 
 def dealt(blocks, axis):
     return lax.all_to_all(blocks, axis, 0, 0, tiled=True)
 
 
-def total(sums):
+def total(sums, beside_it):
     along = lax.axis_size("x")
     parts = dealt(sums.reshape((along, BLOCKS // along) + sums.shape[1:]), "x")
+    parts, *beside_it = lax.optimization_barrier((parts, *beside_it))
     parts = dealt(call_add_parts(parts), "yh")
-    return dealt(call_owner(parts), GRAIN)
+    parts = dealt(call_owner(parts), "yh")
+    return dealt(call_copies(parts, along), "x").reshape(sums.shape), beside_it
 
 
 def shards(grain_ids, group_of, group_mobility, seed_noise, concentration):
     count = lax.axis_size("yl") * lax.axis_size("z") * lax.axis_size("core")
     first = (lax.axis_index(GRAIN) * GRAINS).astype(jnp.int32).reshape(1)
     core = lax.axis_index("core").astype(jnp.int32).reshape(1)
-    sums, to_next, to_prev = call_first_sums(first, seed_noise, grain_ids, concentration)
-    above, below = exchange(to_next, to_prev, count)
-    eta, sums, to_next, to_prev, bulk = call_first_step(
-        first, group_of, group_mobility, seed_noise, grain_ids, concentration, total(sums), above, below
+    sums, inner, outer = call_first_sums(first, core, seed_noise, grain_ids, concentration)
+    sums, (inner, outer) = total(sums, swapped(inner, outer, count))
+    eta, sums, mid_inner, mid_outer, bulk = call_first_step(
+        first, core, group_of, group_mobility, seed_noise, grain_ids, concentration, sums, inner, outer
     )
-    mid_above, mid_below = exchange(to_next, to_prev, count)
-    sums = total(sums)
-    solute, part, ends = call_solute_step(concentration, bulk, above, below, mid_above, mid_below)
+    mid_inner, mid_outer = swapped(mid_inner, mid_outer, count)
+    later = call_solute_step(core, concentration, bulk, inner, outer, mid_inner, mid_outer)
+    sums, (mid_inner, mid_outer, solute, part, ends) = total(sums, (mid_inner, mid_outer, *later))
     inner, outer = swapped(*call_end_rows(core, ends, sums), count)
-    eta = call_second_step(group_of, group_mobility, eta, solute, sums, mid_above, mid_below)
+    eta = call_second_step(core, group_of, group_mobility, eta, solute, sums, mid_inner, mid_outer)
     solute = call_solute_end(core, solute, part, sums, inner, outer)
     return eta, solute
 

time: 151 us -> 151 us (level)
  the two profiles are of different devices: /device:TPU:1 before, /device:TPU:8 now
where the time goes in v6:
time: 151 us
  blocking collectives  80.3 us (53%)
  starting transfers between devices  41.7 us (28%)
  Pallas kernels  19.4 us (13%)
  waiting for transfers between devices  6.96 us (5%)
    all_to_all x6, blocking collectives, dealt(): return lax.all_to_all(blocks, axis, 0, 0, tiled=True)  80.3 us
    ppermute x3, starting transfers between devices, swapped(): lax.ppermute(outer, SPACE, [(i, (i + 2 * (i % 2) - 1) % count) for i in r...  28.2 us
    all_to_all x2, starting transfers between devices, dealt(): return lax.all_to_all(blocks, axis, 0, 0, tiled=True)  7.79 us
    ppermute x3, waiting for transfers between devices, swapped(): lax.ppermute(outer, SPACE, [(i, (i + 2 * (i % 2) - 1) % count) for i in r...  6.95 us
    pallas_call x1, Pallas kernels, call_first_step(): pl.pallas_call(first_step, grid=(GRAINS,), in_specs=[smem(), smem(), smem...  5.87 us
    ppermute x3, starting transfers between devices, swapped(): inner = lax.ppermute(inner, SPACE, [(i, i ^ 1) for i in range(count)])  5.75 us
    pallas_call x1, Pallas kernels, call_second_step(): pl.pallas_call(second_step, grid=(GRAINS,), in_specs=[smem(), smem(), sme...  4.4 us
    pallas_call x1, Pallas kernels, call_first_sums(): pl.pallas_call(first_sums, grid=(COLS // width,), in_specs=[smem(), smem(...  4.11 us
  transfers between devices with their start and end apart: 8, of which 2 were waited for; matrix products, arithmetic and copies ran while one was open for 0% of the time, Pallas kernels for 5%

profile of v6, /device:TPU:8, one launch (start us, length us, event | category | flops | bytes accessed | tf_op | source)
XLA Modules:
  0.0 150.6 jit_solution(1588952144454693378)
XLA Ops:
  0.6 4.1 %first_sums.1 = (f32[16,6,16,128]{3,2,1,0:T(8,128)}, f32[27,2048]{1,0:T(8,128)}, f32[27,2048]{1,0:T(8,128)}) custom-call(s32[1]{0:T(128)} %bitcast.1.first_ref, s32[1]{0:T(128)} %bitcast.core_ref, f32[6,3,16,2048]{3,2,1,0:T(8,128)} %noise_ref.3, f32[6,3,16,2048]{3,2,1,0:T(8,128)} %noise_ref.3, s32[3,16,2048]{2,1,0:T(8,128)} %ids_ref.3, f32[3,16,2048]{2,1,0:T(8,128)} %solute_ref.5), custom_call_target="tpu_custom_call" | custom-call | tf_op jit(solution)/shard_map/first_sums/pallas_call | solution.py:91
  4.8 4.3 %all-to-all-start = ((f32[4,4,6,16,128]{4,3,2,1,0:T(8,128)}), f32[4,4,6,16,128]{4,3,2,1,0:T(8,128)S(1)}, u32[]{:S(2)}, u32[]{:S(2)}) async-start(f32[4,4,6,16,128]{4,3,2,1,0:T(8,128)} %bitcast.10), calls=%async_computation | async-start | bytes 1572864 | tf_op jit(solution)/shard_map/all_to_all | solution.py:422
  9.0 1.9 %collective-permute-start = (f32[27,2048]{1,0:T(8,128)}, f32[27,2048]{1,0:T(8,128)S(1)}, u32[]{:S(2)}, u32[]{:S(2)}) collective-permute-start(f32[27,2048]{1,0:T(8,128)} %get-tuple-element.25), channel_id=1, source_target_pairs={{0,16},{16,0},{32,48},{48,32},{64,80},{80,64},{96,112},{112,96},{1... | collective-permute-start | bytes 663560 | tf_op jit(solution)/shard_map/ppermute | solution.py:371
  11.0 0.0 copy-start
  11.0 0.0 copy-start.1
  11.0 0.0 copy-start.11
  11.0 0.0 copy-start.12
  11.0 11.2 %collective-permute-start.1 = (f32[27,2048]{1,0:T(8,128)}, f32[27,2048]{1,0:T(8,128)}, u32[]{:S(2)}, u32[]{:S(2)}) collective-permute-start(f32[27,2048]{1,0:T(8,128)} %get-tuple-element.26), channel_id=1, source_target_pairs={{0,496},{16,32},{32,16},{48,64},{64,48},{80,96},{96,80},{112,128},... | collective-permute-start | bytes 663560 | tf_op jit(solution)/shard_map/ppermute | solution.py:372
  22.2 0.0 collective-permute-done.inner_ref
  22.2 0.0 copy-start.13
  22.2 0.7 copy-done.13
  22.9 3.6 %collective-permute-done.1.outer_ref = f32[27,2048]{1,0:T(8,128)} collective-permute-done((f32[27,2048]{1,0:T(8,128)}, f32[27,2048]{1,0:T(8,128)}, u32[]{:S(2)}, u32[]{:S(2)}) %collective-permute-start.1) | collective-permute-done | bytes 221216 | tf_op jit(solution)/shard_map/ppermute | solution.py:372
  26.6 0.0 all-to-all-done.parts_ref
  26.6 16.8 %all_to_all.40.parts_ref = f32[4,6,16,128]{3,2,1,0:T(8,128)S(1)} all-to-all(f32[4,6,16,128]{3,2,1,0:T(8,128)S(1)} %add_parts.2), channel_id=1, replica_groups=mesh['yl'=2,'z'=8,'core'=2,'x'=4,'yh'=4] {'yh'}, dimensions={0} | all-to-all | bytes 393216 | tf_op jit(solution)/shard_map/all_to_all | solution.py:422
  43.5 11.6 %all_to_all.41.value_ref = f32[4,6,16,128]{3,2,1,0:T(8,128)S(1)} all-to-all(f32[4,6,16,128]{3,2,1,0:T(8,128)S(1)} %owner.2), channel_id=1, replica_groups=mesh['yl'=2,'z'=8,'core'=2,'x'=4,'yh'=4] {'yh'}, dimensions={0} | all-to-all | bytes 393216 | tf_op jit(solution)/shard_map/all_to_all | solution.py:422
  55.1 0.1 copies.2
  55.1 14.1 %all_to_all.42 = f32[4,4,6,16,128]{4,3,2,1,0:T(8,128)S(1)} all-to-all(f32[4,4,6,16,128]{4,3,2,1,0:T(8,128)S(1)} %copies.2), channel_id=1, replica_groups=mesh['yl'=2,'z'=8,'core'=2,'x'=4,'yh'=4] {'x'}, dimensions={0} | all-to-all | bytes 1572864 | tf_op jit(solution)/shard_map/all_to_all | solution.py:422
  69.2 0.0 copy-done
  69.2 0.0 copy-done.1
  69.2 0.0 copy-done.11
  69.2 0.0 copy-done.12
  69.2 0.0 copy-done.3
  69.3 5.9 %first_step.1 = (f32[6,3,16,2048]{3,2,1,0:T(8,128)}, f32[16,6,16,128]{3,2,1,0:T(8,128)}, f32[24,2048]{1,0:T(8,128)S(1)}, f32[24,2048]{1,0:T(8,128)S(1)}, f32[3,16,2048]{2,1,0:T(8,128)}) custom-call(s32[1]{0:T(128)} %bitcast.1.first_ref, s32[1]{0:T(128)} %bitcast.core_ref, s32[6]{0:T(128)S(1)} %copy-done.11, f32[4]{0:T(128)S(1)} %copy-done.12, ...), custom_call_target="tpu_custom_call" | custom-call | tf_op jit(solution)/shard_map/first_step/pallas_call | solution.py:202
  75.1 3.5 %all-to-all-start.4 = ((f32[4,4,6,16,128]{4,3,2,1,0:T(8,128)}), f32[4,4,6,16,128]{4,3,2,1,0:T(8,128)S(1)}, u32[]{:S(2)}, u32[]{:S(2)}) async-start(f32[4,4,6,16,128]{4,3,2,1,0:T(8,128)} %bitcast.4), calls=%async_computation.4 | async-start | bytes 1572864 | tf_op jit(solution)/shard_map/all_to_all | solution.py:422
  78.6 1.9 %collective-permute-start.2 = (f32[24,2048]{1,0:T(8,128)S(1)}, f32[24,2048]{1,0:T(8,128)S(1)}, u32[]{:S(2)}, u32[]{:S(2)}) collective-permute-start(f32[24,2048]{1,0:T(8,128)S(1)} %get-tuple-element.32), channel_id=1, source_target_pairs={{0,16},{16,0},{32,48},{48,32},{64,80},{80,64},{96,112},{112,96},{1... | collective-permute-start | bytes 589832 | tf_op jit(solution)/shard_map/ppermute | solution.py:371
  80.6 8.8 %collective-permute-start.3 = (f32[24,2048]{1,0:T(8,128)S(1)}, f32[24,2048]{1,0:T(8,128)S(1)}, u32[]{:S(2)}, u32[]{:S(2)}) collective-permute-start(f32[24,2048]{1,0:T(8,128)S(1)} %get-tuple-element.33), channel_id=1, source_target_pairs={{0,496},{16,32},{32,16},{48,64},{64,48},{80,96},{96,80},{112,128},... | collective-permute-start | bytes 589832 | tf_op jit(solution)/shard_map/ppermute | solution.py:372
  89.4 0.0 collective-permute-done.2.mid_inner_ref.inner_ref
  89.4 0.0 copy-start.5
  89.4 3.3 %collective-permute-done.3.mid_outer_ref.outer_ref = f32[24,2048]{1,0:T(8,128)S(1)} collective-permute-done((f32[24,2048]{1,0:T(8,128)S(1)}, f32[24,2048]{1,0:T(8,128)S(1)}, u32[]{:S(2)}, u32[]{:S(2)}) %collective-permute-start.3) | collective-permute-done | bytes 196640 | tf_op jit(solution)/shard_map/ppermute | solution.py:372
  92.7 0.0 copy-done.5
  92.7 0.7 copy-done.7
  93.4 3.6 %solute_step.1 = (f32[3,16,2048]{2,1,0:T(8,128)}, f32[3,16,2048]{2,1,0:T(8,128)}, f32[6,2048]{1,0:T(8,128)}) custom-call(s32[1]{0:T(128)} %bitcast.core_ref, f32[3,16,2048]{2,1,0:T(8,128)} %solute_ref.5, f32[3,16,2048]{2,1,0:T(8,128)} %get-tuple-element.34.middle_ref, f32[27,2048]{1,0:T(8,128)} %copy-done.13, f32[27,2048]{1,0:T(8,128)} %collective-permute-done.1.outer_ref, ...), custom_call_target="tpu_custom_call" | custom-call | tf_op jit(solution)/shard_map/solute_step/pallas_call | solution.py:275
  97.0 0.0 all-to-all-done.4.parts_ref
  97.1 0.0 copy-start.2
  97.1 0.0 copy-start.4
  97.1 0.0 copy-start.6
  97.1 0.0 copy-start.8
  97.1 12.0 %all_to_all.43.parts_ref = f32[4,6,16,128]{3,2,1,0:T(8,128)S(1)} all-to-all(f32[4,6,16,128]{3,2,1,0:T(8,128)S(1)} %add_parts.3), channel_id=1, replica_groups=mesh['yl'=2,'z'=8,'core'=2,'x'=4,'yh'=4] {'yh'}, dimensions={0} | all-to-all | bytes 393216 | tf_op jit(solution)/shard_map/all_to_all | solution.py:422
  109.1 11.7 %all_to_all.44.value_ref = f32[4,6,16,128]{3,2,1,0:T(8,128)S(1)} all-to-all(f32[4,6,16,128]{3,2,1,0:T(8,128)S(1)} %owner.3), channel_id=1, replica_groups=mesh['yl'=2,'z'=8,'core'=2,'x'=4,'yh'=4] {'yh'}, dimensions={0} | all-to-all | bytes 393216 | tf_op jit(solution)/shard_map/all_to_all | solution.py:422
  120.8 0.1 copies.3
  120.9 14.0 %all_to_all.45 = f32[4,4,6,16,128]{4,3,2,1,0:T(8,128)S(1)} all-to-all(f32[4,4,6,16,128]{4,3,2,1,0:T(8,128)S(1)} %copies.3), channel_id=1, replica_groups=mesh['yl'=2,'z'=8,'core'=2,'x'=4,'yh'=4] {'x'}, dimensions={0} | all-to-all | bytes 1572864 | tf_op jit(solution)/shard_map/all_to_all | solution.py:422
  134.9 0.1 end_rows.1
  135.0 1.9 %collective-permute-start.4 = (f32[3,2048]{1,0:T(4,128)S(1)}, f32[3,2048]{1,0:T(4,128)S(1)}, u32[]{:S(2)}, u32[]{:S(2)}) collective-permute-start(f32[3,2048]{1,0:T(4,128)S(1)} %get-tuple-element.44), channel_id=1, source_target_pairs={{0,16},{16,0},{32,48},{48,32},{64,80},{80,64},{96,112},{112,96},{1... | collective-permute-start | bytes 73736 | tf_op jit(solution)/shard_map/ppermute | solution.py:371
  136.9 8.2 %collective-permute-start.5 = (f32[3,2048]{1,0:T(4,128)S(1)}, f32[3,2048]{1,0:T(4,128)S(1)}, u32[]{:S(2)}, u32[]{:S(2)}) collective-permute-start(f32[3,2048]{1,0:T(4,128)S(1)} %get-tuple-element.45), channel_id=1, source_target_pairs={{0,496},{16,32},{32,16},{48,64},{64,48},{80,96},{96,80},{112,128},... | collective-permute-start | bytes 73736 | tf_op jit(solution)/shard_map/ppermute | solution.py:372
  145.2 4.4 %second_step.1 = f32[6,3,16,2048]{3,2,1,0:T(8,128)} custom-call(s32[1]{0:T(128)} %bitcast.core_ref, s32[6]{0:T(128)S(1)} %copy-done.11, f32[4]{0:T(128)S(1)} %copy-done.12, f32[6,3,16,2048]{3,2,1,0:T(8,128)S(1)} %copy-done.2, f32[3,16,2048]{2,1,0:T(8,128)S(1)} %copy-done.4, f32[16,6,16,128]{3,2,1,0:T(8,128)S(1)} %bitcast.7, f32[24,2048]{1,0:T(8,128)S(1)} %copy-done.6, ...), custom_call_target="tpu_custom_call" | custom-call | flops 20000000 | bytes 10000000 | tf_op jit(solution)/shard_map/second_step/pallas_call | solution.py:325
  149.5 0.0 collective-permute-done.4.inner_ref
  149.6 0.0 collective-permute-done.5.outer_ref
  149.6 1.1 solute_end.1
  (14 shorter events, 0.1 us)
Async XLA Ops:
  4.8 21.8 %all-to-all-start = ((f32[4,4,6,16,128]{4,3,2,1,0:T(8,128)}), f32[4,4,6,16,128]{4,3,2,1,0:T(8,128)S(1)}, u32[]{:S(2)}, u32[]{:S(2)}) async-start(f32[4,4,6,16,128]{4,3,2,1,0:T(8,128)} %bitcast.10), calls=%async_computation | async-start | bytes 1572864 | tf_op jit(solution)/shard_map/all_to_all | solution.py:422
  9.0 13.2 %collective-permute-start = (f32[27,2048]{1,0:T(8,128)}, f32[27,2048]{1,0:T(8,128)S(1)}, u32[]{:S(2)}, u32[]{:S(2)}) collective-permute-start(f32[27,2048]{1,0:T(8,128)} %get-tuple-element.25), channel_id=1, source_target_pairs={{0,16},{16,0},{32,48},{48,32},{64,80},{80,64},{96,112},{112,96},{1... | collective-permute-start | bytes 663560 | tf_op jit(solution)/shard_map/ppermute | solution.py:371
  11.0 58.3 %copy-start = (f32[6,3,16,2048]{3,2,1,0:T(8,128)S(1)}, f32[6,3,16,2048]{3,2,1,0:T(8,128)}, u32[]{:S(2)}) copy-start(f32[6,3,16,2048]{3,2,1,0:T(8,128)} %noise_ref.3) | copy-start | bytes 7077892
  11.0 58.3 %copy-start.1 = (f32[3,16,2048]{2,1,0:T(8,128)S(1)}, f32[3,16,2048]{2,1,0:T(8,128)}, u32[]{:S(2)}) copy-start(f32[3,16,2048]{2,1,0:T(8,128)} %solute_ref.5) | copy-start | bytes 1179652
  11.0 58.2 %copy-start.11 = (s32[6]{0:T(128)S(1)}, s32[6]{0:T(128)}, u32[]{:S(2)}) copy-start(s32[6]{0:T(128)} %group_ref.3) | copy-start | bytes 76
  11.0 58.2 %copy-start.12 = (f32[4]{0:T(128)S(1)}, f32[4]{0:T(128)}, u32[]{:S(2)}) copy-start(f32[4]{0:T(128)} %mobility_ref.3) | copy-start | bytes 52
  11.0 15.6 %collective-permute-start.1 = (f32[27,2048]{1,0:T(8,128)}, f32[27,2048]{1,0:T(8,128)}, u32[]{:S(2)}, u32[]{:S(2)}) collective-permute-start(f32[27,2048]{1,0:T(8,128)} %get-tuple-element.26), channel_id=1, source_target_pairs={{0,496},{16,32},{32,16},{48,64},{64,48},{80,96},{96,80},{112,128},... | collective-permute-start | bytes 663560 | tf_op jit(solution)/shard_map/ppermute | solution.py:372
  22.2 0.7 copy-start.13
  26.6 42.7 %copy-start.3 = (s32[3,16,2048]{2,1,0:T(8,128)S(1)}, s32[3,16,2048]{2,1,0:T(8,128)}, u32[]{:S(2)}) copy-start(s32[3,16,2048]{2,1,0:T(8,128)} %ids_ref.3) | copy-start | bytes 1179652
  75.1 21.9 %all-to-all-start.4 = ((f32[4,4,6,16,128]{4,3,2,1,0:T(8,128)}), f32[4,4,6,16,128]{4,3,2,1,0:T(8,128)S(1)}, u32[]{:S(2)}, u32[]{:S(2)}) async-start(f32[4,4,6,16,128]{4,3,2,1,0:T(8,128)} %bitcast.4), calls=%async_computation.4 | async-start | bytes 1572864 | tf_op jit(solution)/shard_map/all_to_all | solution.py:422
  78.6 10.8 %collective-permute-start.2 = (f32[24,2048]{1,0:T(8,128)S(1)}, f32[24,2048]{1,0:T(8,128)S(1)}, u32[]{:S(2)}, u32[]{:S(2)}) collective-permute-start(f32[24,2048]{1,0:T(8,128)S(1)} %get-tuple-element.32), channel_id=1, source_target_pairs={{0,16},{16,0},{32,48},{48,32},{64,80},{80,64},{96,112},{112,96},{1... | collective-permute-start | bytes 589832 | tf_op jit(solution)/shard_map/ppermute | solution.py:371
  80.6 12.2 %collective-permute-start.3 = (f32[24,2048]{1,0:T(8,128)S(1)}, f32[24,2048]{1,0:T(8,128)S(1)}, u32[]{:S(2)}, u32[]{:S(2)}) collective-permute-start(f32[24,2048]{1,0:T(8,128)S(1)} %get-tuple-element.33), channel_id=1, source_target_pairs={{0,496},{16,32},{32,16},{48,64},{64,48},{80,96},{96,80},{112,128},... | collective-permute-start | bytes 589832 | tf_op jit(solution)/shard_map/ppermute | solution.py:372
  89.4 3.3 %copy-start.5 = (f32[24,2048]{1,0:T(8,128)}, f32[24,2048]{1,0:T(8,128)S(1)}, u32[]{:S(2)}) copy-start(f32[24,2048]{1,0:T(8,128)S(1)} %collective-permute-done.2.mid_inner_ref.inner_ref) | copy-start | bytes 589828
  92.7 0.7 copy-start.7
  97.0 37.9 %copy-start.10 = (f32[6,2048]{1,0:T(8,128)S(1)}, f32[6,2048]{1,0:T(8,128)}, u32[]{:S(2)}) copy-start(f32[6,2048]{1,0:T(8,128)} %get-tuple-element.43.ends_ref) | copy-start | bytes 147460
  97.1 48.0 %copy-start.2 = (f32[6,3,16,2048]{3,2,1,0:T(8,128)S(1)}, f32[6,3,16,2048]{3,2,1,0:T(8,128)}, u32[]{:S(2)}) copy-start(f32[6,3,16,2048]{3,2,1,0:T(8,128)} %get-tuple-element.30.old_ref) | copy-start | bytes 7077892
  97.1 48.0 %copy-start.4 = (f32[3,16,2048]{2,1,0:T(8,128)S(1)}, f32[3,16,2048]{2,1,0:T(8,128)}, u32[]{:S(2)}) copy-start(f32[3,16,2048]{2,1,0:T(8,128)} %get-tuple-element.38.solute_ref) | copy-start | bytes 1179652
  97.1 48.0 %copy-start.6 = (f32[24,2048]{1,0:T(8,128)S(1)}, f32[24,2048]{1,0:T(8,128)}, u32[]{:S(2)}) copy-start(f32[24,2048]{1,0:T(8,128)} %copy-done.5) | copy-start | bytes 589828
  97.1 48.0 %copy-start.8 = (f32[24,2048]{1,0:T(8,128)S(1)}, f32[24,2048]{1,0:T(8,128)}, u32[]{:S(2)}) copy-start(f32[24,2048]{1,0:T(8,128)} %copy-done.7) | copy-start | bytes 589828
  135.0 14.5 %collective-permute-start.4 = (f32[3,2048]{1,0:T(4,128)S(1)}, f32[3,2048]{1,0:T(4,128)S(1)}, u32[]{:S(2)}, u32[]{:S(2)}) collective-permute-start(f32[3,2048]{1,0:T(4,128)S(1)} %get-tuple-element.44), channel_id=1, source_target_pairs={{0,16},{16,0},{32,48},{48,32},{64,80},{80,64},{96,112},{112,96},{1... | collective-permute-start | bytes 73736 | tf_op jit(solution)/shard_map/ppermute | solution.py:371
  136.9 12.6 %collective-permute-start.5 = (f32[3,2048]{1,0:T(4,128)S(1)}, f32[3,2048]{1,0:T(4,128)S(1)}, u32[]{:S(2)}, u32[]{:S(2)}) collective-permute-start(f32[3,2048]{1,0:T(4,128)S(1)} %get-tuple-element.45), channel_id=1, source_target_pairs={{0,496},{16,32},{32,16},{48,64},{64,48},{80,96},{96,80},{112,128},... | collective-permute-start | bytes 73736 | tf_op jit(solution)/shard_map/ppermute | solution.py:372
  145.1 4.4 %copy-start.9 = (f32[3,16,2048]{2,1,0:T(8,128)S(1)}, f32[3,16,2048]{2,1,0:T(8,128)}, u32[]{:S(2)}) copy-start(f32[3,16,2048]{2,1,0:T(8,128)} %get-tuple-element.42.part_ref) | copy-start | bytes 1179652

commit v7 on v6

--- a/solution.py
+++ b/solution.py
@@ -61,15 +61,14 @@
     return slice(block * LANES, (block + 1) * LANES)
 
 
-def first_sums(first_ref, core_ref, noise_ref, more_ref, ids_ref, solute_ref, sums_ref, inner_ref, outer_ref):
+def first_sums(first_ref, core_ref, noise_ref, ids_ref, sums_ref, inner_ref, outer_ref):
     first_core = core_ref[0] == 0
-    half = noise_ref.shape[0]
     for plane in range(PLANES):
         ids = ids_ref[plane]
         two = four = None
         for grain in range(GRAINS):
             seed = jnp.where(ids == first_ref[0] + grain, 0.9, 0.0).astype(F32)
-            eta = seed + (noise_ref[grain, plane] if grain < half else more_ref[grain - half, plane])
+            eta = seed + noise_ref[grain, plane]
             row = slice(grain * PLANES + plane, grain * PLANES + plane + 1)
             inner_ref[row, :] = jnp.where(first_core, eta[ROWS - 1 :], eta[:1])
             outer_ref[row, :] = jnp.where(first_core, eta[:1], eta[ROWS - 1 :])
@@ -79,24 +78,18 @@
         for block in range(sums_ref.shape[0]):
             sums_ref[block, plane] = two[:, column_block(block)]
             sums_ref[block, PLANES + plane] = four[:, column_block(block)]
-        row = slice(GRAINS * PLANES + 3 * plane, GRAINS * PLANES + 3 * plane + 3)
-        top, bottom = solute_ref[plane, :3], solute_ref[plane, ROWS - 3 :]
-        inner_ref[row, :] = jnp.where(first_core, bottom, top)
-        outer_ref[row, :] = jnp.where(first_core, top, bottom)
-
-
-def call_first_sums(first, core, noise, ids, solute):
+
+
+def call_first_sums(first, core, noise, ids):
     width = 512
-    edge = GRAINS * PLANES + 3 * PLANES
+    edge = GRAINS * PLANES
     return pl.pallas_call(
         first_sums,
         grid=(COLS // width,),
         in_specs=[
             smem(),
             smem(),
-            pl.BlockSpec((GRAINS // 2, PLANES, ROWS, width), lambda i: (0, 0, 0, i)),
-            pl.BlockSpec((GRAINS // 2, PLANES, ROWS, width), lambda i: (1, 0, 0, i)),
-            pl.BlockSpec((PLANES, ROWS, width), lambda i: (0, 0, i)),
+            pl.BlockSpec((GRAINS, PLANES, ROWS, width), lambda i: (0, 0, 0, i)),
             pl.BlockSpec((PLANES, ROWS, width), lambda i: (0, 0, i)),
         ],
         out_specs=[
@@ -111,7 +104,7 @@
         ],
         compiler_params=params(60),
         name="first_sums",
-    )(first, core, noise, noise, ids, solute)
+    )(first, core, noise, ids)
 
 
 def factors(sums_ref, solute_ref, base_ref, slope_ref):
@@ -166,6 +159,10 @@
                 bulk_ref[plane, :, columns] = bulk
                 next_inner_ref[row : row + 2, columns] = jnp.where(first_core, bulk[ROWS - 2 :], bulk[:2])
                 next_outer_ref[row : row + 2, columns] = jnp.where(first_core, bulk[:2], bulk[ROWS - 2 :])
+            row = slice((GRAINS + 2 + plane) * PLANES, (GRAINS + 3 + plane) * PLANES)
+            top, bottom = solute_ref[plane, :3], solute_ref[plane, ROWS - 3 :]
+            next_inner_ref[row, :] = jnp.where(first_core, bottom, top)
+            next_outer_ref[row, :] = jnp.where(first_core, top, bottom)
 
     rate = time_step * mobility_ref[group_ref[grain]]
     planes = [
@@ -197,7 +194,7 @@
 
 
 def call_first_step(first, core, groups, mobility, noise, ids, solute, sums, inner, outer):
-    edge = GRAINS * PLANES + 2 * PLANES
+    edge = GRAINS * PLANES + 5 * PLANES
     grain_block = pl.BlockSpec((1, PLANES, ROWS, COLS), lambda i: (i, 0, 0, 0))
     return pl.pallas_call(
         first_step,
@@ -232,7 +229,7 @@
 
 
 def solute_step(
-    core_ref, solute_ref, middle_ref, inner_ref, outer_ref, mid_inner_ref, mid_outer_ref,
+    core_ref, solute_ref, middle_ref, inner_ref, outer_ref,
     out_ref, part_ref, ends_ref, deep_ref, bulk_ref,
 ):
     first_core = core_ref[0] == 0
@@ -244,13 +241,13 @@
         for ref in (deep_ref, bulk_ref):
             ref[plane, :PAD] = jnp.zeros((PAD, COLS), F32)
             ref[plane, PAD + ROWS :] = jnp.zeros((PAD, COLS), F32)
-        row = GRAINS * PLANES + 3 * plane
+        row = (GRAINS + 2 + plane) * PLANES
         above, below = sides(inner_ref[row : row + 3, :], outer_ref[row : row + 3, :])
         deep_ref[plane, PAD - 3 : PAD] = above
         deep_ref[plane, PAD : PAD + ROWS] = solute_ref[plane]
         deep_ref[plane, PAD + ROWS : PAD + ROWS + 3] = below
         row = GRAINS * PLANES + 2 * plane
-        above, below = sides(mid_inner_ref[row : row + 2, :], mid_outer_ref[row : row + 2, :])
+        above, below = sides(inner_ref[row : row + 2, :], outer_ref[row : row + 2, :])
         bulk_ref[plane, PAD - 2 : PAD] = above
         bulk_ref[plane, PAD + ROWS : PAD + ROWS + 2] = below
         bulk_ref[plane, PAD : PAD + ROWS] = middle_ref[plane]
@@ -275,7 +272,7 @@
     return pl.pallas_call(
         solute_step,
         in_specs=[smem()] + [whole(*array.shape) for array in arrays],
-        out_shape=[hbm(*solute.shape)] * 2 + [hbm(2 * PLANES, COLS)],
+        out_shape=[shape(*solute.shape)] * 2 + [shape(2 * PLANES, COLS)],
         scratch_shapes=[pltpu.VMEM((PLANES, DEEP, COLS), F32)] * 2,
         compiler_params=params(),
         name="solute_step",
@@ -335,7 +332,7 @@
         compiler_params=params(),
         cost_estimate=pl.CostEstimate(flops=20_000_000, bytes_accessed=10_000_000, transcendentals=0),
         name="second_step",
-    )(core, groups, mobility, eta, solute, sums, inner, outer)
+    )(core, groups, mobility, eta, solute, sums, *from_hbm(inner, outer))
 
 
 def solute_end(core_ref, solute_ref, part_ref, sums_ref, inner_ref, outer_ref, out_ref, potential_ref):
@@ -435,14 +432,13 @@
     count = lax.axis_size("yl") * lax.axis_size("z") * lax.axis_size("core")
     first = (lax.axis_index(GRAIN) * GRAINS).astype(jnp.int32).reshape(1)
     core = lax.axis_index("core").astype(jnp.int32).reshape(1)
-    sums, inner, outer = call_first_sums(first, core, seed_noise, grain_ids, concentration)
+    sums, inner, outer = call_first_sums(first, core, seed_noise, grain_ids)
     sums, (inner, outer) = total(sums, swapped(inner, outer, count))
-    eta, sums, mid_inner, mid_outer, bulk = call_first_step(
+    eta, sums, inner, outer, bulk = call_first_step(
         first, core, group_of, group_mobility, seed_noise, grain_ids, concentration, sums, inner, outer
     )
-    mid_inner, mid_outer = swapped(mid_inner, mid_outer, count)
-    later = call_solute_step(core, concentration, bulk, inner, outer, mid_inner, mid_outer)
-    sums, (mid_inner, mid_outer, solute, part, ends) = total(sums, (mid_inner, mid_outer, *later))
+    sums, (mid_inner, mid_outer) = total(sums, swapped(inner, outer, count))
+    solute, part, ends = call_solute_step(core, concentration, bulk, mid_inner, mid_outer)
     inner, outer = swapped(*call_end_rows(core, ends, sums), count)
     eta = call_second_step(core, group_of, group_mobility, eta, solute, sums, mid_inner, mid_outer)
     solute = call_solute_end(core, solute, part, sums, inner, outer)

time: 151 us -> 150 us (level)
  the two profiles are of different devices: /device:TPU:8 before, /device:TPU:2 now
where the time goes in v7:
time: 150 us
  blocking collectives  64.6 us (43%)
  starting transfers between devices  48.9 us (33%)
  Pallas kernels  19.9 us (13%)
  waiting for transfers between devices  12.5 us (8%)
  local copies, waits for them, and re-layouts  2.93 us (2%)
    all_to_all x5, blocking collectives, dealt(): return lax.all_to_all(blocks, axis, 0, 0, tiled=True)  64.6 us
    ppermute x3, starting transfers between devices, swapped(): lax.ppermute(outer, SPACE, [(i, (i + 2 * (i % 2) - 1) % count) for i in r...  23.9 us
    all_to_all x3, starting transfers between devices, dealt(): return lax.all_to_all(blocks, axis, 0, 0, tiled=True)  19.2 us
    ppermute x3, waiting for transfers between devices, swapped(): lax.ppermute(outer, SPACE, [(i, (i + 2 * (i % 2) - 1) % count) for i in r...  8.61 us
    pallas_call x1, Pallas kernels, call_first_step(): pl.pallas_call(first_step, grid=(GRAINS,), in_specs=[smem(), smem(), smem...  5.9 us
    ppermute x3, starting transfers between devices, swapped(): inner = lax.ppermute(inner, SPACE, [(i, i ^ 1) for i in range(count)])  5.74 us
    pallas_call x1, Pallas kernels, call_second_step(): pl.pallas_call(second_step, grid=(GRAINS,), in_specs=[smem(), smem(), sme...  4.99 us
    pallas_call x1, Pallas kernels, call_first_sums(): pl.pallas_call(first_sums, grid=(COLS // width,), in_specs=[smem(), smem(...  3.99 us
  transfers between devices with their start and end apart: 9, of which 3 were waited for; matrix products, arithmetic and copies ran while one was open for 0% of the time, Pallas kernels for 5%

profile of v7, /device:TPU:2, one launch (start us, length us, event | category | flops | bytes accessed | tf_op | source)
XLA Modules:
  0.0 149.6 jit_solution(16870073926864478984)
XLA Ops:
  0.6 4.0 %first_sums.1 = (f32[16,6,16,128]{3,2,1,0:T(8,128)}, f32[18,2048]{1,0:T(8,128)}, f32[18,2048]{1,0:T(8,128)}) custom-call(s32[1]{0:T(128)} %bitcast.1.first_ref, s32[1]{0:T(128)} %bitcast.core_ref, f32[6,3,16,2048]{3,2,1,0:T(8,128)} %noise_ref.3, s32[3,16,2048]{2,1,0:T(8,128)} %ids_ref.3), custom_call_target="tpu_custom_call" | custom-call | tf_op jit(solution)/shard_map/first_sums/pallas_call | solution.py:86
  4.6 9.4 %all-to-all-start = ((f32[4,4,6,16,128]{4,3,2,1,0:T(8,128)}), f32[4,4,6,16,128]{4,3,2,1,0:T(8,128)S(1)}, u32[]{:S(2)}, u32[]{:S(2)}) async-start(f32[4,4,6,16,128]{4,3,2,1,0:T(8,128)} %bitcast.10), calls=%async_computation | async-start | bytes 1572864 | tf_op jit(solution)/shard_map/all_to_all | solution.py:419
  14.0 1.9 %collective-permute-start = (f32[18,2048]{1,0:T(8,128)}, f32[18,2048]{1,0:T(8,128)S(1)}, u32[]{:S(2)}, u32[]{:S(2)}) collective-permute-start(f32[18,2048]{1,0:T(8,128)} %get-tuple-element.22), channel_id=1, source_target_pairs={{0,16},{16,0},{32,48},{48,32},{64,80},{80,64},{96,112},{112,96},{1... | collective-permute-start | bytes 442376 | tf_op jit(solution)/shard_map/ppermute | solution.py:368
  15.9 0.0 copy-start
  15.9 0.0 copy-start.2
  15.9 0.0 copy-start.8
  15.9 0.0 copy-start.9
  16.0 7.8 %collective-permute-start.1 = (f32[18,2048]{1,0:T(8,128)}, f32[18,2048]{1,0:T(8,128)}, u32[]{:S(2)}, u32[]{:S(2)}) collective-permute-start(f32[18,2048]{1,0:T(8,128)} %get-tuple-element.23), channel_id=1, source_target_pairs={{0,496},{16,32},{32,16},{48,64},{64,48},{80,96},{96,80},{112,128},... | collective-permute-start | bytes 442376 | tf_op jit(solution)/shard_map/ppermute | solution.py:369
  23.8 0.0 collective-permute-done.inner_ref
  23.8 0.0 copy-start.12
  23.8 0.7 copy-done.12
  24.4 3.0 %collective-permute-done.1.outer_ref = f32[18,2048]{1,0:T(8,128)} collective-permute-done((f32[18,2048]{1,0:T(8,128)}, f32[18,2048]{1,0:T(8,128)}, u32[]{:S(2)}, u32[]{:S(2)}) %collective-permute-start.1) | collective-permute-done | bytes 147488 | tf_op jit(solution)/shard_map/ppermute | solution.py:369
  27.4 0.0 all-to-all-done.parts_ref
  27.5 15.8 %all_to_all.40.parts_ref = f32[4,6,16,128]{3,2,1,0:T(8,128)S(1)} all-to-all(f32[4,6,16,128]{3,2,1,0:T(8,128)S(1)} %add_parts.2), channel_id=1, replica_groups=mesh['yl'=2,'z'=8,'core'=2,'x'=4,'yh'=4] {'yh'}, dimensions={0} | all-to-all | bytes 393216 | tf_op jit(solution)/shard_map/all_to_all | solution.py:419
  43.3 12.2 %all_to_all.41.value_ref = f32[4,6,16,128]{3,2,1,0:T(8,128)S(1)} all-to-all(f32[4,6,16,128]{3,2,1,0:T(8,128)S(1)} %owner.2), channel_id=1, replica_groups=mesh['yl'=2,'z'=8,'core'=2,'x'=4,'yh'=4] {'yh'}, dimensions={0} | all-to-all | bytes 393216 | tf_op jit(solution)/shard_map/all_to_all | solution.py:419
  55.4 0.1 copies.2
  55.5 12.4 %all_to_all.42 = f32[4,4,6,16,128]{4,3,2,1,0:T(8,128)S(1)} all-to-all(f32[4,4,6,16,128]{4,3,2,1,0:T(8,128)S(1)} %copies.2), channel_id=1, replica_groups=mesh['yl'=2,'z'=8,'core'=2,'x'=4,'yh'=4] {'x'}, dimensions={0} | all-to-all | bytes 1572864 | tf_op jit(solution)/shard_map/all_to_all | solution.py:419
  67.9 0.0 copy-done
  67.9 0.0 copy-done.2
  68.0 0.0 copy-done.8
  68.0 0.0 copy-done.9
  68.0 5.9 %first_step.1 = (f32[6,3,16,2048]{3,2,1,0:T(8,128)}, f32[16,6,16,128]{3,2,1,0:T(8,128)}, f32[33,2048]{1,0:T(8,128)S(1)}, f32[33,2048]{1,0:T(8,128)S(1)}, f32[3,16,2048]{2,1,0:T(8,128)}) custom-call(s32[1]{0:T(128)} %bitcast.1.first_ref, s32[1]{0:T(128)} %bitcast.core_ref, s32[6]{0:T(128)S(1)} %copy-done.8, f32[4]{0:T(128)S(1)} %copy-done.9, ...), custom_call_target="tpu_custom_call" | custom-call | tf_op jit(solution)/shard_map/first_step/pallas_call | solution.py:199
  73.9 4.9 %all-to-all-start.4 = ((f32[4,4,6,16,128]{4,3,2,1,0:T(8,128)}), f32[4,4,6,16,128]{4,3,2,1,0:T(8,128)S(1)}, u32[]{:S(2)}, u32[]{:S(2)}) async-start(f32[4,4,6,16,128]{4,3,2,1,0:T(8,128)} %bitcast.4), calls=%async_computation.4 | async-start | bytes 1572864 | tf_op jit(solution)/shard_map/all_to_all | solution.py:419
  78.8 1.9 %collective-permute-start.2 = (f32[33,2048]{1,0:T(8,128)S(1)}, f32[33,2048]{1,0:T(8,128)S(1)}, u32[]{:S(2)}, u32[]{:S(2)}) collective-permute-start(f32[33,2048]{1,0:T(8,128)S(1)} %get-tuple-element.30), channel_id=1, source_target_pairs={{0,16},{16,0},{32,48},{48,32},{64,80},{80,64},{96,112},{112,96},{1... | collective-permute-start | bytes 811016 | tf_op jit(solution)/shard_map/ppermute | solution.py:368
  80.7 9.4 %collective-permute-start.3 = (f32[33,2048]{1,0:T(8,128)S(1)}, f32[33,2048]{1,0:T(8,128)S(1)}, u32[]{:S(2)}, u32[]{:S(2)}) collective-permute-start(f32[33,2048]{1,0:T(8,128)S(1)} %get-tuple-element.31), channel_id=1, source_target_pairs={{0,496},{16,32},{32,16},{48,64},{64,48},{80,96},{96,80},{112,128},... | collective-permute-start | bytes 811016 | tf_op jit(solution)/shard_map/ppermute | solution.py:369
  90.1 0.0 collective-permute-done.2.inner_ref
  90.2 5.6 %collective-permute-done.3.outer_ref = f32[33,2048]{1,0:T(8,128)S(1)} collective-permute-done((f32[33,2048]{1,0:T(8,128)S(1)}, f32[33,2048]{1,0:T(8,128)S(1)}, u32[]{:S(2)}, u32[]{:S(2)}) %collective-permute-start.3) | collective-permute-done | bytes 270368 | tf_op jit(solution)/shard_map/ppermute | solution.py:369
  95.8 0.0 all-to-all-done.4.parts_ref
  95.9 12.5 %all_to_all.43.parts_ref = f32[4,6,16,128]{3,2,1,0:T(8,128)S(1)} all-to-all(f32[4,6,16,128]{3,2,1,0:T(8,128)S(1)} %add_parts.3), channel_id=1, replica_groups=mesh['yl'=2,'z'=8,'core'=2,'x'=4,'yh'=4] {'yh'}, dimensions={0} | all-to-all | bytes 393216 | tf_op jit(solution)/shard_map/all_to_all | solution.py:419
  108.3 0.0 copy-done.10
  108.3 0.0 copy-done.11
  108.3 11.7 %all_to_all.44.value_ref = f32[4,6,16,128]{3,2,1,0:T(8,128)S(1)} all-to-all(f32[4,6,16,128]{3,2,1,0:T(8,128)S(1)} %owner.3), channel_id=1, replica_groups=mesh['yl'=2,'z'=8,'core'=2,'x'=4,'yh'=4] {'yh'}, dimensions={0} | all-to-all | bytes 393216 | tf_op jit(solution)/shard_map/all_to_all | solution.py:419
  120.1 0.9 copies.3
  121.0 4.9 %all-to-all-start.7 = ((f32[4,4,6,16,128]{4,3,2,1,0:T(8,128)}), f32[4,4,6,16,128]{4,3,2,1,0:T(8,128)S(1)}, u32[]{:S(2)}, u32[]{:S(2)}) async-start(f32[4,4,6,16,128]{4,3,2,1,0:T(8,128)} %copies.3), calls=%async_computation.7 | async-start | bytes 1572864 | tf_op jit(solution)/shard_map/all_to_all | solution.py:419
  125.9 2.8 %solute_step.1 = (f32[3,16,2048]{2,1,0:T(8,128)S(1)}, f32[3,16,2048]{2,1,0:T(8,128)S(1)}, f32[6,2048]{1,0:T(8,128)S(1)}) custom-call(s32[1]{0:T(128)} %bitcast.core_ref, f32[3,16,2048]{2,1,0:T(8,128)} %solute_ref.3, f32[3,16,2048]{2,1,0:T(8,128)} %get-tuple-element.28.middle_ref, f32[33,2048]{1,0:T(8,128)} %copy-done.10, f32[33,2048]{1,0:T(8,128)} %copy-done.11), custom_call_target="tpu_custom_call" | custom-call | tf_op jit(solution)/shard_map/solute_step/pallas_call | solution.py:272
  128.7 0.0 copy-start.4
  128.8 0.7 copy-done.4
  129.5 0.6 copy-done.6
  130.1 3.8 %all-to-all-done.7 = f32[4,4,6,16,128]{4,3,2,1,0:T(8,128)S(1)} async-done(((f32[4,4,6,16,128]{4,3,2,1,0:T(8,128)}), f32[4,4,6,16,128]{4,3,2,1,0:T(8,128)S(1)}, u32[]{:S(2)}, u32[]{:S(2)}) %all-to-all-start.7) | async-done | bytes 786464 | tf_op jit(solution)/shard_map/all_to_all | solution.py:419
  134.0 0.8 copy-done.7
  134.8 0.1 end_rows.1
  134.9 1.9 %collective-permute-start.4 = (f32[3,2048]{1,0:T(4,128)S(1)}, f32[3,2048]{1,0:T(4,128)S(1)}, u32[]{:S(2)}, u32[]{:S(2)}) collective-permute-start(f32[3,2048]{1,0:T(4,128)S(1)} %get-tuple-element.38), channel_id=1, source_target_pairs={{0,16},{16,0},{32,48},{48,32},{64,80},{80,64},{96,112},{112,96},{1... | collective-permute-start | bytes 73736 | tf_op jit(solution)/shard_map/ppermute | solution.py:368
  136.8 6.7 %collective-permute-start.5 = (f32[3,2048]{1,0:T(4,128)S(1)}, f32[3,2048]{1,0:T(4,128)S(1)}, u32[]{:S(2)}, u32[]{:S(2)}) collective-permute-start(f32[3,2048]{1,0:T(4,128)S(1)} %get-tuple-element.39), channel_id=1, source_target_pairs={{0,496},{16,32},{32,16},{48,64},{64,48},{80,96},{96,80},{112,128},... | collective-permute-start | bytes 73736 | tf_op jit(solution)/shard_map/ppermute | solution.py:369
  143.5 0.0 copy-start.5
  143.5 5.0 %second_step.1 = f32[6,3,16,2048]{3,2,1,0:T(8,128)} custom-call(s32[1]{0:T(128)} %bitcast.core_ref, s32[6]{0:T(128)S(1)} %copy-done.8, f32[4]{0:T(128)S(1)} %copy-done.9, f32[6,3,16,2048]{3,2,1,0:T(8,128)S(1)} %copy-done.1, f32[3,16,2048]{2,1,0:T(8,128)S(1)} %get-tuple-element.34.solute_ref, f32[16,6,16,128]{3,2,1,0:T(8,128)S(1)} %bitcast.7, ...), custom_call_target="tpu_custom_call" | custom-call | flops 20000000 | bytes 10000000 | tf_op jit(solution)/shard_map/second_step/pallas_call | solution.py:322
  148.5 0.0 collective-permute-done.4.inner_ref
  148.5 0.0 collective-permute-done.5.outer_ref
  148.6 1.1 solute_end.1
  (13 shorter events, 0.1 us)
Async XLA Ops:
  4.6 22.8 %all-to-all-start = ((f32[4,4,6,16,128]{4,3,2,1,0:T(8,128)}), f32[4,4,6,16,128]{4,3,2,1,0:T(8,128)S(1)}, u32[]{:S(2)}, u32[]{:S(2)}) async-start(f32[4,4,6,16,128]{4,3,2,1,0:T(8,128)} %bitcast.10), calls=%async_computation | async-start | bytes 1572864 | tf_op jit(solution)/shard_map/all_to_all | solution.py:419
  14.0 9.8 %collective-permute-start = (f32[18,2048]{1,0:T(8,128)}, f32[18,2048]{1,0:T(8,128)S(1)}, u32[]{:S(2)}, u32[]{:S(2)}) collective-permute-start(f32[18,2048]{1,0:T(8,128)} %get-tuple-element.22), channel_id=1, source_target_pairs={{0,16},{16,0},{32,48},{48,32},{64,80},{80,64},{96,112},{112,96},{1... | collective-permute-start | bytes 442376 | tf_op jit(solution)/shard_map/ppermute | solution.py:368
  15.9 52.0 %copy-start = (f32[6,3,16,2048]{3,2,1,0:T(8,128)S(1)}, f32[6,3,16,2048]{3,2,1,0:T(8,128)}, u32[]{:S(2)}) copy-start(f32[6,3,16,2048]{3,2,1,0:T(8,128)} %noise_ref.3) | copy-start | bytes 7077892
  15.9 52.0 %copy-start.2 = (s32[3,16,2048]{2,1,0:T(8,128)S(1)}, s32[3,16,2048]{2,1,0:T(8,128)}, u32[]{:S(2)}) copy-start(s32[3,16,2048]{2,1,0:T(8,128)} %ids_ref.3) | copy-start | bytes 1179652
  15.9 52.0 %copy-start.8 = (s32[6]{0:T(128)S(1)}, s32[6]{0:T(128)}, u32[]{:S(2)}) copy-start(s32[6]{0:T(128)} %group_ref.3) | copy-start | bytes 76
  15.9 52.0 %copy-start.9 = (f32[4]{0:T(128)S(1)}, f32[4]{0:T(128)}, u32[]{:S(2)}) copy-start(f32[4]{0:T(128)} %mobility_ref.3) | copy-start | bytes 52
  16.0 11.4 %collective-permute-start.1 = (f32[18,2048]{1,0:T(8,128)}, f32[18,2048]{1,0:T(8,128)}, u32[]{:S(2)}, u32[]{:S(2)}) collective-permute-start(f32[18,2048]{1,0:T(8,128)} %get-tuple-element.23), channel_id=1, source_target_pairs={{0,496},{16,32},{32,16},{48,64},{64,48},{80,96},{96,80},{112,128},... | collective-permute-start | bytes 442376 | tf_op jit(solution)/shard_map/ppermute | solution.py:369
  23.8 0.7 copy-start.12
  27.4 40.6 %copy-start.3 = (f32[3,16,2048]{2,1,0:T(8,128)S(1)}, f32[3,16,2048]{2,1,0:T(8,128)}, u32[]{:S(2)}) copy-start(f32[3,16,2048]{2,1,0:T(8,128)} %solute_ref.3) | copy-start | bytes 1179652
  73.9 21.9 %all-to-all-start.4 = ((f32[4,4,6,16,128]{4,3,2,1,0:T(8,128)}), f32[4,4,6,16,128]{4,3,2,1,0:T(8,128)S(1)}, u32[]{:S(2)}, u32[]{:S(2)}) async-start(f32[4,4,6,16,128]{4,3,2,1,0:T(8,128)} %bitcast.4), calls=%async_computation.4 | async-start | bytes 1572864 | tf_op jit(solution)/shard_map/all_to_all | solution.py:419
  78.8 11.3 %collective-permute-start.2 = (f32[33,2048]{1,0:T(8,128)S(1)}, f32[33,2048]{1,0:T(8,128)S(1)}, u32[]{:S(2)}, u32[]{:S(2)}) collective-permute-start(f32[33,2048]{1,0:T(8,128)S(1)} %get-tuple-element.30), channel_id=1, source_target_pairs={{0,16},{16,0},{32,48},{48,32},{64,80},{80,64},{96,112},{112,96},{1... | collective-permute-start | bytes 811016 | tf_op jit(solution)/shard_map/ppermute | solution.py:368
  80.7 15.1 %collective-permute-start.3 = (f32[33,2048]{1,0:T(8,128)S(1)}, f32[33,2048]{1,0:T(8,128)S(1)}, u32[]{:S(2)}, u32[]{:S(2)}) collective-permute-start(f32[33,2048]{1,0:T(8,128)S(1)} %get-tuple-element.31), channel_id=1, source_target_pairs={{0,496},{16,32},{32,16},{48,64},{64,48},{80,96},{96,80},{112,128},... | collective-permute-start | bytes 811016 | tf_op jit(solution)/shard_map/ppermute | solution.py:369
  90.1 18.2 %copy-start.10 = (f32[33,2048]{1,0:T(8,128)}, f32[33,2048]{1,0:T(8,128)S(1)}, u32[]{:S(2)}) copy-start(f32[33,2048]{1,0:T(8,128)S(1)} %collective-permute-done.2.inner_ref) | copy-start | bytes 811012
  95.8 12.5 %copy-start.11 = (f32[33,2048]{1,0:T(8,128)}, f32[33,2048]{1,0:T(8,128)S(1)}, u32[]{:S(2)}) copy-start(f32[33,2048]{1,0:T(8,128)S(1)} %collective-permute-done.3.outer_ref) | copy-start | bytes 811012
  120.1 23.5 %copy-start.1 = (f32[6,3,16,2048]{3,2,1,0:T(8,128)S(1)}, f32[6,3,16,2048]{3,2,1,0:T(8,128)}, u32[]{:S(2)}) copy-start(f32[6,3,16,2048]{3,2,1,0:T(8,128)} %get-tuple-element.27.old_ref) | copy-start | bytes 7077892
  121.0 13.0 %all-to-all-start.7 = ((f32[4,4,6,16,128]{4,3,2,1,0:T(8,128)}), f32[4,4,6,16,128]{4,3,2,1,0:T(8,128)S(1)}, u32[]{:S(2)}, u32[]{:S(2)}) async-start(f32[4,4,6,16,128]{4,3,2,1,0:T(8,128)} %copies.3), calls=%async_computation.7 | async-start | bytes 1572864 | tf_op jit(solution)/shard_map/all_to_all | solution.py:419
  128.7 0.7 copy-start.4
  129.5 0.6 copy-start.6
  134.0 0.8 copy-start.7
  134.9 13.7 %collective-permute-start.4 = (f32[3,2048]{1,0:T(4,128)S(1)}, f32[3,2048]{1,0:T(4,128)S(1)}, u32[]{:S(2)}, u32[]{:S(2)}) collective-permute-start(f32[3,2048]{1,0:T(4,128)S(1)} %get-tuple-element.38), channel_id=1, source_target_pairs={{0,16},{16,0},{32,48},{48,32},{64,80},{80,64},{96,112},{112,96},{1... | collective-permute-start | bytes 73736 | tf_op jit(solution)/shard_map/ppermute | solution.py:368
  136.8 11.7 %collective-permute-start.5 = (f32[3,2048]{1,0:T(4,128)S(1)}, f32[3,2048]{1,0:T(4,128)S(1)}, u32[]{:S(2)}, u32[]{:S(2)}) collective-permute-start(f32[3,2048]{1,0:T(4,128)S(1)} %get-tuple-element.39), channel_id=1, source_target_pairs={{0,496},{16,32},{32,16},{48,64},{64,48},{80,96},{96,80},{112,128},... | collective-permute-start | bytes 73736 | tf_op jit(solution)/shard_map/ppermute | solution.py:369
  143.5 5.0 %copy-start.5 = (f32[3,16,2048]{2,1,0:T(8,128)S(1)}, f32[3,16,2048]{2,1,0:T(8,128)}, u32[]{:S(2)}) copy-start(f32[3,16,2048]{2,1,0:T(8,128)} %copy-done.4) | copy-start | bytes 1179652

commit v8 on v5

--- a/solution.py
+++ b/solution.py
@@ -139,7 +139,7 @@
 
 def first_step(
     first_ref, group_ref, mobility_ref, noise_ref, ids_ref, solute_ref, sums_ref, above_ref, below_ref,
-    eta_ref, next_sums_ref, next_ref, prev_ref, bulk_ref, base_ref, slope_ref,
+    eta_ref, next_sums_ref, next_ref, prev_ref, bulk_ref, rows_above_ref, rows_below_ref, base_ref, slope_ref,
 ):
     grain = pl.program_id(0)
 
@@ -154,6 +154,8 @@
                 bulk_ref[plane, :, columns] = bulk
                 prev_ref[row : row + 2, columns] = bulk[:2]
                 next_ref[row : row + 2, columns] = bulk[ROWS - 2 :]
+        rows_above_ref[...] = above_ref[GRAINS * PLANES :]
+        rows_below_ref[...] = below_ref[GRAINS * PLANES :]
 
     rate = time_step * mobility_ref[group_ref[grain]]
     planes = [
@@ -197,14 +199,16 @@
         ],
         out_specs=[grain_block, whole(*sums.shape)]
         + [whole(edge, COLS)] * 2
-        + [whole(*solute.shape)],
+        + [whole(*solute.shape)]
+        + [whole(3 * PLANES, COLS)] * 2,
         out_shape=[hbm(*noise.shape), shape(*sums.shape)]
         + [shape(edge, COLS)] * 2
-        + [hbm(*solute.shape)],
+        + [hbm(*solute.shape)]
+        + [hbm(3 * PLANES, COLS)] * 2,
         scratch_shapes=[pltpu.VMEM(solute.shape, F32)] * 2,
         compiler_params=params(),
         name="first_step",
-    )(first, groups, mobility, *from_hbm(noise, ids, solute), sums, *from_hbm(above, below))
+    )(first, groups, mobility, noise, ids, solute, sums, above, below)
 
 
 PAD = 8
@@ -227,7 +231,7 @@
         for ref in (deep_ref, bulk_ref):
             ref[plane, :PAD] = jnp.zeros((PAD, COLS), F32)
             ref[plane, PAD + ROWS :] = jnp.zeros((PAD, COLS), F32)
-        row = GRAINS * PLANES + 3 * plane
+        row = 3 * plane
         deep_ref[plane, PAD - 3 : PAD] = above_ref[row : row + 3, :]
         deep_ref[plane, PAD : PAD + ROWS] = solute_ref[plane]
         deep_ref[plane, PAD + ROWS : PAD + ROWS + 3] = below_ref[row : row + 3, :]
@@ -254,11 +258,11 @@
 def call_solute_step(solute, bulk, above, below, mid_above, mid_below):
     return pl.pallas_call(
         solute_step,
-        out_shape=[hbm(*solute.shape)] * 2 + [hbm(2 * PLANES, COLS)],
+        out_shape=[shape(*solute.shape)] * 2 + [hbm(2 * PLANES, COLS)],
         scratch_shapes=[pltpu.VMEM((PLANES, DEEP, COLS), F32)] * 2,
         compiler_params=params(),
         name="solute_step",
-    )(*from_hbm(solute, bulk, above, below, mid_above, mid_below))
+    )(solute, bulk, above, below, mid_above, mid_below)
 
 
 def end_rows(core_ref, ends_ref, sums_ref, inner_ref, outer_ref):
@@ -280,7 +284,7 @@
         out_shape=[shape(PLANES, COLS)] * 2,
         compiler_params=params(),
         name="end_rows",
-    )(core, ends, sums)
+    )(core, *from_hbm(ends), sums)
 
 
 def second_step(
@@ -314,7 +318,7 @@
         compiler_params=params(),
         cost_estimate=pl.CostEstimate(flops=20_000_000, bytes_accessed=10_000_000, transcendentals=0),
         name="second_step",
-    )(groups, mobility, *from_hbm(eta, solute), sums, *from_hbm(above, below))
+    )(groups, mobility, eta, solute, sums, above, below)
 
 
 def solute_end(core_ref, solute_ref, part_ref, sums_ref, inner_ref, outer_ref, out_ref, potential_ref):
@@ -347,8 +351,8 @@
 
 
 def swapped(inner, outer, count):
+    outer = lax.ppermute(outer, SPACE, [(i, (i + 2 * (i % 2) - 1) % count) for i in range(count)])
     inner = lax.ppermute(inner, SPACE, [(i, i ^ 1) for i in range(count)])
-    outer = lax.ppermute(outer, SPACE, [(i, (i + 2 * (i % 2) - 1) % count) for i in range(count)])
     return inner, outer
 
 
@@ -388,33 +392,46 @@
 
 def call_owner(parts):
     return pl.pallas_call(
-        owner, out_shape=hbm(BLOCKS, *parts.shape[1:]), compiler_params=params(), name="owner"
+        owner, out_shape=shape(*parts.shape), compiler_params=params(), name="owner"
     )(parts)
+
+
+def copies(value_ref, out_ref):
+    for copy in range(out_ref.shape[0]):
+        out_ref[copy] = value_ref[...]
+
+
+def call_copies(value, count):
+    return pl.pallas_call(
+        copies, out_shape=shape(count, *value.shape), compiler_params=params(), name="copies"
+    )(value)
 
 
 def dealt(blocks, axis):
     return lax.all_to_all(blocks, axis, 0, 0, tiled=True)
 
 
-def total(sums):
+def total(sums, to_next, to_prev):
+    count = lax.axis_size("yl") * lax.axis_size("z") * lax.axis_size("core")
     along = lax.axis_size("x")
     parts = dealt(sums.reshape((along, BLOCKS // along) + sums.shape[1:]), "x")
+    parts, above, below = lax.optimization_barrier((parts, *exchange(to_next, to_prev, count)))
     parts = dealt(call_add_parts(parts), "yh")
-    return dealt(call_owner(parts), GRAIN)
+    parts = dealt(call_owner(parts), "yh")
+    return dealt(call_copies(parts, along), "x").reshape(sums.shape), above, below
 
 
 def shards(grain_ids, group_of, group_mobility, seed_noise, concentration):
     count = lax.axis_size("yl") * lax.axis_size("z") * lax.axis_size("core")
     first = (lax.axis_index(GRAIN) * GRAINS).astype(jnp.int32).reshape(1)
+    sums, to_next, to_prev = call_first_sums(first, seed_noise, grain_ids, concentration)
+    sums, above, below = total(sums, to_next, to_prev)
+    eta, sums, to_next, to_prev, bulk, rows_above, rows_below = call_first_step(
+        first, group_of, group_mobility, seed_noise, grain_ids, concentration, sums, above, below
+    )
+    sums, mid_above, mid_below = total(sums, to_next, to_prev)
+    solute, part, ends = call_solute_step(concentration, bulk, rows_above, rows_below, mid_above, mid_below)
     core = lax.axis_index("core").astype(jnp.int32).reshape(1)
-    sums, to_next, to_prev = call_first_sums(first, seed_noise, grain_ids, concentration)
-    above, below = exchange(to_next, to_prev, count)
-    eta, sums, to_next, to_prev, bulk = call_first_step(
-        first, group_of, group_mobility, seed_noise, grain_ids, concentration, total(sums), above, below
-    )
-    mid_above, mid_below = exchange(to_next, to_prev, count)
-    sums = total(sums)
-    solute, part, ends = call_solute_step(concentration, bulk, above, below, mid_above, mid_below)
     inner, outer = swapped(*call_end_rows(core, ends, sums), count)
     eta = call_second_step(group_of, group_mobility, eta, solute, sums, mid_above, mid_below)
     solute = call_solute_end(core, solute, part, sums, inner, outer)

time: 151 us -> 147 us (0.974)
  starting transfers between devices: 58.2 us -> 50.3 us
  blocking collectives: 52.6 us -> 58.5 us
  Pallas kernels: 23.7 us -> 18.9 us
  local copies, waits for them, and re-layouts: 1.54 us -> 3.12 us
    ppermute x2, starting transfers between devices: 15.7 us -> 6.85 us  [exchange(): lax.ppermute(to_prev, SPACE, [((i + 1) % count, i) for i in range(count)])]
    ppermute x1, starting transfers between devices: 16.1 us -> 8.08 us  [swapped(): inner = lax.ppermute(inner, SPACE, [(i, i ^ 1) for i in range(count)])]
    all_to_all x4 -> x5, blocking collectives: 52.6 us -> 58.5 us  [dealt(): return lax.all_to_all(blocks, axis, 0, 0, tiled=True)]
    all_to_all x2 -> x3, starting transfers between devices: 7.23 us -> 12.8 us  [dealt(): return lax.all_to_all(blocks, axis, 0, 0, tiled=True)]
    ppermute x1, starting transfers between devices: 1.92 us -> 6.12 us  [swapped(): lax.ppermute(outer, SPACE, [(i, (i + 2 * (i % 2) - 1) % count) for i in r...]
    pallas_call x3 -> x5, Pallas kernels: 5.53 us -> 3.19 us  [the longest x1 2.16 us: call_solute_step(): pl.pallas_call(solute_step, out_shape=[shape(*solute.shape)] * 2 + [hbm(2...]
    ppermute x2, waiting for transfers between devices: 5.72 us -> 7.79 us  [exchange(): lax.ppermute(to_prev, SPACE, [((i + 1) % count, i) for i in range(count)])]
    pallas_call x1, Pallas kernels: 6.13 us -> 4.21 us  [call_second_step(): pl.pallas_call(second_step, grid=(GRAINS,), in_specs=[smem(), smem(), gra...]
  transfers between devices with their start and end apart: 8 -> 9, of which waited for: 4 -> 4; matrix products, arithmetic and copies ran while one was open for 0% -> 0% of each run, Pallas kernels for 6% -> 4%
where the time goes in v8:
time: 147 us; the launch traced here: 146 us
  blocking collectives  58.5 us (40%)
  starting transfers between devices  50.3 us (34%)
  Pallas kernels  18.9 us (13%)
  waiting for transfers between devices  14.5 us (10%)
  local copies, waits for them, and re-layouts  3.12 us (2%)
    all_to_all x5, blocking collectives, dealt(): return lax.all_to_all(blocks, axis, 0, 0, tiled=True)  58.5 us
    ppermute x2, starting transfers between devices, exchange(): lax.ppermute(to_next, SPACE, [(i, (i + 1) % count) for i in range(count)])  16.4 us
    all_to_all x3, starting transfers between devices, dealt(): return lax.all_to_all(blocks, axis, 0, 0, tiled=True)  12.8 us
    ppermute x1, starting transfers between devices, swapped(): inner = lax.ppermute(inner, SPACE, [(i, i ^ 1) for i in range(count)])  8.08 us
    ppermute x2, waiting for transfers between devices, exchange(): lax.ppermute(to_prev, SPACE, [((i + 1) % count, i) for i in range(count)])  7.79 us
    ppermute x2, starting transfers between devices, exchange(): lax.ppermute(to_prev, SPACE, [((i + 1) % count, i) for i in range(count)])  6.85 us
    all_to_all x3, waiting for transfers between devices, dealt(): return lax.all_to_all(blocks, axis, 0, 0, tiled=True)  6.17 us
    ppermute x1, starting transfers between devices, swapped(): lax.ppermute(outer, SPACE, [(i, (i + 2 * (i % 2) - 1) % count) for i in r...  6.12 us
  transfers between devices with their start and end apart: 9, of which 4 were waited for; matrix products, arithmetic and copies ran while one was open for 0% of the time, Pallas kernels for 4%

profile of v8, /device:TPU:1, one launch (start us, length us, event | category | flops | bytes accessed | tf_op | source)
XLA Modules:
  0.0 146.1 jit_solution(4234685066360930531)
XLA Ops:
  0.6 4.0 %first_sums.1 = (f32[16,6,16,128]{3,2,1,0:T(8,128)}, f32[27,2048]{1,0:T(8,128)}, f32[27,2048]{1,0:T(8,128)}) custom-call(s32[1]{0:T(128)} %bitcast.first_ref, f32[6,3,16,2048]{3,2,1,0:T(8,128)} %noise_ref.3, s32[3,16,2048]{2,1,0:T(8,128)} %ids_ref.3, f32[3,16,2048]{2,1,0:T(8,128)} %solute_ref.5), custom_call_target="tpu_custom_call" | custom-call | tf_op jit(solution)/shard_map/first_sums/pallas_call | solution.py:88
  4.6 4.8 %all-to-all-start = ((f32[4,4,6,16,128]{4,3,2,1,0:T(8,128)}), f32[4,4,6,16,128]{4,3,2,1,0:T(8,128)S(1)}, u32[]{:S(2)}, u32[]{:S(2)}) async-start(f32[4,4,6,16,128]{4,3,2,1,0:T(8,128)} %bitcast.10), calls=%async_computation | async-start | bytes 1572864 | tf_op jit(solution)/shard_map/all_to_all | solution.py:411
  9.5 4.8 %collective-permute-start = (f32[27,2048]{1,0:T(8,128)}, f32[27,2048]{1,0:T(8,128)S(1)}, u32[]{:S(2)}, u32[]{:S(2)}) collective-permute-start(f32[27,2048]{1,0:T(8,128)} %get-tuple-element.24), channel_id=1, source_target_pairs={{0,16},{16,32},{32,48},{48,64},{64,80},{80,96},{96,112},{112,128},... | collective-permute-start | bytes 663560 | tf_op jit(solution)/shard_map/ppermute | solution.py:360
  14.3 0.0 copy-start
  14.3 0.0 copy-start.1
  14.3 0.0 copy-start.11
  14.4 0.0 copy-start.12
  14.4 4.8 %collective-permute-start.1 = (f32[27,2048]{1,0:T(8,128)}, f32[27,2048]{1,0:T(8,128)S(1)}, u32[]{:S(2)}, u32[]{:S(2)}) collective-permute-start(f32[27,2048]{1,0:T(8,128)} %get-tuple-element.25), channel_id=1, source_target_pairs={{16,0},{32,16},{48,32},{64,48},{80,64},{96,80},{112,96},{128,112},... | collective-permute-start | bytes 663560 | tf_op jit(solution)/shard_map/ppermute | solution.py:361
  19.2 0.0 collective-permute-done.above_ref
  19.2 0.0 copy-start.5
  19.2 0.7 copy-done.5
  19.9 2.9 %collective-permute-done.1.below_ref = f32[27,2048]{1,0:T(8,128)S(1)} collective-permute-done((f32[27,2048]{1,0:T(8,128)}, f32[27,2048]{1,0:T(8,128)S(1)}, u32[]{:S(2)}, u32[]{:S(2)}) %collective-permute-start.1) | collective-permute-done | bytes 221216 | tf_op jit(solution)/shard_map/ppermute | solution.py:361
  22.8 0.7 copy-done.7
  23.5 0.0 all-to-all-done.parts_ref
  23.6 14.7 %all_to_all.40.parts_ref = f32[4,6,16,128]{3,2,1,0:T(8,128)S(1)} all-to-all(f32[4,6,16,128]{3,2,1,0:T(8,128)S(1)} %add_parts.2), channel_id=1, replica_groups=mesh['yl'=2,'z'=8,'core'=2,'x'=4,'yh'=4] {'yh'}, dimensions={0} | all-to-all | bytes 393216 | tf_op jit(solution)/shard_map/all_to_all | solution.py:411
  38.3 10.4 %all_to_all.41.value_ref = f32[4,6,16,128]{3,2,1,0:T(8,128)S(1)} all-to-all(f32[4,6,16,128]{3,2,1,0:T(8,128)S(1)} %owner.2), channel_id=1, replica_groups=mesh['yl'=2,'z'=8,'core'=2,'x'=4,'yh'=4] {'yh'}, dimensions={0} | all-to-all | bytes 393216 | tf_op jit(solution)/shard_map/all_to_all | solution.py:411
  48.7 0.1 copies.2
  48.7 12.7 %all_to_all.42 = f32[4,4,6,16,128]{4,3,2,1,0:T(8,128)S(1)} all-to-all(f32[4,4,6,16,128]{4,3,2,1,0:T(8,128)S(1)} %copies.2), channel_id=1, replica_groups=mesh['yl'=2,'z'=8,'core'=2,'x'=4,'yh'=4] {'x'}, dimensions={0} | all-to-all | bytes 1572864 | tf_op jit(solution)/shard_map/all_to_all | solution.py:411
  61.4 0.0 copy-done
  61.4 0.0 copy-done.1
  61.4 0.0 copy-done.11
  61.4 0.0 copy-done.12
  61.4 0.0 copy-done.3
  61.4 0.0 copy-done.6
  61.5 0.0 copy-done.8
  61.5 5.4 %first_step.1 = (f32[6,3,16,2048]{3,2,1,0:T(8,128)}, f32[16,6,16,128]{3,2,1,0:T(8,128)}, f32[24,2048]{1,0:T(8,128)S(1)}, f32[24,2048]{1,0:T(8,128)S(1)}, f32[3,1...) custom-call(s32[1]{0:T(128)} %bitcast.first_ref, s32[6]{0:T(128)S(1)} %copy-done.11, f32[4]{0:T(128)S(1)} %copy-done.12, ...), custom_call_target="tpu_custom_call" | custom-call | tf_op jit(solution)/shard_map/first_step/pallas_call | solution.py:192
  66.9 3.5 %all-to-all-start.4 = ((f32[4,4,6,16,128]{4,3,2,1,0:T(8,128)}), f32[4,4,6,16,128]{4,3,2,1,0:T(8,128)S(1)}, u32[]{:S(2)}, u32[]{:S(2)}) async-start(f32[4,4,6,16,128]{4,3,2,1,0:T(8,128)} %bitcast.3), calls=%async_computation.4 | async-start | bytes 1572864 | tf_op jit(solution)/shard_map/all_to_all | solution.py:411
  70.4 11.6 %collective-permute-start.2 = (f32[24,2048]{1,0:T(8,128)S(1)}, f32[24,2048]{1,0:T(8,128)S(1)}, u32[]{:S(2)}, u32[]{:S(2)}) collective-permute-start(f32[24,2048]{1,0:T(8,128)S(1)} %get-tuple-element.34), channel_id=1, source_target_pairs={{0,16},{16,32},{32,48},{48,64},{64,80},{80,96},{96,112},{112,128},... | collective-permute-start | bytes 589832 | tf_op jit(solution)/shard_map/ppermute | solution.py:360
  82.0 0.0 copy-start.4
  82.0 2.1 %collective-permute-start.3 = (f32[24,2048]{1,0:T(8,128)S(1)}, f32[24,2048]{1,0:T(8,128)S(1)}, u32[]{:S(2)}, u32[]{:S(2)}) collective-permute-start(f32[24,2048]{1,0:T(8,128)S(1)} %get-tuple-element.35), channel_id=1, source_target_pairs={{16,0},{32,16},{48,32},{64,48},{80,64},{96,80},{112,96},{128,112},... | collective-permute-start | bytes 589832 | tf_op jit(solution)/shard_map/ppermute | solution.py:361
  84.1 0.5 collective-permute-done.2.mid_above_ref.above_ref
  84.6 4.9 %collective-permute-done.3.mid_below_ref.below_ref = f32[24,2048]{1,0:T(8,128)S(1)} collective-permute-done((f32[24,2048]{1,0:T(8,128)S(1)}, f32[24,2048]{1,0:T(8,128)S(1)}, u32[]{:S(2)}, u32[]{:S(2)}) %collective-permute-start.3) | collective-permute-done | bytes 196640 | tf_op jit(solution)/shard_map/ppermute | solution.py:361
  89.4 0.0 all-to-all-done.4.parts_ref
  89.5 10.5 %all_to_all.43.parts_ref = f32[4,6,16,128]{3,2,1,0:T(8,128)S(1)} all-to-all(f32[4,6,16,128]{3,2,1,0:T(8,128)S(1)} %add_parts.3), channel_id=1, replica_groups=mesh['yl'=2,'z'=8,'core'=2,'x'=4,'yh'=4] {'yh'}, dimensions={0} | all-to-all | bytes 393216 | tf_op jit(solution)/shard_map/all_to_all | solution.py:411
  100.0 10.3 %all_to_all.44.value_ref = f32[4,6,16,128]{3,2,1,0:T(8,128)S(1)} all-to-all(f32[4,6,16,128]{3,2,1,0:T(8,128)S(1)} %owner.3), channel_id=1, replica_groups=mesh['yl'=2,'z'=8,'core'=2,'x'=4,'yh'=4] {'yh'}, dimensions={0} | all-to-all | bytes 393216 | tf_op jit(solution)/shard_map/all_to_all | solution.py:411
  110.3 0.9 copies.3
  111.2 4.5 %all-to-all-start.7 = ((f32[4,4,6,16,128]{4,3,2,1,0:T(8,128)}), f32[4,4,6,16,128]{4,3,2,1,0:T(8,128)S(1)}, u32[]{:S(2)}, u32[]{:S(2)}) async-start(f32[4,4,6,16,128]{4,3,2,1,0:T(8,128)} %copies.3), calls=%async_computation.7 | async-start | bytes 1572864 | tf_op jit(solution)/shard_map/all_to_all | solution.py:411
  115.7 2.2 %solute_step.1 = (f32[3,16,2048]{2,1,0:T(8,128)S(1)}, f32[3,16,2048]{2,1,0:T(8,128)S(1)}, f32[6,2048]{1,0:T(8,128)}) custom-call(f32[3,16,2048]{2,1,0:T(8,128)S(1)} %copy-done.1, f32[3,16,2048]{2,1,0:T(8,128)S(1)} %copy-done.4, f32[9,2048]{1,0:T(8,128)S(1)} %copy-done.9, f32[9,2048]{1,0:T(8,128)S(1)} %copy-done.10, ...), custom_call_target="tpu_custom_call" | custom-call | tf_op jit(solution)/shard_map/solute_step/pallas_call | solution.py:259
  117.9 6.2 %all-to-all-done.7 = f32[4,4,6,16,128]{4,3,2,1,0:T(8,128)S(1)} async-done(((f32[4,4,6,16,128]{4,3,2,1,0:T(8,128)}), f32[4,4,6,16,128]{4,3,2,1,0:T(8,128)S(1)}, u32[]{:S(2)}, u32[]{:S(2)}) %all-to-all-start.7) | async-done | bytes 786464 | tf_op jit(solution)/shard_map/all_to_all | solution.py:411
  124.0 0.9 end_rows.1
  124.9 8.1 %collective-permute-start.4 = (f32[3,2048]{1,0:T(4,128)S(1)}, f32[3,2048]{1,0:T(4,128)S(1)}, u32[]{:S(2)}, u32[]{:S(2)}) collective-permute-start(f32[3,2048]{1,0:T(4,128)S(1)} %get-tuple-element.42), channel_id=1, source_target_pairs={{0,16},{16,0},{32,48},{48,32},{64,80},{80,64},{96,112},{112,96},{1... | collective-permute-start | bytes 73736 | tf_op jit(solution)/shard_map/ppermute | solution.py:355
  133.0 6.1 %collective-permute-start.5 = (f32[3,2048]{1,0:T(4,128)S(1)}, f32[3,2048]{1,0:T(4,128)S(1)}, u32[]{:S(2)}, u32[]{:S(2)}) collective-permute-start(f32[3,2048]{1,0:T(4,128)S(1)} %get-tuple-element.43), channel_id=1, source_target_pairs={{0,496},{16,32},{32,16},{48,64},{64,48},{80,96},{96,80},{112,128},... | collective-permute-start | bytes 73736 | tf_op jit(solution)/shard_map/ppermute | solution.py:354
  139.2 0.0 copy-start.2
  139.2 1.7 %copy-done.2 = f32[6,3,16,2048]{3,2,1,0:T(8,128)S(1)} copy-done((f32[6,3,16,2048]{3,2,1,0:T(8,128)S(1)}, f32[6,3,16,2048]{3,2,1,0:T(8,128)}, u32[]{:S(2)}) %copy-start.2) | copy-done | bytes 2359320
  140.8 4.2 %second_step.1 = f32[6,3,16,2048]{3,2,1,0:T(8,128)} custom-call(s32[6]{0:T(128)S(1)} %copy-done.11, f32[4]{0:T(128)S(1)} %copy-done.12, f32[6,3,16,2048]{3,2,1,0:T(8,128)S(1)} %copy-done.2, f32[3,16,2048]{2,1,0:T(8,128)S(1)} %get-tuple-element.38.solute_ref, f32[16,6,16,128]{3,2,1,0:T(8,128)S(1)} %bitcast.7, ...), custom_call_target="tpu_custom_call" | custom-call | flops 20000000 | bytes 10000000 | tf_op jit(solution)/shard_map/second_step/pallas_call | solution.py:308
  145.1 0.0 collective-permute-done.4.inner_ref
  145.1 0.0 collective-permute-done.5.outer_ref
  145.1 1.1 solute_end.1
  (13 shorter events, 0.1 us)
Async XLA Ops:
  4.6 18.9 %all-to-all-start = ((f32[4,4,6,16,128]{4,3,2,1,0:T(8,128)}), f32[4,4,6,16,128]{4,3,2,1,0:T(8,128)S(1)}, u32[]{:S(2)}, u32[]{:S(2)}) async-start(f32[4,4,6,16,128]{4,3,2,1,0:T(8,128)} %bitcast.10), calls=%async_computation | async-start | bytes 1572864 | tf_op jit(solution)/shard_map/all_to_all | solution.py:411
  9.5 9.7 %collective-permute-start = (f32[27,2048]{1,0:T(8,128)}, f32[27,2048]{1,0:T(8,128)S(1)}, u32[]{:S(2)}, u32[]{:S(2)}) collective-permute-start(f32[27,2048]{1,0:T(8,128)} %get-tuple-element.24), channel_id=1, source_target_pairs={{0,16},{16,32},{32,48},{48,64},{64,80},{80,96},{96,112},{112,128},... | collective-permute-start | bytes 663560 | tf_op jit(solution)/shard_map/ppermute | solution.py:360
  14.3 47.1 %copy-start = (f32[6,3,16,2048]{3,2,1,0:T(8,128)S(1)}, f32[6,3,16,2048]{3,2,1,0:T(8,128)}, u32[]{:S(2)}) copy-start(f32[6,3,16,2048]{3,2,1,0:T(8,128)} %noise_ref.3) | copy-start | bytes 7077892
  14.3 47.1 %copy-start.1 = (f32[3,16,2048]{2,1,0:T(8,128)S(1)}, f32[3,16,2048]{2,1,0:T(8,128)}, u32[]{:S(2)}) copy-start(f32[3,16,2048]{2,1,0:T(8,128)} %solute_ref.5) | copy-start | bytes 1179652
  14.3 47.1 %copy-start.11 = (s32[6]{0:T(128)S(1)}, s32[6]{0:T(128)}, u32[]{:S(2)}) copy-start(s32[6]{0:T(128)} %group_ref.3) | copy-start | bytes 76
  14.4 47.1 %copy-start.12 = (f32[4]{0:T(128)S(1)}, f32[4]{0:T(128)}, u32[]{:S(2)}) copy-start(f32[4]{0:T(128)} %mobility_ref.3) | copy-start | bytes 52
  14.4 8.5 %collective-permute-start.1 = (f32[27,2048]{1,0:T(8,128)}, f32[27,2048]{1,0:T(8,128)S(1)}, u32[]{:S(2)}, u32[]{:S(2)}) collective-permute-start(f32[27,2048]{1,0:T(8,128)} %get-tuple-element.25), channel_id=1, source_target_pairs={{16,0},{32,16},{48,32},{64,48},{80,64},{96,80},{112,96},{128,112},... | collective-permute-start | bytes 663560 | tf_op jit(solution)/shard_map/ppermute | solution.py:361
  19.2 0.7 copy-start.5
  22.8 0.7 copy-start.7
  23.5 37.9 %copy-start.3 = (s32[3,16,2048]{2,1,0:T(8,128)S(1)}, s32[3,16,2048]{2,1,0:T(8,128)}, u32[]{:S(2)}) copy-start(s32[3,16,2048]{2,1,0:T(8,128)} %ids_ref.3) | copy-start | bytes 1179652
  23.5 37.9 %copy-start.6 = (f32[27,2048]{1,0:T(8,128)S(1)}, f32[27,2048]{1,0:T(8,128)}, u32[]{:S(2)}) copy-start(f32[27,2048]{1,0:T(8,128)} %copy-done.5) | copy-start | bytes 663556
  23.5 37.9 %copy-start.8 = (f32[27,2048]{1,0:T(8,128)S(1)}, f32[27,2048]{1,0:T(8,128)}, u32[]{:S(2)}) copy-start(f32[27,2048]{1,0:T(8,128)} %copy-done.7) | copy-start | bytes 663556
  66.9 22.6 %all-to-all-start.4 = ((f32[4,4,6,16,128]{4,3,2,1,0:T(8,128)}), f32[4,4,6,16,128]{4,3,2,1,0:T(8,128)S(1)}, u32[]{:S(2)}, u32[]{:S(2)}) async-start(f32[4,4,6,16,128]{4,3,2,1,0:T(8,128)} %bitcast.3), calls=%async_computation.4 | async-start | bytes 1572864 | tf_op jit(solution)/shard_map/all_to_all | solution.py:411
  70.4 14.2 %collective-permute-start.2 = (f32[24,2048]{1,0:T(8,128)S(1)}, f32[24,2048]{1,0:T(8,128)S(1)}, u32[]{:S(2)}, u32[]{:S(2)}) collective-permute-start(f32[24,2048]{1,0:T(8,128)S(1)} %get-tuple-element.34), channel_id=1, source_target_pairs={{0,16},{16,32},{32,48},{48,64},{64,80},{80,96},{96,112},{112,128},... | collective-permute-start | bytes 589832 | tf_op jit(solution)/shard_map/ppermute | solution.py:360
  82.0 33.7 %copy-start.4 = (f32[3,16,2048]{2,1,0:T(8,128)S(1)}, f32[3,16,2048]{2,1,0:T(8,128)}, u32[]{:S(2)}) copy-start(f32[3,16,2048]{2,1,0:T(8,128)} %get-tuple-element.30.middle_ref) | copy-start | bytes 1179652
  82.0 33.7 %copy-start.9 = (f32[9,2048]{1,0:T(8,128)S(1)}, f32[9,2048]{1,0:T(8,128)}, u32[]{:S(2)}) copy-start(f32[9,2048]{1,0:T(8,128)} %get-tuple-element.31.above_ref) | copy-start | bytes 221188
  82.0 33.7 %copy-start.10 = (f32[9,2048]{1,0:T(8,128)S(1)}, f32[9,2048]{1,0:T(8,128)}, u32[]{:S(2)}) copy-start(f32[9,2048]{1,0:T(8,128)} %get-tuple-element.32.below_ref) | copy-start | bytes 221188
  82.0 7.4 %collective-permute-start.3 = (f32[24,2048]{1,0:T(8,128)S(1)}, f32[24,2048]{1,0:T(8,128)S(1)}, u32[]{:S(2)}, u32[]{:S(2)}) collective-permute-start(f32[24,2048]{1,0:T(8,128)S(1)} %get-tuple-element.35), channel_id=1, source_target_pairs={{16,0},{32,16},{48,32},{64,48},{80,64},{96,80},{112,96},{128,112},... | collective-permute-start | bytes 589832 | tf_op jit(solution)/shard_map/ppermute | solution.py:361
  111.2 12.8 %all-to-all-start.7 = ((f32[4,4,6,16,128]{4,3,2,1,0:T(8,128)}), f32[4,4,6,16,128]{4,3,2,1,0:T(8,128)S(1)}, u32[]{:S(2)}, u32[]{:S(2)}) async-start(f32[4,4,6,16,128]{4,3,2,1,0:T(8,128)} %copies.3), calls=%async_computation.7 | async-start | bytes 1572864 | tf_op jit(solution)/shard_map/all_to_all | solution.py:411
  124.9 20.1 %collective-permute-start.4 = (f32[3,2048]{1,0:T(4,128)S(1)}, f32[3,2048]{1,0:T(4,128)S(1)}, u32[]{:S(2)}, u32[]{:S(2)}) collective-permute-start(f32[3,2048]{1,0:T(4,128)S(1)} %get-tuple-element.42), channel_id=1, source_target_pairs={{0,16},{16,0},{32,48},{48,32},{64,80},{80,64},{96,112},{112,96},{1... | collective-permute-start | bytes 73736 | tf_op jit(solution)/shard_map/ppermute | solution.py:355
  133.0 12.0 %collective-permute-start.5 = (f32[3,2048]{1,0:T(4,128)S(1)}, f32[3,2048]{1,0:T(4,128)S(1)}, u32[]{:S(2)}, u32[]{:S(2)}) collective-permute-start(f32[3,2048]{1,0:T(4,128)S(1)} %get-tuple-element.43), channel_id=1, source_target_pairs={{0,496},{16,32},{32,16},{48,64},{64,48},{80,96},{96,80},{112,128},... | collective-permute-start | bytes 73736 | tf_op jit(solution)/shard_map/ppermute | solution.py:354
  139.2 1.7 %copy-start.2 = (f32[6,3,16,2048]{3,2,1,0:T(8,128)S(1)}, f32[6,3,16,2048]{3,2,1,0:T(8,128)}, u32[]{:S(2)}) copy-start(f32[6,3,16,2048]{3,2,1,0:T(8,128)} %get-tuple-element.29.old_ref) | copy-start | bytes 7077892

commit v9 on v4

--- a/solution.py
+++ b/solution.py
@@ -31,6 +31,10 @@
 
 def hbm(*dims):
     return pltpu.HBM(dims, F32)
+
+
+def from_hbm(*arrays):
+    return [pltpu.with_memory_space_constraint(array, pltpu.HBM) for array in arrays]
 
 
 def params(mib=16):
@@ -135,7 +139,7 @@
 
 def first_step(
     first_ref, group_ref, mobility_ref, noise_ref, ids_ref, solute_ref, sums_ref, above_ref, below_ref,
-    eta_ref, next_sums_ref, next_ref, prev_ref, bulk_ref, rows_above_ref, rows_below_ref, base_ref, slope_ref,
+    eta_ref, next_sums_ref, next_ref, prev_ref, bulk_ref, base_ref, slope_ref,
 ):
     grain = pl.program_id(0)
 
@@ -150,8 +154,6 @@
                 bulk_ref[plane, :, columns] = bulk
                 prev_ref[row : row + 2, columns] = bulk[:2]
                 next_ref[row : row + 2, columns] = bulk[ROWS - 2 :]
-        rows_above_ref[...] = above_ref[GRAINS * PLANES :]
-        rows_below_ref[...] = below_ref[GRAINS * PLANES :]
 
     rate = time_step * mobility_ref[group_ref[grain]]
     planes = [
@@ -195,16 +197,14 @@
         ],
         out_specs=[grain_block, whole(*sums.shape)]
         + [whole(edge, COLS)] * 2
-        + [whole(*solute.shape)]
-        + [whole(3 * PLANES, COLS)] * 2,
+        + [whole(*solute.shape)],
         out_shape=[hbm(*noise.shape), shape(*sums.shape)]
         + [shape(edge, COLS)] * 2
-        + [hbm(*solute.shape)]
-        + [hbm(3 * PLANES, COLS)] * 2,
+        + [hbm(*solute.shape)],
         scratch_shapes=[pltpu.VMEM(solute.shape, F32)] * 2,
         compiler_params=params(),
         name="first_step",
-    )(first, groups, mobility, noise, ids, solute, sums, above, below)
+    )(first, groups, mobility, noise, *from_hbm(ids), solute, sums, *from_hbm(above, below))
 
 
 PAD = 8
@@ -227,7 +227,7 @@
         for ref in (deep_ref, bulk_ref):
             ref[plane, :PAD] = jnp.zeros((PAD, COLS), F32)
             ref[plane, PAD + ROWS :] = jnp.zeros((PAD, COLS), F32)
-        row = 3 * plane
+        row = GRAINS * PLANES + 3 * plane
         deep_ref[plane, PAD - 3 : PAD] = above_ref[row : row + 3, :]
         deep_ref[plane, PAD : PAD + ROWS] = solute_ref[plane]
         deep_ref[plane, PAD + ROWS : PAD + ROWS + 3] = below_ref[row : row + 3, :]
@@ -256,7 +256,7 @@
         scratch_shapes=[pltpu.VMEM((PLANES, DEEP, COLS), F32)] * 2,
         compiler_params=params(),
         name="solute_step",
-    )(solute, bulk, above, below, mid_above, mid_below)
+    )(*from_hbm(solute, bulk, above, below, mid_above, mid_below))
 
 
 def second_potential(part_ref, sums_ref, out_ref, next_ref, prev_ref):
@@ -309,7 +309,7 @@
         compiler_params=params(),
         cost_estimate=pl.CostEstimate(flops=20_000_000, bytes_accessed=10_000_000, transcendentals=0),
         name="second_step",
-    )(groups, mobility, eta, solute, sums, above, below)
+    )(groups, mobility, eta, solute, sums, *from_hbm(above, below))
 
 
 def solute_end(solute_ref, potential_ref, above_ref, below_ref, out_ref):
@@ -387,26 +387,25 @@
     return lax.all_to_all(blocks, axis, 0, 0, tiled=True)
 
 
-def total(sums, to_next, to_prev):
-    count = lax.axis_size("yl") * lax.axis_size("z") * lax.axis_size("core")
+def total(sums):
     along = lax.axis_size("x")
     parts = dealt(sums.reshape((along, BLOCKS // along) + sums.shape[1:]), "x")
-    parts, above, below = lax.optimization_barrier((parts, *exchange(to_next, to_prev, count)))
     parts = dealt(call_add_parts(parts), "yh")
     parts = dealt(call_owner(parts), "yh")
-    return dealt(call_copies(parts, along), "x").reshape(sums.shape), above, below
+    return dealt(call_copies(parts, along), "x").reshape(sums.shape)
 
 
 def shards(grain_ids, group_of, group_mobility, seed_noise, concentration):
     count = lax.axis_size("yl") * lax.axis_size("z") * lax.axis_size("core")
     first = (lax.axis_index(GRAIN) * GRAINS).astype(jnp.int32).reshape(1)
     sums, to_next, to_prev = call_first_sums(first, seed_noise, grain_ids, concentration)
-    sums, above, below = total(sums, to_next, to_prev)
-    eta, sums, to_next, to_prev, bulk, rows_above, rows_below = call_first_step(
-        first, group_of, group_mobility, seed_noise, grain_ids, concentration, sums, above, below
+    above, below = exchange(to_next, to_prev, count)
+    eta, sums, to_next, to_prev, bulk = call_first_step(
+        first, group_of, group_mobility, seed_noise, grain_ids, concentration, total(sums), above, below
     )
-    sums, mid_above, mid_below = total(sums, to_next, to_prev)
-    solute, part = call_solute_step(concentration, bulk, rows_above, rows_below, mid_above, mid_below)
+    mid_above, mid_below = exchange(to_next, to_prev, count)
+    sums = total(sums)
+    solute, part = call_solute_step(concentration, bulk, above, below, mid_above, mid_below)
     potential, to_next, to_prev = call_second_potential(part, sums)
     end_above, end_below = exchange(to_next, to_prev, count)
     eta = call_second_step(group_of, group_mobility, eta, solute, sums, mid_above, mid_below)

time: 146 us -> 150 us (1.027)
  the two profiles are of different devices: /device:TPU:1 before, /device:TPU:2 now
where the time goes in v9:
time: 150 us; the launch traced here: 149 us
  blocking collectives  82.4 us (55%)
  starting transfers between devices  34.2 us (23%)
  Pallas kernels  20.5 us (14%)
  waiting for transfers between devices  6.97 us (5%)
  local copies, waits for them, and re-layouts  3.8 us (3%)
    all_to_all x6, blocking collectives, dealt(): return lax.all_to_all(blocks, axis, 0, 0, tiled=True)  82.4 us
    ppermute x3, starting transfers between devices, exchange(): lax.ppermute(to_prev, SPACE, [((i + 1) % count, i) for i in range(count)])  18.3 us
    all_to_all x2, starting transfers between devices, dealt(): return lax.all_to_all(blocks, axis, 0, 0, tiled=True)  9.97 us
    ppermute x3, starting transfers between devices, exchange(): lax.ppermute(to_next, SPACE, [(i, (i + 1) % count) for i in range(count)])  5.92 us
    pallas_call x1, Pallas kernels, call_first_step(): pl.pallas_call(first_step, grid=(GRAINS,), in_specs=[smem(), smem(), smem...  5.7 us
    pallas_call x1, Pallas kernels, call_second_step(): pl.pallas_call(second_step, grid=(GRAINS,), in_specs=[smem(), smem(), gra...  4.88 us
    pallas_call x1, Pallas kernels, call_first_sums(): pl.pallas_call(first_sums, grid=(COLS // width,), in_specs=[smem(), pl.Bl...  4 us
    unnamed x26, local copies, waits for them, and re-layouts  3.8 us
  transfers between devices with their start and end apart: 8, of which 4 were waited for; matrix products, arithmetic and copies ran while one was open for 0% of the time, Pallas kernels for 5%

profile of v9, /device:TPU:2, one launch (start us, length us, event | category | flops | bytes accessed | tf_op | source)
XLA Modules:
  0.0 148.7 jit_solution(15373756457892925897)
XLA Ops:
  0.6 4.0 %first_sums.1 = (f32[16,6,16,128]{3,2,1,0:T(8,128)}, f32[27,2048]{1,0:T(8,128)}, f32[27,2048]{1,0:T(8,128)}) custom-call(s32[1]{0:T(128)} %bitcast.first_ref, f32[6,3,16,2048]{3,2,1,0:T(8,128)} %noise_ref.3, s32[3,16,2048]{2,1,0:T(8,128)} %ids_ref.3, f32[3,16,2048]{2,1,0:T(8,128)} %solute_ref.5), custom_call_target="tpu_custom_call" | custom-call | tf_op jit(solution)/shard_map/first_sums/pallas_call | solution.py:88
  4.6 17.4 %all_to_all.40.parts_ref = f32[4,4,6,16,128]{4,3,2,1,0:T(8,128)S(1)} all-to-all(f32[4,4,6,16,128]{4,3,2,1,0:T(8,128)} %bitcast.9), channel_id=1, replica_groups=mesh['yl'=2,'z'=8,'core'=2,'x'=4,'yh'=4] {'x'}, dimensions={0} | all-to-all | bytes 1572864 | tf_op jit(solution)/shard_map/all_to_all | solution.py:387
  22.0 0.0 copy-start
  22.0 0.0 copy-start.1
  22.0 0.0 copy-start.5
  22.0 0.0 copy-start.6
  22.1 14.6 %all_to_all.41.parts_ref = f32[4,6,16,128]{3,2,1,0:T(8,128)S(1)} all-to-all(f32[4,6,16,128]{3,2,1,0:T(8,128)S(1)} %add_parts.2), channel_id=1, replica_groups=mesh['yl'=2,'z'=8,'core'=2,'x'=4,'yh'=4] {'yh'}, dimensions={0} | all-to-all | bytes 393216 | tf_op jit(solution)/shard_map/all_to_all | solution.py:387
  36.8 11.4 %all_to_all.42.value_ref = f32[4,6,16,128]{3,2,1,0:T(8,128)S(1)} all-to-all(f32[4,6,16,128]{3,2,1,0:T(8,128)S(1)} %owner.2), channel_id=1, replica_groups=mesh['yl'=2,'z'=8,'core'=2,'x'=4,'yh'=4] {'yh'}, dimensions={0} | all-to-all | bytes 393216 | tf_op jit(solution)/shard_map/all_to_all | solution.py:387
  48.2 0.9 copies.2
  49.1 4.9 %all-to-all-start.3 = ((f32[4,4,6,16,128]{4,3,2,1,0:T(8,128)}), f32[4,4,6,16,128]{4,3,2,1,0:T(8,128)S(1)}, u32[]{:S(2)}, u32[]{:S(2)}) async-start(f32[4,4,6,16,128]{4,3,2,1,0:T(8,128)} %copies.2), calls=%async_computation.3 | async-start | bytes 1572864 | tf_op jit(solution)/shard_map/all_to_all | solution.py:387
  54.1 1.9 %collective-permute-start = (f32[27,2048]{1,0:T(8,128)}, f32[27,2048]{1,0:T(8,128)S(1)}, u32[]{:S(2)}, u32[]{:S(2)}) collective-permute-start(f32[27,2048]{1,0:T(8,128)} %get-tuple-element.16), channel_id=1, source_target_pairs={{0,16},{16,32},{32,48},{48,64},{64,80},{80,96},{96,112},{112,128},... | collective-permute-start | bytes 663560 | tf_op jit(solution)/shard_map/ppermute | solution.py:336
  56.0 6.9 %collective-permute-start.1 = (f32[27,2048]{1,0:T(8,128)}, f32[27,2048]{1,0:T(8,128)}, u32[]{:S(2)}, u32[]{:S(2)}) collective-permute-start(f32[27,2048]{1,0:T(8,128)} %get-tuple-element.17), channel_id=1, source_target_pairs={{16,0},{32,16},{48,32},{64,48},{80,64},{96,80},{112,96},{128,112},... | collective-permute-start | bytes 663560 | tf_op jit(solution)/shard_map/ppermute | solution.py:337
  62.9 2.3 %collective-permute-done.above_ref = f32[27,2048]{1,0:T(8,128)S(1)} collective-permute-done((f32[27,2048]{1,0:T(8,128)}, f32[27,2048]{1,0:T(8,128)S(1)}, u32[]{:S(2)}, u32[]{:S(2)}) %collective-permute-start) | collective-permute-done | bytes 221216 | tf_op jit(solution)/shard_map/ppermute | solution.py:336
  65.2 0.7 copy-done.10
  65.9 1.2 collective-permute-done.1.below_ref
  67.1 0.0 all-to-all-done.3
  67.1 0.0 copy-done
  67.1 0.0 copy-done.1
  67.1 0.0 copy-done.5
  67.1 0.0 copy-done.6
  67.1 5.7 %first_step.1 = (f32[6,3,16,2048]{3,2,1,0:T(8,128)}, f32[16,6,16,128]{3,2,1,0:T(8,128)S(1)}, f32[24,2048]{1,0:T(8,128)S(1)}, f32[24,2048]{1,0:T(8,128)S(1)}, f32[3,16,2048]{2,1,0:T(8,128)}) custom-call(s32[1]{0:T(128)} %bitcast.first_ref, s32[6]{0:T(128)S(1)} %copy-done.5, f32[4]{0:T(128)S(1)} %copy-done.6, f32[6,3,16,2048]{3,2,1,0:T(8,128)S(1)} %copy-done, ...), custom_call_target="tpu_custom_call" | custom-call | tf_op jit(solution)/shard_map/first_step/pallas_call | solution.py:190
  72.8 0.7 copy-done.8
  73.5 14.9 %all_to_all.43.parts_ref = f32[4,4,6,16,128]{4,3,2,1,0:T(8,128)S(1)} all-to-all(f32[4,4,6,16,128]{4,3,2,1,0:T(8,128)S(1)} %bitcast.8), channel_id=1, replica_groups=mesh['yl'=2,'z'=8,'core'=2,'x'=4,'yh'=4] {'x'}, dimensions={0} | all-to-all | bytes 1572864 | tf_op jit(solution)/shard_map/all_to_all | solution.py:387
  88.5 12.2 %all_to_all.44.parts_ref = f32[4,6,16,128]{3,2,1,0:T(8,128)S(1)} all-to-all(f32[4,6,16,128]{3,2,1,0:T(8,128)S(1)} %add_parts.3), channel_id=1, replica_groups=mesh['yl'=2,'z'=8,'core'=2,'x'=4,'yh'=4] {'yh'}, dimensions={0} | all-to-all | bytes 393216 | tf_op jit(solution)/shard_map/all_to_all | solution.py:387
  100.7 11.8 %all_to_all.45.value_ref = f32[4,6,16,128]{3,2,1,0:T(8,128)S(1)} all-to-all(f32[4,6,16,128]{3,2,1,0:T(8,128)S(1)} %owner.3), channel_id=1, replica_groups=mesh['yl'=2,'z'=8,'core'=2,'x'=4,'yh'=4] {'yh'}, dimensions={0} | all-to-all | bytes 393216 | tf_op jit(solution)/shard_map/all_to_all | solution.py:387
  112.5 0.0 copy-done.7
  112.5 0.9 copies.3
  113.4 5.1 %all-to-all-start.7 = ((f32[4,4,6,16,128]{4,3,2,1,0:T(8,128)}), f32[4,4,6,16,128]{4,3,2,1,0:T(8,128)S(1)}, u32[]{:S(2)}, u32[]{:S(2)}) async-start(f32[4,4,6,16,128]{4,3,2,1,0:T(8,128)} %copies.3), calls=%async_computation.7 | async-start | bytes 1572864 | tf_op jit(solution)/shard_map/all_to_all | solution.py:387
  118.5 0.0 copy-done.9
  118.5 1.9 %collective-permute-start.2 = (f32[24,2048]{1,0:T(8,128)S(1)}, f32[24,2048]{1,0:T(8,128)S(1)}, u32[]{:S(2)}, u32[]{:S(2)}) collective-permute-start(f32[24,2048]{1,0:T(8,128)S(1)} %copy-done.9), channel_id=1, source_target_pairs={{0,16},{16,32},{32,48},{48,64},{64,80},{80,96},{96,112},{112,128},... | collective-permute-start | bytes 589832 | tf_op jit(solution)/shard_map/ppermute | solution.py:336
  120.4 5.8 %collective-permute-start.3 = (f32[24,2048]{1,0:T(8,128)}, f32[24,2048]{1,0:T(8,128)S(1)}, u32[]{:S(2)}, u32[]{:S(2)}) collective-permute-start(f32[24,2048]{1,0:T(8,128)} %copy-done.7), channel_id=1, source_target_pairs={{16,0},{32,16},{48,32},{64,48},{80,64},{96,80},{112,96},{128,112},... | collective-permute-start | bytes 589832 | tf_op jit(solution)/shard_map/ppermute | solution.py:337
  126.2 1.4 collective-permute-done.2.mid_above_ref.above_ref
  127.6 2.1 %collective-permute-done.3.mid_below_ref.below_ref = f32[24,2048]{1,0:T(8,128)S(1)} collective-permute-done((f32[24,2048]{1,0:T(8,128)}, f32[24,2048]{1,0:T(8,128)S(1)}, u32[]{:S(2)}, u32[]{:S(2)}) %collective-permute-start.3) | collective-permute-done | bytes 196640 | tf_op jit(solution)/shard_map/ppermute | solution.py:337
  129.7 0.0 copy-done.11
  129.7 0.7 copy-done.12
  130.3 2.8 %solute_step.1 = (f32[3,16,2048]{2,1,0:T(8,128)S(1)}, f32[3,16,2048]{2,1,0:T(8,128)S(1)}) custom-call(f32[3,16,2048]{2,1,0:T(8,128)} %solute_ref.5, f32[3,16,2048]{2,1,0:T(8,128)} %get-tuple-element.19.middle_ref, f32[27,2048]{1,0:T(8,128)} %copy-done.10, f32[27,2048]{1,0:T(8,128)} %collective-permute-done.1.below_ref, f32[24,2048]{1,0:T(8,128)} %copy-done.11, ...), custom_call_target="tpu_custom_call" | custom-call | tf_op jit(solution)/shard_map/solute_step/pallas_call | solution.py:253
  133.2 0.0 copy-start.3
  133.2 0.7 copy-done.3
  133.9 0.0 all-to-all-done.7
  133.9 1.0 copy-done.4
  134.9 0.1 second_potential.1
  135.0 2.1 %collective-permute-start.4 = (f32[3,2048]{1,0:T(4,128)S(1)}, f32[3,2048]{1,0:T(4,128)S(1)}, u32[]{:S(2)}, u32[]{:S(2)}) collective-permute-start(f32[3,2048]{1,0:T(4,128)S(1)} %get-tuple-element.26), channel_id=1, source_target_pairs={{0,16},{16,32},{32,48},{48,64},{64,80},{80,96},{96,112},{112,128},... | collective-permute-start | bytes 73736 | tf_op jit(solution)/shard_map/ppermute | solution.py:336
  137.1 5.6 %collective-permute-start.5 = (f32[3,2048]{1,0:T(4,128)S(1)}, f32[3,2048]{1,0:T(4,128)S(1)}, u32[]{:S(2)}, u32[]{:S(2)}) collective-permute-start(f32[3,2048]{1,0:T(4,128)S(1)} %get-tuple-element.27), channel_id=1, source_target_pairs={{16,0},{32,16},{48,32},{64,48},{80,64},{96,80},{112,96},{128,112},... | collective-permute-start | bytes 73736 | tf_op jit(solution)/shard_map/ppermute | solution.py:337
  142.7 0.0 copy-done.2
  142.7 4.9 %second_step.1 = f32[6,3,16,2048]{3,2,1,0:T(8,128)} custom-call(s32[6]{0:T(128)S(1)} %copy-done.5, f32[4]{0:T(128)S(1)} %copy-done.6, f32[6,3,16,2048]{3,2,1,0:T(8,128)S(1)} %copy-done.2, f32[3,16,2048]{2,1,0:T(8,128)S(1)} %get-tuple-element.22.solute_ref, f32[16,6,16,128]{3,2,1,0:T(8,128)S(1)} %bitcast.6, f32[24,2048]{1,0:T(8,128)} %copy-done.11, ...), custom_call_target="tpu_custom_call" | custom-call | flops 20000000 | bytes 10000000 | tf_op jit(solution)/shard_map/second_step/pallas_call | solution.py:299
  147.6 0.0 collective-permute-done.4.above_ref
  147.6 0.0 collective-permute-done.5.below_ref
  147.6 1.1 solute_end.1
  (12 shorter events, 0.1 us)
Async XLA Ops:
  22.0 45.1 %copy-start = (f32[6,3,16,2048]{3,2,1,0:T(8,128)S(1)}, f32[6,3,16,2048]{3,2,1,0:T(8,128)}, u32[]{:S(2)}) copy-start(f32[6,3,16,2048]{3,2,1,0:T(8,128)} %noise_ref.3) | copy-start | bytes 7077892
  22.0 45.1 %copy-start.1 = (f32[3,16,2048]{2,1,0:T(8,128)S(1)}, f32[3,16,2048]{2,1,0:T(8,128)}, u32[]{:S(2)}) copy-start(f32[3,16,2048]{2,1,0:T(8,128)} %solute_ref.5) | copy-start | bytes 1179652
  22.0 45.1 %copy-start.5 = (s32[6]{0:T(128)S(1)}, s32[6]{0:T(128)}, u32[]{:S(2)}) copy-start(s32[6]{0:T(128)} %group_ref.3) | copy-start | bytes 76
  22.0 45.1 %copy-start.6 = (f32[4]{0:T(128)S(1)}, f32[4]{0:T(128)}, u32[]{:S(2)}) copy-start(f32[4]{0:T(128)} %mobility_ref.3) | copy-start | bytes 52
  49.1 18.0 %all-to-all-start.3 = ((f32[4,4,6,16,128]{4,3,2,1,0:T(8,128)}), f32[4,4,6,16,128]{4,3,2,1,0:T(8,128)S(1)}, u32[]{:S(2)}, u32[]{:S(2)}) async-start(f32[4,4,6,16,128]{4,3,2,1,0:T(8,128)} %copies.2), calls=%async_computation.3 | async-start | bytes 1572864 | tf_op jit(solution)/shard_map/all_to_all | solution.py:387
  54.1 11.2 %collective-permute-start = (f32[27,2048]{1,0:T(8,128)}, f32[27,2048]{1,0:T(8,128)S(1)}, u32[]{:S(2)}, u32[]{:S(2)}) collective-permute-start(f32[27,2048]{1,0:T(8,128)} %get-tuple-element.16), channel_id=1, source_target_pairs={{0,16},{16,32},{32,48},{48,64},{64,80},{80,96},{96,112},{112,128},... | collective-permute-start | bytes 663560 | tf_op jit(solution)/shard_map/ppermute | solution.py:336
  56.0 11.1 %collective-permute-start.1 = (f32[27,2048]{1,0:T(8,128)}, f32[27,2048]{1,0:T(8,128)}, u32[]{:S(2)}, u32[]{:S(2)}) collective-permute-start(f32[27,2048]{1,0:T(8,128)} %get-tuple-element.17), channel_id=1, source_target_pairs={{16,0},{32,16},{48,32},{64,48},{80,64},{96,80},{112,96},{128,112},... | collective-permute-start | bytes 663560 | tf_op jit(solution)/shard_map/ppermute | solution.py:337
  65.2 0.7 copy-start.10
  72.8 0.7 copy-start.8
  73.5 39.0 %copy-start.7 = (f32[24,2048]{1,0:T(8,128)}, f32[24,2048]{1,0:T(8,128)S(1)}, u32[]{:S(2)}) copy-start(f32[24,2048]{1,0:T(8,128)S(1)} %get-tuple-element.21) | copy-start | bytes 589828
  88.4 30.1 %copy-start.9 = (f32[24,2048]{1,0:T(8,128)S(1)}, f32[24,2048]{1,0:T(8,128)}, u32[]{:S(2)}) copy-start(f32[24,2048]{1,0:T(8,128)} %copy-done.8) | copy-start | bytes 589828
  113.4 29.3 %copy-start.2 = (f32[6,3,16,2048]{3,2,1,0:T(8,128)S(1)}, f32[6,3,16,2048]{3,2,1,0:T(8,128)}, u32[]{:S(2)}) copy-start(f32[6,3,16,2048]{3,2,1,0:T(8,128)} %get-tuple-element.18.old_ref) | copy-start | bytes 7077892
  113.4 20.5 %all-to-all-start.7 = ((f32[4,4,6,16,128]{4,3,2,1,0:T(8,128)}), f32[4,4,6,16,128]{4,3,2,1,0:T(8,128)S(1)}, u32[]{:S(2)}, u32[]{:S(2)}) async-start(f32[4,4,6,16,128]{4,3,2,1,0:T(8,128)} %copies.3), calls=%async_computation.7 | async-start | bytes 1572864 | tf_op jit(solution)/shard_map/all_to_all | solution.py:387
  118.5 9.1 %collective-permute-start.2 = (f32[24,2048]{1,0:T(8,128)S(1)}, f32[24,2048]{1,0:T(8,128)S(1)}, u32[]{:S(2)}, u32[]{:S(2)}) collective-permute-start(f32[24,2048]{1,0:T(8,128)S(1)} %copy-done.9), channel_id=1, source_target_pairs={{0,16},{16,32},{32,48},{48,64},{64,80},{80,96},{96,112},{112,128},... | collective-permute-start | bytes 589832 | tf_op jit(solution)/shard_map/ppermute | solution.py:336
  120.4 9.2 %collective-permute-start.3 = (f32[24,2048]{1,0:T(8,128)}, f32[24,2048]{1,0:T(8,128)S(1)}, u32[]{:S(2)}, u32[]{:S(2)}) collective-permute-start(f32[24,2048]{1,0:T(8,128)} %copy-done.7), channel_id=1, source_target_pairs={{16,0},{32,16},{48,32},{64,48},{80,64},{96,80},{112,96},{128,112},... | collective-permute-start | bytes 589832 | tf_op jit(solution)/shard_map/ppermute | solution.py:337
  127.6 2.1 %copy-start.11 = (f32[24,2048]{1,0:T(8,128)}, f32[24,2048]{1,0:T(8,128)S(1)}, u32[]{:S(2)}) copy-start(f32[24,2048]{1,0:T(8,128)S(1)} %collective-permute-done.2.mid_above_ref.above_ref) | copy-start | bytes 589828
  129.7 0.7 copy-start.12
  133.2 0.7 copy-start.3
  133.9 1.0 copy-start.4
  135.0 12.6 %collective-permute-start.4 = (f32[3,2048]{1,0:T(4,128)S(1)}, f32[3,2048]{1,0:T(4,128)S(1)}, u32[]{:S(2)}, u32[]{:S(2)}) collective-permute-start(f32[3,2048]{1,0:T(4,128)S(1)} %get-tuple-element.26), channel_id=1, source_target_pairs={{0,16},{16,32},{32,48},{48,64},{64,80},{80,96},{96,112},{112,128},... | collective-permute-start | bytes 73736 | tf_op jit(solution)/shard_map/ppermute | solution.py:336
  137.1 10.5 %collective-permute-start.5 = (f32[3,2048]{1,0:T(4,128)S(1)}, f32[3,2048]{1,0:T(4,128)S(1)}, u32[]{:S(2)}, u32[]{:S(2)}) collective-permute-start(f32[3,2048]{1,0:T(4,128)S(1)} %get-tuple-element.27), channel_id=1, source_target_pairs={{16,0},{32,16},{48,32},{64,48},{80,64},{96,80},{112,96},{128,112},... | collective-permute-start | bytes 73736 | tf_op jit(solution)/shard_map/ppermute | solution.py:337

commit v10 on v4

--- a/solution.py
+++ b/solution.py
@@ -31,6 +31,10 @@
 
 def hbm(*dims):
     return pltpu.HBM(dims, F32)
+
+
+def from_hbm(*arrays):
+    return [pltpu.with_memory_space_constraint(array, pltpu.HBM) for array in arrays]
 
 
 def params(mib=16):
@@ -204,7 +208,7 @@
         scratch_shapes=[pltpu.VMEM(solute.shape, F32)] * 2,
         compiler_params=params(),
         name="first_step",
-    )(first, groups, mobility, noise, ids, solute, sums, above, below)
+    )(first, groups, mobility, noise, *from_hbm(ids), solute, sums, *from_hbm(above, below))
 
 
 PAD = 8
@@ -387,25 +391,25 @@
     return lax.all_to_all(blocks, axis, 0, 0, tiled=True)
 
 
-def total(sums, to_next, to_prev):
-    count = lax.axis_size("yl") * lax.axis_size("z") * lax.axis_size("core")
+def total(sums, *beside_it):
     along = lax.axis_size("x")
     parts = dealt(sums.reshape((along, BLOCKS // along) + sums.shape[1:]), "x")
-    parts, above, below = lax.optimization_barrier((parts, *exchange(to_next, to_prev, count)))
+    parts, *beside_it = lax.optimization_barrier((parts, *beside_it))
     parts = dealt(call_add_parts(parts), "yh")
     parts = dealt(call_owner(parts), "yh")
-    return dealt(call_copies(parts, along), "x").reshape(sums.shape), above, below
+    return dealt(call_copies(parts, along), "x").reshape(sums.shape), *beside_it
 
 
 def shards(grain_ids, group_of, group_mobility, seed_noise, concentration):
     count = lax.axis_size("yl") * lax.axis_size("z") * lax.axis_size("core")
     first = (lax.axis_index(GRAIN) * GRAINS).astype(jnp.int32).reshape(1)
     sums, to_next, to_prev = call_first_sums(first, seed_noise, grain_ids, concentration)
-    sums, above, below = total(sums, to_next, to_prev)
+    above, below = exchange(to_next, to_prev, count)
+    (sums,) = total(sums)
     eta, sums, to_next, to_prev, bulk, rows_above, rows_below = call_first_step(
         first, group_of, group_mobility, seed_noise, grain_ids, concentration, sums, above, below
     )
-    sums, mid_above, mid_below = total(sums, to_next, to_prev)
+    sums, mid_above, mid_below = total(sums, *exchange(to_next, to_prev, count))
     solute, part = call_solute_step(concentration, bulk, rows_above, rows_below, mid_above, mid_below)
     potential, to_next, to_prev = call_second_potential(part, sums)
     end_above, end_below = exchange(to_next, to_prev, count)

time: 146 us -> 146 us (level)
  starting transfers between devices: 50.3 us -> 40.9 us
  blocking collectives: 58.5 us -> 63 us
  waiting for transfers between devices: 15.1 us -> 17.6 us
  local copies, waits for them, and re-layouts: 3.12 us -> 4.62 us
    ppermute x3, starting transfers between devices: 28.7 us -> 22.2 us  [exchange(): lax.ppermute(to_next, SPACE, [(i, (i + 1) % count) for i in range(count)])]
    all_to_all x5, blocking collectives: 58.5 us -> 63 us  [dealt(): return lax.all_to_all(blocks, axis, 0, 0, tiled=True)]
    ppermute x3, starting transfers between devices: 8.77 us -> 7.21 us  [exchange(): lax.ppermute(to_prev, SPACE, [((i + 1) % count, i) for i in range(count)])]
    unnamed x26 -> x24, local copies, waits for them, and re-layouts: 3.12 us -> 4.62 us
  transfers between devices with their start and end apart: 9 -> 9, of which waited for: 4 -> 5; matrix products, arithmetic and copies ran while one was open for 0% -> 0% of each run, Pallas kernels for 4% -> 4%
where the time goes in v10:
time: 146 us
  blocking collectives  63 us (43%)
  starting transfers between devices  40.9 us (28%)
  Pallas kernels  18.6 us (13%)
  waiting for transfers between devices  17.6 us (12%)
  local copies, waits for them, and re-layouts  4.62 us (3%)
    all_to_all x5, blocking collectives, dealt(): return lax.all_to_all(blocks, axis, 0, 0, tiled=True)  63 us
    ppermute x3, starting transfers between devices, exchange(): lax.ppermute(to_next, SPACE, [(i, (i + 1) % count) for i in range(count)])  22.2 us
    all_to_all x3, starting transfers between devices, dealt(): return lax.all_to_all(blocks, axis, 0, 0, tiled=True)  11.5 us
    ppermute x3, waiting for transfers between devices, exchange(): lax.ppermute(to_prev, SPACE, [((i + 1) % count, i) for i in range(count)])  8.59 us
    all_to_all x3, waiting for transfers between devices, dealt(): return lax.all_to_all(blocks, axis, 0, 0, tiled=True)  7.33 us
    ppermute x3, starting transfers between devices, exchange(): lax.ppermute(to_prev, SPACE, [((i + 1) % count, i) for i in range(count)])  7.21 us
    pallas_call x1, Pallas kernels, call_first_step(): pl.pallas_call(first_step, grid=(GRAINS,), in_specs=[smem(), smem(), smem...  5.77 us
    unnamed x24, local copies, waits for them, and re-layouts  4.62 us
  transfers between devices with their start and end apart: 9, of which 5 were waited for; matrix products, arithmetic and copies ran while one was open for 0% of the time, Pallas kernels for 4%

profile of v10, /device:TPU:1, one launch (start us, length us, event | category | flops | bytes accessed | tf_op | source)
XLA Modules:
  0.0 145.5 jit_solution(9412089970525449704)
XLA Ops:
  0.6 4.0 %first_sums.1 = (f32[16,6,16,128]{3,2,1,0:T(8,128)}, f32[27,2048]{1,0:T(8,128)}, f32[27,2048]{1,0:T(8,128)}) custom-call(s32[1]{0:T(128)} %bitcast.first_ref, f32[6,3,16,2048]{3,2,1,0:T(8,128)} %noise_ref.3, s32[3,16,2048]{2,1,0:T(8,128)} %ids_ref.3, f32[3,16,2048]{2,1,0:T(8,128)} %solute_ref.5), custom_call_target="tpu_custom_call" | custom-call | tf_op jit(solution)/shard_map/first_sums/pallas_call | solution.py:88
  4.6 13.2 %all_to_all.40.parts_ref = f32[4,4,6,16,128]{4,3,2,1,0:T(8,128)S(1)} all-to-all(f32[4,4,6,16,128]{4,3,2,1,0:T(8,128)} %bitcast.9), channel_id=1, replica_groups=mesh['yl'=2,'z'=8,'core'=2,'x'=4,'yh'=4] {'x'}, dimensions={0} | all-to-all | bytes 1572864 | tf_op jit(solution)/shard_map/all_to_all | solution.py:391
  17.8 0.0 copy-start
  17.9 17.9 %all_to_all.41.parts_ref = f32[4,6,16,128]{3,2,1,0:T(8,128)S(1)} all-to-all(f32[4,6,16,128]{3,2,1,0:T(8,128)S(1)} %add_parts.2), channel_id=1, replica_groups=mesh['yl'=2,'z'=8,'core'=2,'x'=4,'yh'=4] {'yh'}, dimensions={0} | all-to-all | bytes 393216 | tf_op jit(solution)/shard_map/all_to_all | solution.py:391
  35.8 10.4 %all_to_all.42.value_ref = f32[4,6,16,128]{3,2,1,0:T(8,128)S(1)} all-to-all(f32[4,6,16,128]{3,2,1,0:T(8,128)S(1)} %owner.2), channel_id=1, replica_groups=mesh['yl'=2,'z'=8,'core'=2,'x'=4,'yh'=4] {'yh'}, dimensions={0} | all-to-all | bytes 393216 | tf_op jit(solution)/shard_map/all_to_all | solution.py:391
  46.1 0.9 copies.2
  47.0 3.5 %all-to-all-start.3 = ((f32[4,4,6,16,128]{4,3,2,1,0:T(8,128)}), f32[4,4,6,16,128]{4,3,2,1,0:T(8,128)S(1)}, u32[]{:S(2)}, u32[]{:S(2)}) async-start(f32[4,4,6,16,128]{4,3,2,1,0:T(8,128)} %copies.2), calls=%async_computation.3 | async-start | bytes 1572864 | tf_op jit(solution)/shard_map/all_to_all | solution.py:391
  50.5 8.4 %collective-permute-start = (f32[27,2048]{1,0:T(8,128)}, f32[27,2048]{1,0:T(8,128)S(1)}, u32[]{:S(2)}, u32[]{:S(2)}) collective-permute-start(f32[27,2048]{1,0:T(8,128)} %get-tuple-element.21), channel_id=1, source_target_pairs={{0,16},{16,32},{32,48},{48,64},{64,80},{80,96},{96,112},{112,128},... | collective-permute-start | bytes 663560 | tf_op jit(solution)/shard_map/ppermute | solution.py:340
  59.0 1.9 %collective-permute-start.1 = (f32[27,2048]{1,0:T(8,128)}, f32[27,2048]{1,0:T(8,128)}, u32[]{:S(2)}, u32[]{:S(2)}) collective-permute-start(f32[27,2048]{1,0:T(8,128)} %get-tuple-element.22), channel_id=1, source_target_pairs={{16,0},{32,16},{48,32},{64,48},{80,64},{96,80},{112,96},{128,112},... | collective-permute-start | bytes 663560 | tf_op jit(solution)/shard_map/ppermute | solution.py:341
  60.9 1.7 %collective-permute-done.above_ref = f32[27,2048]{1,0:T(8,128)S(1)} collective-permute-done((f32[27,2048]{1,0:T(8,128)}, f32[27,2048]{1,0:T(8,128)S(1)}, u32[]{:S(2)}, u32[]{:S(2)}) %collective-permute-start) | collective-permute-done | bytes 221216 | tf_op jit(solution)/shard_map/ppermute | solution.py:340
  62.6 0.7 copy-done.11
  63.3 3.7 %collective-permute-done.1.below_ref = f32[27,2048]{1,0:T(8,128)} collective-permute-done((f32[27,2048]{1,0:T(8,128)}, f32[27,2048]{1,0:T(8,128)}, u32[]{:S(2)}, u32[]{:S(2)}) %collective-permute-start.1) | collective-permute-done | bytes 221216 | tf_op jit(solution)/shard_map/ppermute | solution.py:341
  67.0 0.0 all-to-all-done.3
  67.0 0.0 copy-done
  67.0 0.0 copy-done.1
  67.0 0.0 copy-done.7
  67.0 0.0 copy-done.8
  67.0 5.8 %first_step.1 = (f32[6,3,16,2048]{3,2,1,0:T(8,128)}, f32[16,6,16,128]{3,2,1,0:T(8,128)S(1)}, f32[24,2048]{1,0:T(8,128)S(1)}, f32[24,2048]{1,0:T(8,128)S(1)}, f32...) custom-call(s32[1]{0:T(128)} %bitcast.first_ref, s32[6]{0:T(128)S(1)} %copy-done.7, f32[4]{0:T(128)S(1)} %copy-done.8, ...), custom_call_target="tpu_custom_call" | custom-call | tf_op jit(solution)/shard_map/first_step/pallas_call | solution.py:192
  72.8 0.9 copy-done.3
  73.7 0.7 copy-done.9
  74.3 0.7 copy-done.10
  75.0 4.5 %all-to-all-start.4 = ((f32[4,4,6,16,128]{4,3,2,1,0:T(8,128)}), f32[4,4,6,16,128]{4,3,2,1,0:T(8,128)S(1)}, u32[]{:S(2)}, u32[]{:S(2)}) async-start(f32[4,4,6,16,128]{4,3,2,1,0:T(8,128)} %bitcast.8), calls=%async_computation.4 | async-start | bytes 1572864 | tf_op jit(solution)/shard_map/all_to_all | solution.py:391
  79.5 2.0 %collective-permute-start.2 = (f32[24,2048]{1,0:T(8,128)}, f32[24,2048]{1,0:T(8,128)S(1)}, u32[]{:S(2)}, u32[]{:S(2)}) collective-permute-start(f32[24,2048]{1,0:T(8,128)} %copy-done.10), channel_id=1, source_target_pairs={{0,16},{16,32},{32,48},{48,64},{64,80},{80,96},{96,112},{112,128},... | collective-permute-start | bytes 589832 | tf_op jit(solution)/shard_map/ppermute | solution.py:340
  81.5 0.0 copy-start.4
  81.5 0.0 copy-start.5
  81.5 0.0 copy-start.6
  81.5 3.4 %collective-permute-start.3 = (f32[24,2048]{1,0:T(8,128)}, f32[24,2048]{1,0:T(8,128)S(1)}, u32[]{:S(2)}, u32[]{:S(2)}) collective-permute-start(f32[24,2048]{1,0:T(8,128)} %copy-done.9), channel_id=1, source_target_pairs={{16,0},{32,16},{48,32},{64,48},{80,64},{96,80},{112,96},{128,112},... | collective-permute-start | bytes 589832 | tf_op jit(solution)/shard_map/ppermute | solution.py:341
  84.9 0.0 collective-permute-done.2.mid_above_ref.above_ref
  84.9 4.9 %collective-permute-done.3.mid_below_ref.below_ref = f32[24,2048]{1,0:T(8,128)S(1)} collective-permute-done((f32[24,2048]{1,0:T(8,128)}, f32[24,2048]{1,0:T(8,128)S(1)}, u32[]{:S(2)}, u32[]{:S(2)}) %collective-permute-start.3) | collective-permute-done | bytes 196640 | tf_op jit(solution)/shard_map/ppermute | solution.py:341
  89.8 0.6 all-to-all-done.4.parts_ref
  90.4 11.3 %all_to_all.43.parts_ref = f32[4,6,16,128]{3,2,1,0:T(8,128)S(1)} all-to-all(f32[4,6,16,128]{3,2,1,0:T(8,128)S(1)} %add_parts.3), channel_id=1, replica_groups=mesh['yl'=2,'z'=8,'core'=2,'x'=4,'yh'=4] {'yh'}, dimensions={0} | all-to-all | bytes 393216 | tf_op jit(solution)/shard_map/all_to_all | solution.py:391
  101.7 10.3 %all_to_all.44.value_ref = f32[4,6,16,128]{3,2,1,0:T(8,128)S(1)} all-to-all(f32[4,6,16,128]{3,2,1,0:T(8,128)S(1)} %owner.3), channel_id=1, replica_groups=mesh['yl'=2,'z'=8,'core'=2,'x'=4,'yh'=4] {'yh'}, dimensions={0} | all-to-all | bytes 393216 | tf_op jit(solution)/shard_map/all_to_all | solution.py:391
  112.0 0.9 copies.3
  113.0 3.5 %all-to-all-start.7 = ((f32[4,4,6,16,128]{4,3,2,1,0:T(8,128)}), f32[4,4,6,16,128]{4,3,2,1,0:T(8,128)S(1)}, u32[]{:S(2)}, u32[]{:S(2)}) async-start(f32[4,4,6,16,128]{4,3,2,1,0:T(8,128)} %copies.3), calls=%async_computation.7 | async-start | bytes 1572864 | tf_op jit(solution)/shard_map/all_to_all | solution.py:391
  116.5 0.0 copy-done.4
  116.5 0.0 copy-done.5
  116.5 0.0 copy-done.6
  116.5 1.5 %solute_step.1 = (f32[3,16,2048]{2,1,0:T(8,128)S(1)}, f32[3,16,2048]{2,1,0:T(8,128)S(1)}) custom-call(f32[3,16,2048]{2,1,0:T(8,128)S(1)} %copy-done.1, f32[3,16,2048]{2,1,0:T(8,128)S(1)} %copy-done.4, f32[9,2048]{1,0:T(8,128)S(1)} %copy-done.5, f32[9,2048]{1,0:T(8,128)S(1)} %copy-done.6, f32[24,2048]{1,0:T(8,128)S(1)} %collective-permute-done.2.mid_above_ref.above_ref, ...), custom_call_target="tpu_custom_call" | custom-call | tf_op jit(solution)/shard_map/solute_step/pallas_call | solution.py:257
  118.0 6.8 %all-to-all-done.7 = f32[4,4,6,16,128]{4,3,2,1,0:T(8,128)S(1)} async-done(((f32[4,4,6,16,128]{4,3,2,1,0:T(8,128)}), f32[4,4,6,16,128]{4,3,2,1,0:T(8,128)S(1)}, u32[]{:S(2)}, u32[]{:S(2)}) %all-to-all-start.7) | async-done | bytes 786464 | tf_op jit(solution)/shard_map/all_to_all | solution.py:391
  124.8 0.1 second_potential.1
  124.8 11.8 %collective-permute-start.4 = (f32[3,2048]{1,0:T(4,128)S(1)}, f32[3,2048]{1,0:T(4,128)S(1)}, u32[]{:S(2)}, u32[]{:S(2)}) collective-permute-start(f32[3,2048]{1,0:T(4,128)S(1)} %get-tuple-element.36), channel_id=1, source_target_pairs={{0,16},{16,32},{32,48},{48,64},{64,80},{80,96},{96,112},{112,128},... | collective-permute-start | bytes 73736 | tf_op jit(solution)/shard_map/ppermute | solution.py:340
  136.7 1.9 %collective-permute-start.5 = (f32[3,2048]{1,0:T(4,128)S(1)}, f32[3,2048]{1,0:T(4,128)S(1)}, u32[]{:S(2)}, u32[]{:S(2)}) collective-permute-start(f32[3,2048]{1,0:T(4,128)S(1)} %get-tuple-element.37), channel_id=1, source_target_pairs={{16,0},{32,16},{48,32},{64,48},{80,64},{96,80},{112,96},{128,112},... | collective-permute-start | bytes 73736 | tf_op jit(solution)/shard_map/ppermute | solution.py:341
  138.6 0.0 copy-start.2
  138.6 1.7 %copy-done.2 = f32[6,3,16,2048]{3,2,1,0:T(8,128)S(1)} copy-done((f32[6,3,16,2048]{3,2,1,0:T(8,128)S(1)}, f32[6,3,16,2048]{3,2,1,0:T(8,128)}, u32[]{:S(2)}) %copy-start.2) | copy-done | bytes 2359320
  140.2 4.2 %second_step.1 = f32[6,3,16,2048]{3,2,1,0:T(8,128)} custom-call(s32[6]{0:T(128)S(1)} %copy-done.7, f32[4]{0:T(128)S(1)} %copy-done.8, f32[6,3,16,2048]{3,2,1,0:T(8,128)S(1)} %copy-done.2, f32[3,16,2048]{2,1,0:T(8,128)S(1)} %get-tuple-element.32.solute_ref, f32[16,6,16,128]{3,2,1,0:T(8,128)S(1)} %bitcast.6, ...), custom_call_target="tpu_custom_call" | custom-call | flops 20000000 | bytes 10000000 | tf_op jit(solution)/shard_map/second_step/pallas_call | solution.py:303
  144.5 0.0 collective-permute-done.4.above_ref
  144.5 0.0 collective-permute-done.5.below_ref
  144.5 1.1 solute_end.1
  (11 shorter events, 0.1 us)
Async XLA Ops:
  17.8 49.2 %copy-start = (f32[6,3,16,2048]{3,2,1,0:T(8,128)S(1)}, f32[6,3,16,2048]{3,2,1,0:T(8,128)}, u32[]{:S(2)}) copy-start(f32[6,3,16,2048]{3,2,1,0:T(8,128)} %noise_ref.3) | copy-start | bytes 7077892
  17.8 49.2 %copy-start.1 = (f32[3,16,2048]{2,1,0:T(8,128)S(1)}, f32[3,16,2048]{2,1,0:T(8,128)}, u32[]{:S(2)}) copy-start(f32[3,16,2048]{2,1,0:T(8,128)} %solute_ref.5) | copy-start | bytes 1179652
  17.8 49.2 %copy-start.7 = (s32[6]{0:T(128)S(1)}, s32[6]{0:T(128)}, u32[]{:S(2)}) copy-start(s32[6]{0:T(128)} %group_ref.3) | copy-start | bytes 76
  17.8 49.2 %copy-start.8 = (f32[4]{0:T(128)S(1)}, f32[4]{0:T(128)}, u32[]{:S(2)}) copy-start(f32[4]{0:T(128)} %mobility_ref.3) | copy-start | bytes 52
  47.0 19.9 %all-to-all-start.3 = ((f32[4,4,6,16,128]{4,3,2,1,0:T(8,128)}), f32[4,4,6,16,128]{4,3,2,1,0:T(8,128)S(1)}, u32[]{:S(2)}, u32[]{:S(2)}) async-start(f32[4,4,6,16,128]{4,3,2,1,0:T(8,128)} %copies.2), calls=%async_computation.3 | async-start | bytes 1572864 | tf_op jit(solution)/shard_map/all_to_all | solution.py:391
  50.5 12.0 %collective-permute-start = (f32[27,2048]{1,0:T(8,128)}, f32[27,2048]{1,0:T(8,128)S(1)}, u32[]{:S(2)}, u32[]{:S(2)}) collective-permute-start(f32[27,2048]{1,0:T(8,128)} %get-tuple-element.21), channel_id=1, source_target_pairs={{0,16},{16,32},{32,48},{48,64},{64,80},{80,96},{96,112},{112,128},... | collective-permute-start | bytes 663560 | tf_op jit(solution)/shard_map/ppermute | solution.py:340
  59.0 8.0 %collective-permute-start.1 = (f32[27,2048]{1,0:T(8,128)}, f32[27,2048]{1,0:T(8,128)}, u32[]{:S(2)}, u32[]{:S(2)}) collective-permute-start(f32[27,2048]{1,0:T(8,128)} %get-tuple-element.22), channel_id=1, source_target_pairs={{16,0},{32,16},{48,32},{64,48},{80,64},{96,80},{112,96},{128,112},... | collective-permute-start | bytes 663560 | tf_op jit(solution)/shard_map/ppermute | solution.py:341
  62.6 0.7 copy-start.11
  72.8 0.9 copy-start.3
  73.7 0.7 copy-start.9
  74.3 0.7 copy-start.10
  75.0 15.4 %all-to-all-start.4 = ((f32[4,4,6,16,128]{4,3,2,1,0:T(8,128)}), f32[4,4,6,16,128]{4,3,2,1,0:T(8,128)S(1)}, u32[]{:S(2)}, u32[]{:S(2)}) async-start(f32[4,4,6,16,128]{4,3,2,1,0:T(8,128)} %bitcast.8), calls=%async_computation.4 | async-start | bytes 1572864 | tf_op jit(solution)/shard_map/all_to_all | solution.py:391
  79.5 5.4 %collective-permute-start.2 = (f32[24,2048]{1,0:T(8,128)}, f32[24,2048]{1,0:T(8,128)S(1)}, u32[]{:S(2)}, u32[]{:S(2)}) collective-permute-start(f32[24,2048]{1,0:T(8,128)} %copy-done.10), channel_id=1, source_target_pairs={{0,16},{16,32},{32,48},{48,64},{64,80},{80,96},{96,112},{112,128},... | collective-permute-start | bytes 589832 | tf_op jit(solution)/shard_map/ppermute | solution.py:340
  81.5 35.0 %copy-start.4 = (f32[3,16,2048]{2,1,0:T(8,128)S(1)}, f32[3,16,2048]{2,1,0:T(8,128)}, u32[]{:S(2)}) copy-start(f32[3,16,2048]{2,1,0:T(8,128)} %get-tuple-element.24.middle_ref) | copy-start | bytes 1179652
  81.5 35.0 %copy-start.5 = (f32[9,2048]{1,0:T(8,128)S(1)}, f32[9,2048]{1,0:T(8,128)}, u32[]{:S(2)}) copy-start(f32[9,2048]{1,0:T(8,128)} %get-tuple-element.25.above_ref) | copy-start | bytes 221188
  81.5 35.0 %copy-start.6 = (f32[9,2048]{1,0:T(8,128)S(1)}, f32[9,2048]{1,0:T(8,128)}, u32[]{:S(2)}) copy-start(f32[9,2048]{1,0:T(8,128)} %get-tuple-element.26.below_ref) | copy-start | bytes 221188
  81.5 8.3 %collective-permute-start.3 = (f32[24,2048]{1,0:T(8,128)}, f32[24,2048]{1,0:T(8,128)S(1)}, u32[]{:S(2)}, u32[]{:S(2)}) collective-permute-start(f32[24,2048]{1,0:T(8,128)} %copy-done.9), channel_id=1, source_target_pairs={{16,0},{32,16},{48,32},{64,48},{80,64},{96,80},{112,96},{128,112},... | collective-permute-start | bytes 589832 | tf_op jit(solution)/shard_map/ppermute | solution.py:341
  113.0 11.8 %all-to-all-start.7 = ((f32[4,4,6,16,128]{4,3,2,1,0:T(8,128)}), f32[4,4,6,16,128]{4,3,2,1,0:T(8,128)S(1)}, u32[]{:S(2)}, u32[]{:S(2)}) async-start(f32[4,4,6,16,128]{4,3,2,1,0:T(8,128)} %copies.3), calls=%async_computation.7 | async-start | bytes 1572864 | tf_op jit(solution)/shard_map/all_to_all | solution.py:391
  124.8 19.6 %collective-permute-start.4 = (f32[3,2048]{1,0:T(4,128)S(1)}, f32[3,2048]{1,0:T(4,128)S(1)}, u32[]{:S(2)}, u32[]{:S(2)}) collective-permute-start(f32[3,2048]{1,0:T(4,128)S(1)} %get-tuple-element.36), channel_id=1, source_target_pairs={{0,16},{16,32},{32,48},{48,64},{64,80},{80,96},{96,112},{112,128},... | collective-permute-start | bytes 73736 | tf_op jit(solution)/shard_map/ppermute | solution.py:340
  136.7 7.8 %collective-permute-start.5 = (f32[3,2048]{1,0:T(4,128)S(1)}, f32[3,2048]{1,0:T(4,128)S(1)}, u32[]{:S(2)}, u32[]{:S(2)}) collective-permute-start(f32[3,2048]{1,0:T(4,128)S(1)} %get-tuple-element.37), channel_id=1, source_target_pairs={{16,0},{32,16},{48,32},{64,48},{80,64},{96,80},{112,96},{128,112},... | collective-permute-start | bytes 73736 | tf_op jit(solution)/shard_map/ppermute | solution.py:341
  138.6 1.7 %copy-start.2 = (f32[6,3,16,2048]{3,2,1,0:T(8,128)S(1)}, f32[6,3,16,2048]{3,2,1,0:T(8,128)}, u32[]{:S(2)}) copy-start(f32[6,3,16,2048]{3,2,1,0:T(8,128)} %get-tuple-element.23.old_ref) | copy-start | bytes 7077892

commit v11 on v10

--- a/solution.py
+++ b/solution.py
@@ -201,8 +201,8 @@
         + [whole(edge, COLS)] * 2
         + [whole(*solute.shape)]
         + [whole(3 * PLANES, COLS)] * 2,
-        out_shape=[hbm(*noise.shape), shape(*sums.shape)]
-        + [shape(edge, COLS)] * 2
+        out_shape=[hbm(*noise.shape), hbm(*sums.shape)]
+        + [hbm(edge, COLS)] * 2
         + [hbm(*solute.shape)]
         + [hbm(3 * PLANES, COLS)] * 2,
         scratch_shapes=[pltpu.VMEM(solute.shape, F32)] * 2,

time: 146 us -> 144 us (0.986)
  local copies, waits for them, and re-layouts: 4.62 us -> 2.4 us
    unnamed x24 -> x18, local copies, waits for them, and re-layouts: 4.62 us -> 2.4 us
where the time goes in v11:
time: 144 us
  blocking collectives  63 us (44%)
  starting transfers between devices  40.9 us (28%)
  Pallas kernels  19 us (13%)
  waiting for transfers between devices  17.6 us (12%)
  local copies, waits for them, and re-layouts  2.4 us (2%)
    all_to_all x5, blocking collectives, dealt(): return lax.all_to_all(blocks, axis, 0, 0, tiled=True)  63 us
    ppermute x3, starting transfers between devices, exchange(): lax.ppermute(to_next, SPACE, [(i, (i + 1) % count) for i in range(count)])  22.2 us
    all_to_all x3, starting transfers between devices, dealt(): return lax.all_to_all(blocks, axis, 0, 0, tiled=True)  11.5 us
    ppermute x3, waiting for transfers between devices, exchange(): lax.ppermute(to_prev, SPACE, [((i + 1) % count, i) for i in range(count)])  8.57 us
    all_to_all x3, waiting for transfers between devices, dealt(): return lax.all_to_all(blocks, axis, 0, 0, tiled=True)  7.33 us
    ppermute x3, starting transfers between devices, exchange(): lax.ppermute(to_prev, SPACE, [((i + 1) % count, i) for i in range(count)])  7.21 us
    pallas_call x1, Pallas kernels, call_first_step(): pl.pallas_call(first_step, grid=(GRAINS,), in_specs=[smem(), smem(), smem...  6.17 us
    pallas_call x1, Pallas kernels, call_second_step(): pl.pallas_call(second_step, grid=(GRAINS,), in_specs=[smem(), smem(), gra...  4.21 us
  transfers between devices with their start and end apart: 9, of which 5 were waited for; matrix products, arithmetic and copies ran while one was open for 0% of the time, Pallas kernels for 4%

profile of v11, /device:TPU:1, one launch (start us, length us, event | category | flops | bytes accessed | tf_op | source)
XLA Modules:
  0.0 143.7 jit_solution(16878098792421422182)
XLA Ops:
  0.6 4.0 %first_sums.1 = (f32[16,6,16,128]{3,2,1,0:T(8,128)}, f32[27,2048]{1,0:T(8,128)}, f32[27,2048]{1,0:T(8,128)}) custom-call(s32[1]{0:T(128)} %bitcast.first_ref, f32[6,3,16,2048]{3,2,1,0:T(8,128)} %noise_ref.3, s32[3,16,2048]{2,1,0:T(8,128)} %ids_ref.3, f32[3,16,2048]{2,1,0:T(8,128)} %solute_ref.5), custom_call_target="tpu_custom_call" | custom-call | tf_op jit(solution)/shard_map/first_sums/pallas_call | solution.py:88
  4.6 13.2 %all_to_all.40.parts_ref = f32[4,4,6,16,128]{4,3,2,1,0:T(8,128)S(1)} all-to-all(f32[4,4,6,16,128]{4,3,2,1,0:T(8,128)} %bitcast.9), channel_id=1, replica_groups=mesh['yl'=2,'z'=8,'core'=2,'x'=4,'yh'=4] {'x'}, dimensions={0} | all-to-all | bytes 1572864 | tf_op jit(solution)/shard_map/all_to_all | solution.py:391
  17.8 0.0 copy-start.1
  17.8 0.0 copy-start.6
  17.8 0.0 copy-start.7
  17.9 17.9 %all_to_all.41.parts_ref = f32[4,6,16,128]{3,2,1,0:T(8,128)S(1)} all-to-all(f32[4,6,16,128]{3,2,1,0:T(8,128)S(1)} %add_parts.2), channel_id=1, replica_groups=mesh['yl'=2,'z'=8,'core'=2,'x'=4,'yh'=4] {'yh'}, dimensions={0} | all-to-all | bytes 393216 | tf_op jit(solution)/shard_map/all_to_all | solution.py:391
  35.8 10.4 %all_to_all.42.value_ref = f32[4,6,16,128]{3,2,1,0:T(8,128)S(1)} all-to-all(f32[4,6,16,128]{3,2,1,0:T(8,128)S(1)} %owner.2), channel_id=1, replica_groups=mesh['yl'=2,'z'=8,'core'=2,'x'=4,'yh'=4] {'yh'}, dimensions={0} | all-to-all | bytes 393216 | tf_op jit(solution)/shard_map/all_to_all | solution.py:391
  46.1 0.9 copies.2
  47.0 3.5 %all-to-all-start.3 = ((f32[4,4,6,16,128]{4,3,2,1,0:T(8,128)}), f32[4,4,6,16,128]{4,3,2,1,0:T(8,128)S(1)}, u32[]{:S(2)}, u32[]{:S(2)}) async-start(f32[4,4,6,16,128]{4,3,2,1,0:T(8,128)} %copies.2), calls=%async_computation.3 | async-start | bytes 1572864 | tf_op jit(solution)/shard_map/all_to_all | solution.py:391
  50.5 8.4 %collective-permute-start = (f32[27,2048]{1,0:T(8,128)}, f32[27,2048]{1,0:T(8,128)S(1)}, u32[]{:S(2)}, u32[]{:S(2)}) collective-permute-start(f32[27,2048]{1,0:T(8,128)} %get-tuple-element.21), channel_id=1, source_target_pairs={{0,16},{16,32},{32,48},{48,64},{64,80},{80,96},{96,112},{112,128},... | collective-permute-start | bytes 663560 | tf_op jit(solution)/shard_map/ppermute | solution.py:340
  59.0 1.9 %collective-permute-start.1 = (f32[27,2048]{1,0:T(8,128)}, f32[27,2048]{1,0:T(8,128)}, u32[]{:S(2)}, u32[]{:S(2)}) collective-permute-start(f32[27,2048]{1,0:T(8,128)} %get-tuple-element.22), channel_id=1, source_target_pairs={{16,0},{32,16},{48,32},{64,48},{80,64},{96,80},{112,96},{128,112},... | collective-permute-start | bytes 663560 | tf_op jit(solution)/shard_map/ppermute | solution.py:341
  60.9 1.7 %collective-permute-done.above_ref = f32[27,2048]{1,0:T(8,128)S(1)} collective-permute-done((f32[27,2048]{1,0:T(8,128)}, f32[27,2048]{1,0:T(8,128)S(1)}, u32[]{:S(2)}, u32[]{:S(2)}) %collective-permute-start) | collective-permute-done | bytes 221216 | tf_op jit(solution)/shard_map/ppermute | solution.py:340
  62.6 0.0 copy-start.8
  62.6 0.7 copy-done.8
  63.3 3.7 %collective-permute-done.1.below_ref = f32[27,2048]{1,0:T(8,128)} collective-permute-done((f32[27,2048]{1,0:T(8,128)}, f32[27,2048]{1,0:T(8,128)}, u32[]{:S(2)}, u32[]{:S(2)}) %collective-permute-start.1) | collective-permute-done | bytes 221216 | tf_op jit(solution)/shard_map/ppermute | solution.py:341
  67.0 0.0 all-to-all-done.3
  67.0 0.0 copy-done
  67.0 0.0 copy-done.1
  67.0 0.0 copy-done.6
  67.0 0.0 copy-done.7
  67.0 6.2 %first_step.1 = (f32[6,3,16,2048]{3,2,1,0:T(8,128)}, f32[16,6,16,128]{3,2,1,0:T(8,128)}, f32[24,2048]{1,0:T(8,128)}, f32[24,2048]{1,0:T(8,128)}, f32[3,16,2048]{...) custom-call(s32[1]{0:T(128)} %bitcast.first_ref, s32[6]{0:T(128)S(1)} %copy-done.6, f32[4]{0:T(128)S(1)} %copy-done.7, ...), custom_call_target="tpu_custom_call" | custom-call | tf_op jit(solution)/shard_map/first_step/pallas_call | solution.py:192
  73.2 4.5 %all-to-all-start.4 = ((f32[4,4,6,16,128]{4,3,2,1,0:T(8,128)}), f32[4,4,6,16,128]{4,3,2,1,0:T(8,128)S(1)}, u32[]{:S(2)}, u32[]{:S(2)}) async-start(f32[4,4,6,16,128]{4,3,2,1,0:T(8,128)} %bitcast.8), calls=%async_computation.4 | async-start | bytes 1572864 | tf_op jit(solution)/shard_map/all_to_all | solution.py:391
  77.6 2.0 %collective-permute-start.2 = (f32[24,2048]{1,0:T(8,128)}, f32[24,2048]{1,0:T(8,128)S(1)}, u32[]{:S(2)}, u32[]{:S(2)}) collective-permute-start(f32[24,2048]{1,0:T(8,128)} %get-tuple-element.28), channel_id=1, source_target_pairs={{0,16},{16,32},{32,48},{48,64},{64,80},{80,96},{96,112},{112,128},... | collective-permute-start | bytes 589832 | tf_op jit(solution)/shard_map/ppermute | solution.py:340
  79.7 0.0 copy-start.3
  79.7 0.0 copy-start.4
  79.7 0.0 copy-start.5
  79.7 3.4 %collective-permute-start.3 = (f32[24,2048]{1,0:T(8,128)}, f32[24,2048]{1,0:T(8,128)S(1)}, u32[]{:S(2)}, u32[]{:S(2)}) collective-permute-start(f32[24,2048]{1,0:T(8,128)} %get-tuple-element.29), channel_id=1, source_target_pairs={{16,0},{32,16},{48,32},{64,48},{80,64},{96,80},{112,96},{128,112},... | collective-permute-start | bytes 589832 | tf_op jit(solution)/shard_map/ppermute | solution.py:341
  83.1 0.0 collective-permute-done.2.mid_above_ref.above_ref
  83.1 4.9 %collective-permute-done.3.mid_below_ref.below_ref = f32[24,2048]{1,0:T(8,128)S(1)} collective-permute-done((f32[24,2048]{1,0:T(8,128)}, f32[24,2048]{1,0:T(8,128)S(1)}, u32[]{:S(2)}, u32[]{:S(2)}) %collective-permute-start.3) | collective-permute-done | bytes 196640 | tf_op jit(solution)/shard_map/ppermute | solution.py:341
  88.0 0.6 all-to-all-done.4.parts_ref
  88.6 11.3 %all_to_all.43.parts_ref = f32[4,6,16,128]{3,2,1,0:T(8,128)S(1)} all-to-all(f32[4,6,16,128]{3,2,1,0:T(8,128)S(1)} %add_parts.3), channel_id=1, replica_groups=mesh['yl'=2,'z'=8,'core'=2,'x'=4,'yh'=4] {'yh'}, dimensions={0} | all-to-all | bytes 393216 | tf_op jit(solution)/shard_map/all_to_all | solution.py:391
  99.9 10.3 %all_to_all.44.value_ref = f32[4,6,16,128]{3,2,1,0:T(8,128)S(1)} all-to-all(f32[4,6,16,128]{3,2,1,0:T(8,128)S(1)} %owner.3), channel_id=1, replica_groups=mesh['yl'=2,'z'=8,'core'=2,'x'=4,'yh'=4] {'yh'}, dimensions={0} | all-to-all | bytes 393216 | tf_op jit(solution)/shard_map/all_to_all | solution.py:391
  110.2 0.9 copies.3
  111.1 3.5 %all-to-all-start.7 = ((f32[4,4,6,16,128]{4,3,2,1,0:T(8,128)}), f32[4,4,6,16,128]{4,3,2,1,0:T(8,128)S(1)}, u32[]{:S(2)}, u32[]{:S(2)}) async-start(f32[4,4,6,16,128]{4,3,2,1,0:T(8,128)} %copies.3), calls=%async_computation.7 | async-start | bytes 1572864 | tf_op jit(solution)/shard_map/all_to_all | solution.py:391
  114.6 0.0 copy-done.3
  114.6 0.0 copy-done.4
  114.6 0.0 copy-done.5
  114.6 1.5 %solute_step.1 = (f32[3,16,2048]{2,1,0:T(8,128)S(1)}, f32[3,16,2048]{2,1,0:T(8,128)S(1)}) custom-call(f32[3,16,2048]{2,1,0:T(8,128)S(1)} %copy-done.1, f32[3,16,2048]{2,1,0:T(8,128)S(1)} %copy-done.3, f32[9,2048]{1,0:T(8,128)S(1)} %copy-done.4, f32[9,2048]{1,0:T(8,128)S(1)} %copy-done.5, f32[24,2048]{1,0:T(8,128)S(1)} %collective-permute-done.2.mid_above_ref.above_ref, ...), custom_call_target="tpu_custom_call" | custom-call | tf_op jit(solution)/shard_map/solute_step/pallas_call | solution.py:257
  116.2 6.8 %all-to-all-done.7 = f32[4,4,6,16,128]{4,3,2,1,0:T(8,128)S(1)} async-done(((f32[4,4,6,16,128]{4,3,2,1,0:T(8,128)}), f32[4,4,6,16,128]{4,3,2,1,0:T(8,128)S(1)}, u32[]{:S(2)}, u32[]{:S(2)}) %all-to-all-start.7) | async-done | bytes 786464 | tf_op jit(solution)/shard_map/all_to_all | solution.py:391
  122.9 0.1 second_potential.1
  123.0 11.8 %collective-permute-start.4 = (f32[3,2048]{1,0:T(4,128)S(1)}, f32[3,2048]{1,0:T(4,128)S(1)}, u32[]{:S(2)}, u32[]{:S(2)}) collective-permute-start(f32[3,2048]{1,0:T(4,128)S(1)} %get-tuple-element.36), channel_id=1, source_target_pairs={{0,16},{16,32},{32,48},{48,64},{64,80},{80,96},{96,112},{112,128},... | collective-permute-start | bytes 73736 | tf_op jit(solution)/shard_map/ppermute | solution.py:340
  134.8 1.9 %collective-permute-start.5 = (f32[3,2048]{1,0:T(4,128)S(1)}, f32[3,2048]{1,0:T(4,128)S(1)}, u32[]{:S(2)}, u32[]{:S(2)}) collective-permute-start(f32[3,2048]{1,0:T(4,128)S(1)} %get-tuple-element.37), channel_id=1, source_target_pairs={{16,0},{32,16},{48,32},{64,48},{80,64},{96,80},{112,96},{128,112},... | collective-permute-start | bytes 73736 | tf_op jit(solution)/shard_map/ppermute | solution.py:341
  136.7 0.0 copy-start.2
  136.7 1.7 %copy-done.2 = f32[6,3,16,2048]{3,2,1,0:T(8,128)S(1)} copy-done((f32[6,3,16,2048]{3,2,1,0:T(8,128)S(1)}, f32[6,3,16,2048]{3,2,1,0:T(8,128)}, u32[]{:S(2)}) %copy-start.2) | copy-done | bytes 2359320
  138.4 4.2 %second_step.1 = f32[6,3,16,2048]{3,2,1,0:T(8,128)} custom-call(s32[6]{0:T(128)S(1)} %copy-done.6, f32[4]{0:T(128)S(1)} %copy-done.7, f32[6,3,16,2048]{3,2,1,0:T(8,128)S(1)} %copy-done.2, f32[3,16,2048]{2,1,0:T(8,128)S(1)} %get-tuple-element.32.solute_ref, f32[16,6,16,128]{3,2,1,0:T(8,128)S(1)} %bitcast.6, ...), custom_call_target="tpu_custom_call" | custom-call | flops 20000000 | bytes 10000000 | tf_op jit(solution)/shard_map/second_step/pallas_call | solution.py:303
  142.6 0.0 collective-permute-done.4.above_ref
  142.6 0.0 collective-permute-done.5.below_ref
  142.6 1.1 solute_end.1
  (5 shorter events, 0.1 us)
Async XLA Ops:
  17.8 49.2 %copy-start = (f32[6,3,16,2048]{3,2,1,0:T(8,128)S(1)}, f32[6,3,16,2048]{3,2,1,0:T(8,128)}, u32[]{:S(2)}) copy-start(f32[6,3,16,2048]{3,2,1,0:T(8,128)} %noise_ref.3) | copy-start | bytes 7077892
  17.8 49.2 %copy-start.1 = (f32[3,16,2048]{2,1,0:T(8,128)S(1)}, f32[3,16,2048]{2,1,0:T(8,128)}, u32[]{:S(2)}) copy-start(f32[3,16,2048]{2,1,0:T(8,128)} %solute_ref.5) | copy-start | bytes 1179652
  17.8 49.2 %copy-start.6 = (s32[6]{0:T(128)S(1)}, s32[6]{0:T(128)}, u32[]{:S(2)}) copy-start(s32[6]{0:T(128)} %group_ref.3) | copy-start | bytes 76
  17.8 49.2 %copy-start.7 = (f32[4]{0:T(128)S(1)}, f32[4]{0:T(128)}, u32[]{:S(2)}) copy-start(f32[4]{0:T(128)} %mobility_ref.3) | copy-start | bytes 52
  47.0 19.9 %all-to-all-start.3 = ((f32[4,4,6,16,128]{4,3,2,1,0:T(8,128)}), f32[4,4,6,16,128]{4,3,2,1,0:T(8,128)S(1)}, u32[]{:S(2)}, u32[]{:S(2)}) async-start(f32[4,4,6,16,128]{4,3,2,1,0:T(8,128)} %copies.2), calls=%async_computation.3 | async-start | bytes 1572864 | tf_op jit(solution)/shard_map/all_to_all | solution.py:391
  50.5 12.0 %collective-permute-start = (f32[27,2048]{1,0:T(8,128)}, f32[27,2048]{1,0:T(8,128)S(1)}, u32[]{:S(2)}, u32[]{:S(2)}) collective-permute-start(f32[27,2048]{1,0:T(8,128)} %get-tuple-element.21), channel_id=1, source_target_pairs={{0,16},{16,32},{32,48},{48,64},{64,80},{80,96},{96,112},{112,128},... | collective-permute-start | bytes 663560 | tf_op jit(solution)/shard_map/ppermute | solution.py:340
  59.0 8.0 %collective-permute-start.1 = (f32[27,2048]{1,0:T(8,128)}, f32[27,2048]{1,0:T(8,128)}, u32[]{:S(2)}, u32[]{:S(2)}) collective-permute-start(f32[27,2048]{1,0:T(8,128)} %get-tuple-element.22), channel_id=1, source_target_pairs={{16,0},{32,16},{48,32},{64,48},{80,64},{96,80},{112,96},{128,112},... | collective-permute-start | bytes 663560 | tf_op jit(solution)/shard_map/ppermute | solution.py:341
  62.6 0.7 copy-start.8
  73.2 15.4 %all-to-all-start.4 = ((f32[4,4,6,16,128]{4,3,2,1,0:T(8,128)}), f32[4,4,6,16,128]{4,3,2,1,0:T(8,128)S(1)}, u32[]{:S(2)}, u32[]{:S(2)}) async-start(f32[4,4,6,16,128]{4,3,2,1,0:T(8,128)} %bitcast.8), calls=%async_computation.4 | async-start | bytes 1572864 | tf_op jit(solution)/shard_map/all_to_all | solution.py:391
  77.6 5.4 %collective-permute-start.2 = (f32[24,2048]{1,0:T(8,128)}, f32[24,2048]{1,0:T(8,128)S(1)}, u32[]{:S(2)}, u32[]{:S(2)}) collective-permute-start(f32[24,2048]{1,0:T(8,128)} %get-tuple-element.28), channel_id=1, source_target_pairs={{0,16},{16,32},{32,48},{48,64},{64,80},{80,96},{96,112},{112,128},... | collective-permute-start | bytes 589832 | tf_op jit(solution)/shard_map/ppermute | solution.py:340
  79.7 35.0 %copy-start.3 = (f32[3,16,2048]{2,1,0:T(8,128)S(1)}, f32[3,16,2048]{2,1,0:T(8,128)}, u32[]{:S(2)}) copy-start(f32[3,16,2048]{2,1,0:T(8,128)} %get-tuple-element.24.middle_ref) | copy-start | bytes 1179652
  79.7 35.0 %copy-start.4 = (f32[9,2048]{1,0:T(8,128)S(1)}, f32[9,2048]{1,0:T(8,128)}, u32[]{:S(2)}) copy-start(f32[9,2048]{1,0:T(8,128)} %get-tuple-element.25.above_ref) | copy-start | bytes 221188
  79.7 35.0 %copy-start.5 = (f32[9,2048]{1,0:T(8,128)S(1)}, f32[9,2048]{1,0:T(8,128)}, u32[]{:S(2)}) copy-start(f32[9,2048]{1,0:T(8,128)} %get-tuple-element.26.below_ref) | copy-start | bytes 221188
  79.7 8.3 %collective-permute-start.3 = (f32[24,2048]{1,0:T(8,128)}, f32[24,2048]{1,0:T(8,128)S(1)}, u32[]{:S(2)}, u32[]{:S(2)}) collective-permute-start(f32[24,2048]{1,0:T(8,128)} %get-tuple-element.29), channel_id=1, source_target_pairs={{16,0},{32,16},{48,32},{64,48},{80,64},{96,80},{112,96},{128,112},... | collective-permute-start | bytes 589832 | tf_op jit(solution)/shard_map/ppermute | solution.py:341
  111.1 11.8 %all-to-all-start.7 = ((f32[4,4,6,16,128]{4,3,2,1,0:T(8,128)}), f32[4,4,6,16,128]{4,3,2,1,0:T(8,128)S(1)}, u32[]{:S(2)}, u32[]{:S(2)}) async-start(f32[4,4,6,16,128]{4,3,2,1,0:T(8,128)} %copies.3), calls=%async_computation.7 | async-start | bytes 1572864 | tf_op jit(solution)/shard_map/all_to_all | solution.py:391
  123.0 19.6 %collective-permute-start.4 = (f32[3,2048]{1,0:T(4,128)S(1)}, f32[3,2048]{1,0:T(4,128)S(1)}, u32[]{:S(2)}, u32[]{:S(2)}) collective-permute-start(f32[3,2048]{1,0:T(4,128)S(1)} %get-tuple-element.36), channel_id=1, source_target_pairs={{0,16},{16,32},{32,48},{48,64},{64,80},{80,96},{96,112},{112,128},... | collective-permute-start | bytes 73736 | tf_op jit(solution)/shard_map/ppermute | solution.py:340
  134.8 7.8 %collective-permute-start.5 = (f32[3,2048]{1,0:T(4,128)S(1)}, f32[3,2048]{1,0:T(4,128)S(1)}, u32[]{:S(2)}, u32[]{:S(2)}) collective-permute-start(f32[3,2048]{1,0:T(4,128)S(1)} %get-tuple-element.37), channel_id=1, source_target_pairs={{16,0},{32,16},{48,32},{64,48},{80,64},{96,80},{112,96},{128,112},... | collective-permute-start | bytes 73736 | tf_op jit(solution)/shard_map/ppermute | solution.py:341
  136.7 1.7 %copy-start.2 = (f32[6,3,16,2048]{3,2,1,0:T(8,128)S(1)}, f32[6,3,16,2048]{3,2,1,0:T(8,128)}, u32[]{:S(2)}) copy-start(f32[6,3,16,2048]{3,2,1,0:T(8,128)} %get-tuple-element.23.old_ref) | copy-start | bytes 7077892

commit v12 on v11

--- a/solution.py
+++ b/solution.py
@@ -313,7 +313,7 @@
         compiler_params=params(),
         cost_estimate=pl.CostEstimate(flops=20_000_000, bytes_accessed=10_000_000, transcendentals=0),
         name="second_step",
-    )(groups, mobility, eta, solute, sums, above, below)
+    )(groups, mobility, *from_hbm(eta), solute, sums, above, below)
 
 
 def solute_end(solute_ref, potential_ref, above_ref, below_ref, out_ref):

time: 144 us -> 144 us (level)
  local copies, waits for them, and re-layouts: 2.4 us -> 0.73 us
  Pallas kernels: 19 us -> 20.6 us
    unnamed x18 -> x16, local copies, waits for them, and re-layouts: 2.4 us -> 0.73 us
    pallas_call x1, Pallas kernels: 4.21 us -> 5.79 us  [call_second_step(): pl.pallas_call(second_step, grid=(GRAINS,), in_specs=[smem(), smem(), gra...]
  transfers between devices with their start and end apart: 9 -> 9, of which waited for: 5 -> 5; matrix products, arithmetic and copies ran while one was open for 0% -> 0% of each run, Pallas kernels for 4% -> 5%
where the time goes in v12:
time: 144 us
  blocking collectives  63 us (44%)
  starting transfers between devices  40.9 us (28%)
  Pallas kernels  20.6 us (14%)
  waiting for transfers between devices  17.6 us (12%)
    all_to_all x5, blocking collectives, dealt(): return lax.all_to_all(blocks, axis, 0, 0, tiled=True)  63 us
    ppermute x3, starting transfers between devices, exchange(): lax.ppermute(to_next, SPACE, [(i, (i + 1) % count) for i in range(count)])  22.2 us
    all_to_all x3, starting transfers between devices, dealt(): return lax.all_to_all(blocks, axis, 0, 0, tiled=True)  11.5 us
    ppermute x3, waiting for transfers between devices, exchange(): lax.ppermute(to_prev, SPACE, [((i + 1) % count, i) for i in range(count)])  8.58 us
    all_to_all x3, waiting for transfers between devices, dealt(): return lax.all_to_all(blocks, axis, 0, 0, tiled=True)  7.33 us
    ppermute x3, starting transfers between devices, exchange(): lax.ppermute(to_prev, SPACE, [((i + 1) % count, i) for i in range(count)])  7.21 us
    pallas_call x1, Pallas kernels, call_first_step(): pl.pallas_call(first_step, grid=(GRAINS,), in_specs=[smem(), smem(), smem...  6.19 us
    pallas_call x1, Pallas kernels, call_second_step(): pl.pallas_call(second_step, grid=(GRAINS,), in_specs=[smem(), smem(), gra...  5.79 us
  transfers between devices with their start and end apart: 9, of which 5 were waited for; matrix products, arithmetic and copies ran while one was open for 0% of the time, Pallas kernels for 5%

profile of v12, /device:TPU:1, one launch (start us, length us, event | category | flops | bytes accessed | tf_op | source)
XLA Modules:
  0.0 143.6 jit_solution(5216959159688205450)
XLA Ops:
  0.6 4.0 %first_sums.1 = (f32[16,6,16,128]{3,2,1,0:T(8,128)}, f32[27,2048]{1,0:T(8,128)}, f32[27,2048]{1,0:T(8,128)}) custom-call(s32[1]{0:T(128)} %bitcast.first_ref, f32[6,3,16,2048]{3,2,1,0:T(8,128)} %noise_ref.3, s32[3,16,2048]{2,1,0:T(8,128)} %ids_ref.3, f32[3,16,2048]{2,1,0:T(8,128)} %solute_ref.5), custom_call_target="tpu_custom_call" | custom-call | tf_op jit(solution)/shard_map/first_sums/pallas_call | solution.py:88
  4.6 13.2 %all_to_all.40.parts_ref = f32[4,4,6,16,128]{4,3,2,1,0:T(8,128)S(1)} all-to-all(f32[4,4,6,16,128]{4,3,2,1,0:T(8,128)} %bitcast.9), channel_id=1, replica_groups=mesh['yl'=2,'z'=8,'core'=2,'x'=4,'yh'=4] {'x'}, dimensions={0} | all-to-all | bytes 1572864 | tf_op jit(solution)/shard_map/all_to_all | solution.py:391
  17.8 0.0 copy-start
  17.8 0.0 copy-start.1
  17.8 0.0 copy-start.5
  17.8 0.0 copy-start.6
  17.9 17.9 %all_to_all.41.parts_ref = f32[4,6,16,128]{3,2,1,0:T(8,128)S(1)} all-to-all(f32[4,6,16,128]{3,2,1,0:T(8,128)S(1)} %add_parts.2), channel_id=1, replica_groups=mesh['yl'=2,'z'=8,'core'=2,'x'=4,'yh'=4] {'yh'}, dimensions={0} | all-to-all | bytes 393216 | tf_op jit(solution)/shard_map/all_to_all | solution.py:391
  35.8 10.4 %all_to_all.42.value_ref = f32[4,6,16,128]{3,2,1,0:T(8,128)S(1)} all-to-all(f32[4,6,16,128]{3,2,1,0:T(8,128)S(1)} %owner.2), channel_id=1, replica_groups=mesh['yl'=2,'z'=8,'core'=2,'x'=4,'yh'=4] {'yh'}, dimensions={0} | all-to-all | bytes 393216 | tf_op jit(solution)/shard_map/all_to_all | solution.py:391
  46.1 0.9 copies.2
  47.0 3.5 %all-to-all-start.3 = ((f32[4,4,6,16,128]{4,3,2,1,0:T(8,128)}), f32[4,4,6,16,128]{4,3,2,1,0:T(8,128)S(1)}, u32[]{:S(2)}, u32[]{:S(2)}) async-start(f32[4,4,6,16,128]{4,3,2,1,0:T(8,128)} %copies.2), calls=%async_computation.3 | async-start | bytes 1572864 | tf_op jit(solution)/shard_map/all_to_all | solution.py:391
  50.5 8.4 %collective-permute-start = (f32[27,2048]{1,0:T(8,128)}, f32[27,2048]{1,0:T(8,128)S(1)}, u32[]{:S(2)}, u32[]{:S(2)}) collective-permute-start(f32[27,2048]{1,0:T(8,128)} %get-tuple-element.21), channel_id=1, source_target_pairs={{0,16},{16,32},{32,48},{48,64},{64,80},{80,96},{96,112},{112,128},... | collective-permute-start | bytes 663560 | tf_op jit(solution)/shard_map/ppermute | solution.py:340
  59.0 1.9 %collective-permute-start.1 = (f32[27,2048]{1,0:T(8,128)}, f32[27,2048]{1,0:T(8,128)}, u32[]{:S(2)}, u32[]{:S(2)}) collective-permute-start(f32[27,2048]{1,0:T(8,128)} %get-tuple-element.22), channel_id=1, source_target_pairs={{16,0},{32,16},{48,32},{64,48},{80,64},{96,80},{112,96},{128,112},... | collective-permute-start | bytes 663560 | tf_op jit(solution)/shard_map/ppermute | solution.py:341
  60.9 1.7 %collective-permute-done.above_ref = f32[27,2048]{1,0:T(8,128)S(1)} collective-permute-done((f32[27,2048]{1,0:T(8,128)}, f32[27,2048]{1,0:T(8,128)S(1)}, u32[]{:S(2)}, u32[]{:S(2)}) %collective-permute-start) | collective-permute-done | bytes 221216 | tf_op jit(solution)/shard_map/ppermute | solution.py:340
  62.6 0.0 copy-start.7
  62.6 0.7 copy-done.7
  63.3 3.7 %collective-permute-done.1.below_ref = f32[27,2048]{1,0:T(8,128)} collective-permute-done((f32[27,2048]{1,0:T(8,128)}, f32[27,2048]{1,0:T(8,128)}, u32[]{:S(2)}, u32[]{:S(2)}) %collective-permute-start.1) | collective-permute-done | bytes 221216 | tf_op jit(solution)/shard_map/ppermute | solution.py:341
  67.0 0.0 all-to-all-done.3
  67.0 0.0 copy-done
  67.0 0.0 copy-done.1
  67.0 0.0 copy-done.5
  67.0 0.0 copy-done.6
  67.0 6.2 %first_step.1 = (f32[6,3,16,2048]{3,2,1,0:T(8,128)}, f32[16,6,16,128]{3,2,1,0:T(8,128)}, f32[24,2048]{1,0:T(8,128)}, f32[24,2048]{1,0:T(8,128)}, f32[3,16,2048]{...) custom-call(s32[1]{0:T(128)} %bitcast.first_ref, s32[6]{0:T(128)S(1)} %copy-done.5, f32[4]{0:T(128)S(1)} %copy-done.6, ...), custom_call_target="tpu_custom_call" | custom-call | tf_op jit(solution)/shard_map/first_step/pallas_call | solution.py:192
  73.2 4.5 %all-to-all-start.4 = ((f32[4,4,6,16,128]{4,3,2,1,0:T(8,128)}), f32[4,4,6,16,128]{4,3,2,1,0:T(8,128)S(1)}, u32[]{:S(2)}, u32[]{:S(2)}) async-start(f32[4,4,6,16,128]{4,3,2,1,0:T(8,128)} %bitcast.8), calls=%async_computation.4 | async-start | bytes 1572864 | tf_op jit(solution)/shard_map/all_to_all | solution.py:391
  77.7 2.0 %collective-permute-start.2 = (f32[24,2048]{1,0:T(8,128)}, f32[24,2048]{1,0:T(8,128)S(1)}, u32[]{:S(2)}, u32[]{:S(2)}) collective-permute-start(f32[24,2048]{1,0:T(8,128)} %get-tuple-element.28), channel_id=1, source_target_pairs={{0,16},{16,32},{32,48},{48,64},{64,80},{80,96},{96,112},{112,128},... | collective-permute-start | bytes 589832 | tf_op jit(solution)/shard_map/ppermute | solution.py:340
  79.7 0.0 copy-start.2
  79.7 0.0 copy-start.3
  79.7 0.0 copy-start.4
  79.7 3.4 %collective-permute-start.3 = (f32[24,2048]{1,0:T(8,128)}, f32[24,2048]{1,0:T(8,128)S(1)}, u32[]{:S(2)}, u32[]{:S(2)}) collective-permute-start(f32[24,2048]{1,0:T(8,128)} %get-tuple-element.29), channel_id=1, source_target_pairs={{16,0},{32,16},{48,32},{64,48},{80,64},{96,80},{112,96},{128,112},... | collective-permute-start | bytes 589832 | tf_op jit(solution)/shard_map/ppermute | solution.py:341
  83.1 0.0 collective-permute-done.2.mid_above_ref.above_ref
  83.1 4.9 %collective-permute-done.3.mid_below_ref.below_ref = f32[24,2048]{1,0:T(8,128)S(1)} collective-permute-done((f32[24,2048]{1,0:T(8,128)}, f32[24,2048]{1,0:T(8,128)S(1)}, u32[]{:S(2)}, u32[]{:S(2)}) %collective-permute-start.3) | collective-permute-done | bytes 196640 | tf_op jit(solution)/shard_map/ppermute | solution.py:341
  88.0 0.6 all-to-all-done.4.parts_ref
  88.6 11.3 %all_to_all.43.parts_ref = f32[4,6,16,128]{3,2,1,0:T(8,128)S(1)} all-to-all(f32[4,6,16,128]{3,2,1,0:T(8,128)S(1)} %add_parts.3), channel_id=1, replica_groups=mesh['yl'=2,'z'=8,'core'=2,'x'=4,'yh'=4] {'yh'}, dimensions={0} | all-to-all | bytes 393216 | tf_op jit(solution)/shard_map/all_to_all | solution.py:391
  99.9 10.3 %all_to_all.44.value_ref = f32[4,6,16,128]{3,2,1,0:T(8,128)S(1)} all-to-all(f32[4,6,16,128]{3,2,1,0:T(8,128)S(1)} %owner.3), channel_id=1, replica_groups=mesh['yl'=2,'z'=8,'core'=2,'x'=4,'yh'=4] {'yh'}, dimensions={0} | all-to-all | bytes 393216 | tf_op jit(solution)/shard_map/all_to_all | solution.py:391
  110.2 0.9 copies.3
  111.1 3.5 %all-to-all-start.7 = ((f32[4,4,6,16,128]{4,3,2,1,0:T(8,128)}), f32[4,4,6,16,128]{4,3,2,1,0:T(8,128)S(1)}, u32[]{:S(2)}, u32[]{:S(2)}) async-start(f32[4,4,6,16,128]{4,3,2,1,0:T(8,128)} %copies.3), calls=%async_computation.7 | async-start | bytes 1572864 | tf_op jit(solution)/shard_map/all_to_all | solution.py:391
  114.6 0.0 copy-done.2
  114.7 0.0 copy-done.3
  114.7 0.0 copy-done.4
  114.7 1.5 %solute_step.1 = (f32[3,16,2048]{2,1,0:T(8,128)S(1)}, f32[3,16,2048]{2,1,0:T(8,128)S(1)}) custom-call(f32[3,16,2048]{2,1,0:T(8,128)S(1)} %copy-done.1, f32[3,16,2048]{2,1,0:T(8,128)S(1)} %copy-done.2, f32[9,2048]{1,0:T(8,128)S(1)} %copy-done.3, f32[9,2048]{1,0:T(8,128)S(1)} %copy-done.4, f32[24,2048]{1,0:T(8,128)S(1)} %collective-permute-done.2.mid_above_ref.above_ref, ...), custom_call_target="tpu_custom_call" | custom-call | tf_op jit(solution)/shard_map/solute_step/pallas_call | solution.py:257
  116.2 6.8 %all-to-all-done.7 = f32[4,4,6,16,128]{4,3,2,1,0:T(8,128)S(1)} async-done(((f32[4,4,6,16,128]{4,3,2,1,0:T(8,128)}), f32[4,4,6,16,128]{4,3,2,1,0:T(8,128)S(1)}, u32[]{:S(2)}, u32[]{:S(2)}) %all-to-all-start.7) | async-done | bytes 786464 | tf_op jit(solution)/shard_map/all_to_all | solution.py:391
  122.9 0.1 second_potential.1
  123.0 11.8 %collective-permute-start.4 = (f32[3,2048]{1,0:T(4,128)S(1)}, f32[3,2048]{1,0:T(4,128)S(1)}, u32[]{:S(2)}, u32[]{:S(2)}) collective-permute-start(f32[3,2048]{1,0:T(4,128)S(1)} %get-tuple-element.36), channel_id=1, source_target_pairs={{0,16},{16,32},{32,48},{48,64},{64,80},{80,96},{96,112},{112,128},... | collective-permute-start | bytes 73736 | tf_op jit(solution)/shard_map/ppermute | solution.py:340
  134.8 1.9 %collective-permute-start.5 = (f32[3,2048]{1,0:T(4,128)S(1)}, f32[3,2048]{1,0:T(4,128)S(1)}, u32[]{:S(2)}, u32[]{:S(2)}) collective-permute-start(f32[3,2048]{1,0:T(4,128)S(1)} %get-tuple-element.37), channel_id=1, source_target_pairs={{16,0},{32,16},{48,32},{64,48},{80,64},{96,80},{112,96},{128,112},... | collective-permute-start | bytes 73736 | tf_op jit(solution)/shard_map/ppermute | solution.py:341
  136.8 5.8 %second_step.1 = f32[6,3,16,2048]{3,2,1,0:T(8,128)} custom-call(s32[6]{0:T(128)S(1)} %copy-done.5, f32[4]{0:T(128)S(1)} %copy-done.6, f32[6,3,16,2048]{3,2,1,0:T(8,128)} %get-tuple-element.23.old_ref, f32[3,16,2048]{2,1,0:T(8,128)S(1)} %get-tuple-element.32.solute_ref, f32[16,6,16,128]{3,2,1,0:T(8,128)S(1)} %bitcast.6, ...), custom_call_target="tpu_custom_call" | custom-call | flops 20000000 | bytes 10000000 | tf_op jit(solution)/shard_map/second_step/pallas_call | solution.py:303
  142.6 0.0 collective-permute-done.4.above_ref
  142.6 0.0 collective-permute-done.5.below_ref
  142.6 1.1 solute_end.1
  (4 shorter events, 0.1 us)
Async XLA Ops:
  17.8 49.2 %copy-start = (f32[6,3,16,2048]{3,2,1,0:T(8,128)S(1)}, f32[6,3,16,2048]{3,2,1,0:T(8,128)}, u32[]{:S(2)}) copy-start(f32[6,3,16,2048]{3,2,1,0:T(8,128)} %noise_ref.3) | copy-start | bytes 7077892
  17.8 49.2 %copy-start.1 = (f32[3,16,2048]{2,1,0:T(8,128)S(1)}, f32[3,16,2048]{2,1,0:T(8,128)}, u32[]{:S(2)}) copy-start(f32[3,16,2048]{2,1,0:T(8,128)} %solute_ref.5) | copy-start | bytes 1179652
  17.8 49.2 %copy-start.5 = (s32[6]{0:T(128)S(1)}, s32[6]{0:T(128)}, u32[]{:S(2)}) copy-start(s32[6]{0:T(128)} %group_ref.3) | copy-start | bytes 76
  17.8 49.2 %copy-start.6 = (f32[4]{0:T(128)S(1)}, f32[4]{0:T(128)}, u32[]{:S(2)}) copy-start(f32[4]{0:T(128)} %mobility_ref.3) | copy-start | bytes 52
  47.0 19.9 %all-to-all-start.3 = ((f32[4,4,6,16,128]{4,3,2,1,0:T(8,128)}), f32[4,4,6,16,128]{4,3,2,1,0:T(8,128)S(1)}, u32[]{:S(2)}, u32[]{:S(2)}) async-start(f32[4,4,6,16,128]{4,3,2,1,0:T(8,128)} %copies.2), calls=%async_computation.3 | async-start | bytes 1572864 | tf_op jit(solution)/shard_map/all_to_all | solution.py:391
  50.5 12.0 %collective-permute-start = (f32[27,2048]{1,0:T(8,128)}, f32[27,2048]{1,0:T(8,128)S(1)}, u32[]{:S(2)}, u32[]{:S(2)}) collective-permute-start(f32[27,2048]{1,0:T(8,128)} %get-tuple-element.21), channel_id=1, source_target_pairs={{0,16},{16,32},{32,48},{48,64},{64,80},{80,96},{96,112},{112,128},... | collective-permute-start | bytes 663560 | tf_op jit(solution)/shard_map/ppermute | solution.py:340
  59.0 8.0 %collective-permute-start.1 = (f32[27,2048]{1,0:T(8,128)}, f32[27,2048]{1,0:T(8,128)}, u32[]{:S(2)}, u32[]{:S(2)}) collective-permute-start(f32[27,2048]{1,0:T(8,128)} %get-tuple-element.22), channel_id=1, source_target_pairs={{16,0},{32,16},{48,32},{64,48},{80,64},{96,80},{112,96},{128,112},... | collective-permute-start | bytes 663560 | tf_op jit(solution)/shard_map/ppermute | solution.py:341
  62.6 0.7 copy-start.7
  73.2 15.4 %all-to-all-start.4 = ((f32[4,4,6,16,128]{4,3,2,1,0:T(8,128)}), f32[4,4,6,16,128]{4,3,2,1,0:T(8,128)S(1)}, u32[]{:S(2)}, u32[]{:S(2)}) async-start(f32[4,4,6,16,128]{4,3,2,1,0:T(8,128)} %bitcast.8), calls=%async_computation.4 | async-start | bytes 1572864 | tf_op jit(solution)/shard_map/all_to_all | solution.py:391
  77.7 5.4 %collective-permute-start.2 = (f32[24,2048]{1,0:T(8,128)}, f32[24,2048]{1,0:T(8,128)S(1)}, u32[]{:S(2)}, u32[]{:S(2)}) collective-permute-start(f32[24,2048]{1,0:T(8,128)} %get-tuple-element.28), channel_id=1, source_target_pairs={{0,16},{16,32},{32,48},{48,64},{64,80},{80,96},{96,112},{112,128},... | collective-permute-start | bytes 589832 | tf_op jit(solution)/shard_map/ppermute | solution.py:340
  79.7 35.0 %copy-start.2 = (f32[3,16,2048]{2,1,0:T(8,128)S(1)}, f32[3,16,2048]{2,1,0:T(8,128)}, u32[]{:S(2)}) copy-start(f32[3,16,2048]{2,1,0:T(8,128)} %get-tuple-element.24.middle_ref) | copy-start | bytes 1179652
  79.7 35.0 %copy-start.3 = (f32[9,2048]{1,0:T(8,128)S(1)}, f32[9,2048]{1,0:T(8,128)}, u32[]{:S(2)}) copy-start(f32[9,2048]{1,0:T(8,128)} %get-tuple-element.25.above_ref) | copy-start | bytes 221188
  79.7 35.0 %copy-start.4 = (f32[9,2048]{1,0:T(8,128)S(1)}, f32[9,2048]{1,0:T(8,128)}, u32[]{:S(2)}) copy-start(f32[9,2048]{1,0:T(8,128)} %get-tuple-element.26.below_ref) | copy-start | bytes 221188
  79.7 8.3 %collective-permute-start.3 = (f32[24,2048]{1,0:T(8,128)}, f32[24,2048]{1,0:T(8,128)S(1)}, u32[]{:S(2)}, u32[]{:S(2)}) collective-permute-start(f32[24,2048]{1,0:T(8,128)} %get-tuple-element.29), channel_id=1, source_target_pairs={{16,0},{32,16},{48,32},{64,48},{80,64},{96,80},{112,96},{128,112},... | collective-permute-start | bytes 589832 | tf_op jit(solution)/shard_map/ppermute | solution.py:341
  111.1 11.8 %all-to-all-start.7 = ((f32[4,4,6,16,128]{4,3,2,1,0:T(8,128)}), f32[4,4,6,16,128]{4,3,2,1,0:T(8,128)S(1)}, u32[]{:S(2)}, u32[]{:S(2)}) async-start(f32[4,4,6,16,128]{4,3,2,1,0:T(8,128)} %copies.3), calls=%async_computation.7 | async-start | bytes 1572864 | tf_op jit(solution)/shard_map/all_to_all | solution.py:391
  123.0 19.6 %collective-permute-start.4 = (f32[3,2048]{1,0:T(4,128)S(1)}, f32[3,2048]{1,0:T(4,128)S(1)}, u32[]{:S(2)}, u32[]{:S(2)}) collective-permute-start(f32[3,2048]{1,0:T(4,128)S(1)} %get-tuple-element.36), channel_id=1, source_target_pairs={{0,16},{16,32},{32,48},{48,64},{64,80},{80,96},{96,112},{112,128},... | collective-permute-start | bytes 73736 | tf_op jit(solution)/shard_map/ppermute | solution.py:340
  134.8 7.7 %collective-permute-start.5 = (f32[3,2048]{1,0:T(4,128)S(1)}, f32[3,2048]{1,0:T(4,128)S(1)}, u32[]{:S(2)}, u32[]{:S(2)}) collective-permute-start(f32[3,2048]{1,0:T(4,128)S(1)} %get-tuple-element.37), channel_id=1, source_target_pairs={{16,0},{32,16},{48,32},{64,48},{80,64},{96,80},{112,96},{128,112},... | collective-permute-start | bytes 73736 | tf_op jit(solution)/shard_map/ppermute | solution.py:341
